TPU v7x, 128 devices: a whole 4x4x4 slice. The times are simulated.
128 devices in a mesh: seq: 16 (over x, z), dp: 8 (over y, core).
Axes of the slice: x: 4, y: 4, z: 4, core: 2. Of those that a mesh axis runs over, the one named last changes fastest.
Arguments:
- tokens: bfloat16 [8, 8192, 1280], P('dp', 'seq'), may hold values from -10 to 10
- queries: bfloat16 [1024, 1280], replicated, may hold values from -400 to 400
- key_weight: bfloat16 [1280, 1280], replicated, may hold values from -0.15625 to 0.15625
- value_weight: bfloat16 [1280, 1280], replicated, may hold values from -0.15625 to 0.15625
- out_grad: bfloat16 [8, 1024, 1280], P('dp'), may hold values from -6 to 6
Outputs:
- attended: bfloat16 [8, 1024, 1280], P('dp')
- query_grad: float32 [1024, 1280], replicated
- key_wgrad: float32 [1280, 1280], P(('seq', 'dp'))
- value_wgrad: float32 [1280, 1280], P(('seq', 'dp'))
All inputs are finite; a program needn't handle non-finite values.
Results may differ from a plain program's by a relative error of at most 0.035.
The roundings to bfloat16 on the way count: a program that leaves them out, or rounds other values in their place, can miss the bound.
Values sent between devices are 32-bit elements; how exact they have to be, the bound alone decides.
No kernel may reach another device: no remote copies, remote signals or barrier semaphores. Data moves between devices by JAX's collectives and lax.ppermute only.
A program may use at most 512 MiB of HBM per device.

v0:
```python
import jax
import jax.numpy as jnp
from jax import lax
from jax.sharding import PartitionSpec as P

H = 10
HD = 128


def layer_norm(rows):
    values = rows.astype(jnp.float32)
    centre = values - jnp.mean(values, axis=-1, keepdims=True)
    spread = jnp.mean(centre * centre, axis=-1, keepdims=True)
    return (centre * lax.rsqrt(spread + 1e-05)).astype(jnp.bfloat16)


def on_device(tokens, queries, key_weight, value_weight, out_grad):
    scale = HD ** (-0.5)
    normed = layer_norm(tokens[0])
    tok_rows = normed.shape[0]
    latents, width = queries.shape
    keys = jnp.dot(normed, key_weight, preferred_element_type=jnp.float32).astype(jnp.bfloat16)
    vals = jnp.dot(normed, value_weight, preferred_element_type=jnp.float32).astype(jnp.bfloat16)
    query_heads = queries.reshape(latents, H, HD)
    key_heads = keys.reshape(tok_rows, H, HD)
    val_heads = vals.reshape(tok_rows, H, HD)
    scores = (
        jnp.einsum("lhd,thd->hlt", query_heads, key_heads, preferred_element_type=jnp.float32)
        * scale
    )
    block_top = jnp.max(scores, axis=2)
    shifted = jnp.exp(scores - block_top[:, :, None])
    block_total = jnp.sum(shifted, axis=2)
    weights = shifted.astype(jnp.bfloat16)
    block_numer = jnp.einsum("hlt,thd->lhd", weights, val_heads, preferred_element_type=jnp.float32)
    top = lax.pmax(block_top, "seq")
    factor = jnp.exp(block_top - top)
    total, numer = lax.psum(
        (block_total * factor, block_numer * jnp.transpose(factor)[:, :, None]), "seq"
    )
    attended = (numer / jnp.transpose(total)[:, :, None]).astype(jnp.bfloat16)
    lse = top + jnp.log(total)
    grad_heads = out_grad[0].reshape(latents, H, HD)
    delta = jnp.transpose(
        jnp.sum(grad_heads.astype(jnp.float32) * attended.astype(jnp.float32), axis=2)
    )
    probs = jnp.exp(scores - lse[:, :, None])
    vgrad = jnp.einsum(
        "hlt,lhd->thd", probs.astype(jnp.bfloat16), grad_heads, preferred_element_type=jnp.float32
    ).astype(jnp.bfloat16)
    pgrad = jnp.einsum("lhd,thd->hlt", grad_heads, val_heads, preferred_element_type=jnp.float32)
    sgrad = (probs * (pgrad - delta[:, :, None]) * scale).astype(jnp.bfloat16)
    query_part = jnp.einsum(
        "hlt,thd->lhd", sgrad, key_heads, preferred_element_type=jnp.float32
    ).reshape(latents, width)
    query_grad = lax.psum(query_part, ("seq", "dp"))
    kgrad = jnp.einsum(
        "hlt,lhd->thd", sgrad, query_heads, preferred_element_type=jnp.float32
    ).astype(jnp.bfloat16)
    stacked = jnp.concatenate(
        [kgrad.reshape(tok_rows, width), vgrad.reshape(tok_rows, width)], axis=1
    )
    grads = lax.psum_scatter(
        jnp.einsum("tc,te->ce", normed, stacked, preferred_element_type=jnp.float32),
        ("seq", "dp"),
        scatter_dimension=0,
        tiled=True,
    )
    return (attended.reshape(1, latents, width), query_grad, grads[:, :width], grads[:, width:])


def solution(mesh):
    placed = (P("dp", "seq", None), P(), P(), P(), P("dp", None, None))
    return jax.shard_map(
        on_device,
        mesh=mesh,
        in_specs=placed,
        out_specs=(P("dp", None, None), P(), P(("seq", "dp"), None), P(("seq", "dp"), None)),
        check_vma=False,
    )
```

profile of v0, /device:TPU:1, one launch (start us, length us, event | category | flops | bytes accessed | tf_op | source)
XLA Modules:
  0.0 527.7 jit_solution(8877848470027462172)
XLA Ops:
  7.2 0.0 copy-start
  7.2 0.0 all-reduce.5.cloned.1.call-start
  7.2 0.0 copy-start.7
  7.2 1.7 convert_reduce_fusion
  9.0 1.8 fusion.18
  10.8 3.0 convolution_convert_fusion
  13.8 1.6 copy.38
  15.4 4.9 copy.39
  20.3 10.4 %bitcast_reduce_fusion = (f32[10,1024]{1,0:T(8,128)S(1)}, f32[10,512,1024]{2,1,0:T(8,128)}) fusion(bf16[512,10,128]{0,2,1:T(8,128)(2,1)S(1)} %bitcast.79, bf16[1024,10,128]{0,2,1:T(8,128)(2,1)} %bitcast.81), kind=kOutput, calls=%fused_computation.5 | convolution fusion | flops 1352652800 | bytes 24944640 | tf_op jit(solution)/shard_map/lhd,thd->hlt/dot_general | solution.py:28
  30.7 62.4 %pmax.7 = f32[10,1024]{1,0:T(8,128)S(1)} all-reduce(f32[10,1024]{1,0:T(8,128)S(1)} %get-tuple-element.24), channel_id=1, replica_groups=mesh['seq'=16,'dp'=8] {'seq'}, use_global_device_ids=true, to_apply=%region_3.0 | all-reduce | flops 10240 | bytes 81920 | tf_op jit(solution)/shard_map/pmax | solution.py:36
  93.1 9.8 %fusion.5 = f32[10,1024]{1,0:T(8,128)S(1)} fusion(f32[10,512,1024]{2,1,0:T(8,128)} %get-tuple-element.25, f32[10,1024]{1,0:T(8,128)S(1)} %get-tuple-element.24), kind=kLoop, calls=%fused_computation.9 | loop fusion | flops 15718400 | bytes 21053440 | tf_op jit(solution)/shard_map/reduce_sum | solution.py:33
  103.0 1.9 convolution_convert_fusion.1
  105.0 0.7 copy.37
  105.7 13.9 %bitcast_multiply_fusion.1 = f32[1024,10,128]{0,2,1:T(8,128)} fusion(f32[1024,10]{0,1:T(8,128)S(1)} %get-tuple-element.23, bf16[512,10,128]{0,2,1:T(8,128)(2,1)S(1)} %bitcast.83, f32[10,512,1024]{2,1,0:T(8,128)} %get-tuple-element.25, f32[10,1024]{1,0:T(8,128)S(1)} %get-tuple-element.24), kind=kOutput, calls=%fused_computation.17 | convolution fusion | flops 1359216640 | bytes 27607040 | tf_op jit(solution)/shard_map/hlt,thd->lhd/dot_general | solution.py:35
  119.6 0.0 all-reduce.5.cloned.1.call-update
  119.6 0.0 all-reduce.7.cloned.1.call-start
  119.7 3.0 copy.43
  122.7 57.4 %psum.22 = f32[10,1024]{1,0:T(8,128)S(1)} all-reduce(f32[10,1024]{1,0:T(8,128)S(1)} %get-tuple-element.22), channel_id=1, replica_groups=mesh['seq'=16,'dp'=8] {'seq'}, use_global_device_ids=true, to_apply=%region_6.0 | all-reduce | flops 10240 | bytes 81920 | tf_op jit(solution)/shard_map/psum | solution.py:38
  180.1 10.5 %fusion.26 = bf16[10,512,128]{1,2,0:T(8,128)(2,1)} fusion(bf16[1024,10,128]{0,2,1:T(8,128)(2,1)S(1)} %bitcast.76, f32[10,512,1024]{2,1,0:T(8,128)} %get-tuple-element.25, f32[10,1024]{1,0:T(8,128)S(1)} %log_add_fusion), kind=kOutput, calls=%fused_computation.33 | convolution fusion | flops 1358561280 | bytes 24944640 | tf_op jit(solution)/shard_map/hlt,lhd->thd/dot_general | solution.py:48
  190.6 53.0 %all-reduce.5.cloned.1.call-done = f32[1024,10,128]{0,2,1:T(8,128)} async-done(((f32[1024,10,128]{0,2,1:T(8,128)}), f32[1024,10,128]{0,2,1:T(8,128)}) %all-reduce.5.cloned.1.call-update) | async-done | bytes 5242896 | tf_op jit(solution)/shard_map/psum | solution.py:38
  243.7 5.0 multiply_reduce_fusion
  248.7 13.9 %fusion.1 = bf16[10,1024,512]{1,2,0:T(8,128)(2,1)} fusion(f32[10,512,1024]{2,1,0:T(8,128)} %get-tuple-element.25, f32[10,1024]{1,0:T(8,128)S(1)} %bitcast.87, f32[10,1024]{1,0:T(8,128)S(1)} %log_add_fusion, bf16[512,10,128]{0,2,1:T(8,128)(2,1)} %bitcast.84, bf16[1024,10,128]{0,2,1:T(8,128)(2,1)S(1)} %bitcast.78), kind=kOutput, calls=%fused_computation.2 | convolution fusion | flops 1373634560 | bytes 35471360 | tf_op jit(solution)/shard_map/lhd,thd->hlt/dot_general | solution.py:51
  262.6 8.8 %convolution_convert_fusion.2 = bf16[10,512,128]{1,2,0:T(8,128)(2,1)} fusion(bf16[10,1024,512]{1,2,0:T(8,128)(2,1)} %fusion.1, bf16[1024,10,128]{0,2,1:T(8,128)(2,1)S(1)} %bitcast.82), kind=kOutput, calls=%fused_computation.34 | convolution fusion | flops 1342832640 | bytes 14417920 | tf_op jit(solution)/shard_map/hlt,lhd->thd/dot_general | solution.py:57
  271.3 7.9 %fusion.38 = f32[10,128,1024]{2,1,0:T(8,128)} fusion(bf16[512,10,128]{0,2,1:T(8,128)(2,1)S(1)} %bitcast.80, bf16[10,1024,512]{1,2,0:T(8,128)(2,1)} %fusion.1), kind=kOutput, calls=%fused_computation.46 | convolution fusion | flops 1342177280 | bytes 17039360 | tf_op jit(solution)/shard_map/hlt,thd->lhd/dot_general | solution.py:53
  279.2 6.1 %copy.47 = f32[1024,1280]{1,0:T(8,128)} copy(f32[1024,1280]{0,1:T(8,128)} %bitcast.75) | data formatting | bytes 10485760 | tf_op jit(solution)/shard_map/reshape | solution.py:55
  285.3 8.6 %fusion.20 = f32[1280,2560]{1,0:T(8,128)} fusion(bf16[512,1280]{0,1:T(8,128)(2,1)S(1)} %bitcast.88, bf16[512,1280]{0,1:T(8,128)(2,1)} %bitcast.89, bf16[1,512,1280]{2,1,0:T(8,128)(2,1)S(1)} %copy-done.9, f32[512]{0:T(512)S(1)} %add_rsqrt_fusion, f32[512]{0:T(512)S(1)} %broadcast_multiply_fusion), kind=kOutput, calls=%fused_computation.29 | convolution fusion | flops 3363307520 | bytes 17043456 | tf_op jit(solution)/shard_map/tc,te->ce/dot_general | solution.py:64
  293.9 0.0 all-reduce.7.cloned.1.call-update
  293.9 1.7 copy-done.6
  295.6 2.7 copy.50
  298.3 215.5 %all-reduce.7.cloned.1.call-done = (f32[1024,1280]{1,0:T(8,128)}, f32[1280,2560]{1,0:T(8,128)}) async-done(((f32[1024,1280]{1,0:T(8,128)}, f32[1280,2560]{1,0:T(8,128)}), (f32[1024,1280]{1,0:T(8,128)}, f32[1280,2560]{1,0:T(8,128)})) %all-reduce.7.cloned.1.call-update) | async-done | bytes 18350096 | tf_op jit(solution)/shard_map/psum | solution.py:56
  513.8 1.7 fusion.37
  515.5 5.3 %copy.62 = f32[1024,1280]{1,0:T(8,128)} copy(f32[1024,1280]{1,0:T(8,128)} %get-tuple-element.27) | data formatting | bytes 10485760
  (25 shorter events, 0.1 us)
Async XLA Ops:
  7.2 3.6 copy-start
  7.2 236.5 %all-reduce.5.cloned.1.call-start = ((), (), s32[]{:S(2)}) async-start(), calls=%async_computation | async-start | bytes 10485760 | tf_op jit(solution)/shard_map/psum | solution.py:38
  7.2 3.6 copy-start.7
  15.4 4.9 copy-start.2
  93.1 9.9 %copy-start.8 = (bf16[1,512,1280]{2,1,0:T(8,128)(2,1)S(1)}, bf16[1,512,1280]{2,1,0:T(8,128)(2,1)}, u32[]{:S(2)}) copy-start(bf16[1,512,1280]{2,1,0:T(8,128)(2,1)} %param.5) | copy-start | bytes 3932164
  93.1 9.9 %copy-start.10 = (bf16[1280,1280]{1,0:T(8,128)(2,1)S(1)}, bf16[1280,1280]{1,0:T(8,128)(2,1)}, u32[]{:S(2)}) copy-start(bf16[1280,1280]{1,0:T(8,128)(2,1)} %param.8) | copy-start | bytes 9830404
  105.6 14.0 %copy-start.5 = (bf16[512,1280]{0,1:T(8,128)(2,1)}, bf16[512,1280]{0,1:T(8,128)(2,1)S(1)}, u32[]{:S(2)}) copy-start(bf16[512,1280]{0,1:T(8,128)(2,1)S(1)} %copy.37) | copy-start | bytes 3932164
  119.6 394.2 %all-reduce.7.cloned.1.call-start = ((), (), s32[]{:S(2)}) async-start(), calls=%async_computation.1 | async-start | bytes 36700160 | tf_op jit(solution)/shard_map/psum | solution.py:56
  248.7 13.9 %copy-start.4 = (bf16[1024,1280]{0,1:T(8,128)(2,1)S(1)}, bf16[1024,1280]{0,1:T(8,128)(2,1)}, u32[]{:S(2)}) copy-start(bf16[1024,1280]{0,1:T(8,128)(2,1)} %copy.39) | copy-start | bytes 7864324
  262.6 8.8 %copy-start.3 = (bf16[512,1280]{0,1:T(8,128)(2,1)S(1)}, bf16[512,1280]{0,1:T(8,128)(2,1)}, u32[]{:S(2)}) copy-start(bf16[512,1280]{0,1:T(8,128)(2,1)} %copy-done.2) | copy-start | bytes 3932164
  279.2 6.1 %copy-start.9 = (bf16[1,512,1280]{2,1,0:T(8,128)(2,1)S(1)}, bf16[1,512,1280]{2,1,0:T(8,128)(2,1)}, u32[]{:S(2)}) copy-start(bf16[1,512,1280]{2,1,0:T(8,128)(2,1)} %param.5) | copy-start | bytes 3932164
  279.2 6.1 %copy-start.11 = (bf16[10,512,128]{1,2,0:T(8,128)(2,1)S(1)}, bf16[10,512,128]{1,2,0:T(8,128)(2,1)}, u32[]{:S(2)}) copy-start(bf16[10,512,128]{1,2,0:T(8,128)(2,1)} %fusion.26) | copy-start | bytes 3932164
  293.9 1.7 copy-start.6
  515.5 5.3 %copy-start.1 = (bf16[1280,1280]{1,0:T(8,128)(2,1)S(1)}, bf16[1280,1280]{1,0:T(8,128)(2,1)}, u32[]{:S(2)}) copy-start(bf16[1280,1280]{1,0:T(8,128)(2,1)} %param.7) | copy-start | bytes 9830404
Sparse Core Ops, SparseCore 0:
  119.7 123.8 all-reduce.4
  294.0 219.7 all-reduce.6
where the time goes:
time: 528 us
  waiting for transfers between devices  269 us (51%)
  blocking collectives  120 us (23%)
  matrix products  78.9 us (15%)
  local copies, waits for them, and re-layouts  27.7 us (5%)
  other arithmetic  18.4 us (3%)
  between operations  14.2 us (3%)
    psum x1, waiting for transfers between devices, on_device(): query_grad = lax.psum(query_part, ('seq', 'dp'))  215 us
    pmax x1, blocking collectives, on_device(): top = lax.pmax(block_top, 'seq')  62.4 us
    psum x1, blocking collectives, on_device(): lax.psum((block_total * factor, block_numer * jnp.transpose(factor)[:, :,...  57.4 us
    psum x1, waiting for transfers between devices, on_device(): lax.psum((block_total * factor, block_numer * jnp.transpose(factor)[:, :,...  53 us
    unnamed x28, local copies, waits for them, and re-layouts  17.6 us
    dot_general x1, matrix products, on_device(): jnp.einsum('hlt,thd->lhd', weights, val_heads, preferred_element_type=jnp...  13.9 us
    dot_general x1, matrix products, on_device(): jnp.einsum('lhd,thd->hlt', grad_heads, val_heads, preferred_element_type=...  13.9 us
  transfers between devices with their start and end apart: 2, of which 2 were waited for; matrix products, arithmetic and copies ran while one was open for 3% of the time, Pallas kernels for 0%

commit v1 on v0

v1 whole, which is shorter than its diff:
```python
import functools

import jax
import jax.numpy as jnp
import numpy as np
from jax import lax
from jax.experimental import pallas as pl
from jax.experimental.pallas import tpu as pltpu
from jax.sharding import PartitionSpec as P

H = 10
HD = 128
T = 512
L = 1024
D = 1280
PAIR = 2 * HD
SCALE = HD ** (-0.5)
VMEM_LIMIT = 56 * 1024 * 1024
PARTS = (((0, 1, 2), ("y", "x", "z")), ((3, 4), ("z", "y", "x")))
F32 = jnp.float32
BF16 = jnp.bfloat16


def shift(array, axis, step):
    if axis == "x":
        return lax.ppermute(array, "seq", [(a * 4 + b, (a + step) % 4 * 4 + b) for a in range(4) for b in range(4)])
    if axis == "z":
        return lax.ppermute(array, "seq", [(a * 4 + b, a * 4 + (b + step) % 4) for a in range(4) for b in range(4)])
    if axis == "y":
        return lax.ppermute(array, "dp", [(a * 2 + b, (a + step) % 4 * 2 + b) for a in range(4) for b in range(2)])
    return lax.ppermute(array, "dp", [(a * 2 + b, a * 2 + 1 - b) for a in range(4) for b in range(2)])


def nt_dot(a, b):
    return lax.dot_general(a, b, (((1,), (1,)), ((), ())), preferred_element_type=F32)


def dot(a, b):
    return jnp.dot(a, b, preferred_element_type=F32)


def params():
    return pltpu.CompilerParams(vmem_limit_bytes=VMEM_LIMIT)


def cost(flops, moved):
    return pl.CostEstimate(flops=int(flops), bytes_accessed=int(moved), transcendentals=0)


def full(shape):
    return pl.BlockSpec(shape, lambda *_: (0,) * len(shape))


SMEM = pl.BlockSpec(memory_space=pltpu.SMEM)


def forward_kernel(place, tok, kw, vw, q, g, k_out, v_out, normed_out, n0, n1, n2, n3, stats, normed, s, w, numer):
    @pl.when(pl.program_id(0) == 0)
    def _():
        values = tok[...].astype(F32)
        centre = values - jnp.mean(values, axis=-1, keepdims=True)
        spread = jnp.mean(centre * centre, axis=-1, keepdims=True)
        normed[...] = (centre * lax.rsqrt(spread + 1e-05)).astype(BF16)
        normed_out[...] = normed[...]

    keys = dot(normed[...], kw[...]).astype(BF16)
    vals = dot(normed[...], vw[...]).astype(BF16)
    k_out[...] = keys
    v_out[...] = vals
    vals_t = vals.T
    grad_t = g[...].T
    for j in range(2):
        head = slice(j * HD, (j + 1) * HD)
        s[j] = nt_dot(keys[:, head], q[:, head])
        for tile in range(L // 128):
            at = slice(tile * 128, (tile + 1) * 128)
            scores = s[j, :, at] * SCALE
            high = jnp.max(scores, axis=0, keepdims=True)
            shifted = jnp.exp(scores - high)
            stats[0, j : j + 1, at] = high
            stats[0, 2 + j : 3 + j, at] = jnp.sum(shifted, axis=0, keepdims=True)
            w[j, :, at] = shifted.astype(BF16)
        part = dot(vals_t[head, :], w[j])
        numer[head, :] = part
        stats[0, 4 + j : 5 + j, :] = jnp.sum(part * grad_t[head, :].astype(F32), axis=0, keepdims=True)
    stats[0, 6:8, :] = jnp.zeros((2, L), F32)
    for k, out in enumerate((n0, n1, n2, n3)):
        start = pl.multiple_of(lax.rem(place[0] + k, 4) * 256, 256)
        out[...] = numer[:, pl.ds(start, 256)]


def forward(place, tokens, kw, vw, q, g):
    cols = lambda rows: pl.BlockSpec((rows, PAIR), lambda i: (0, i))
    return pl.pallas_call(
        forward_kernel,
        grid=(H // 2,),
        in_specs=[SMEM, full((T, D)), cols(D), cols(D), cols(L), cols(L)],
        out_specs=[cols(T), cols(T), full((T, D))]
        + [pl.BlockSpec((PAIR, 256), lambda i: (i, 0))] * 4
        + [pl.BlockSpec((1, 8, L), lambda i: (i, 0, 0))],
        out_shape=[jax.ShapeDtypeStruct((T, D), BF16)] * 3
        + [jax.ShapeDtypeStruct((D, 256), F32)] * 4
        + [jax.ShapeDtypeStruct((H // 2, 8, L), F32)],
        scratch_shapes=[
            pltpu.VMEM((T, D), BF16),
            pltpu.VMEM((2, T, L), F32),
            pltpu.VMEM((2, T, L), BF16),
            pltpu.VMEM((PAIR, L), F32),
        ],
        compiler_params=params(),
        cost_estimate=cost(1.2e10, 2.4e7),
        name="forward",
    )(place, tokens, kw, vw, q, g)


def merge(blocks):
    top = functools.reduce(jnp.maximum, [b[:, 0:2, :] for b in blocks])
    total = jnp.zeros_like(top)
    inner = jnp.zeros_like(top)
    for b in blocks:
        factor = jnp.exp(b[:, 0:2, :] - top)
        total += b[:, 2:4, :] * factor
        inner += b[:, 4:6, :] * factor
    return top, total, inner


def merge_kernel(s0, s1, s2, s3, out):
    top, total, inner = merge((s0, s1, s2, s3))
    out[:, 0:2, :] = top
    out[:, 2:4, :] = total
    out[:, 4:6, :] = inner
    out[:, 6:8, :] = jnp.zeros_like(top)


def finish_kernel(s0, s1, s2, s3, out):
    top, total, inner = merge((s0, s1, s2, s3))
    out[:, 0:2, :] = top + jnp.log(total)
    out[:, 2:4, :] = inner / total
    out[:, 4:6, :] = total
    out[:, 6:8, :] = top


def merged(kernel, blocks, name):
    return pl.pallas_call(
        kernel,
        out_shape=jax.ShapeDtypeStruct((H // 2, 8, L), F32),
        compiler_params=params(),
        cost_estimate=cost(1e6, 8e5),
        name=name,
    )(*blocks)


def reorder_kernel(order, normed, out):
    feature = lax.broadcasted_iota(jnp.int32, (D, D), 0)
    choose = jnp.where(feature == order[...], 1.0, 0.0).astype(BF16)
    out[...] = dot(normed[...], choose).astype(BF16).T


def reorder(order, normed):
    return pl.pallas_call(
        reorder_kernel,
        out_shape=jax.ShapeDtypeStruct((D, T), BF16),
        compiler_params=params(),
        cost_estimate=cost(2 * T * D * D, 3e6),
        name="reorder",
    )(order, normed)


def row_order(place, axes):
    digits = np.indices((2, 4, 4, 4, 10)).reshape(5, D)
    own = dict(x=place[0], z=place[1], y=place[2])
    spot = {a: (own[a] + jnp.asarray(digits[1 + i], jnp.int32)) % 4 for i, a in enumerate(axes)}
    core = (place[3] + jnp.asarray(digits[0], jnp.int32)) % 2
    owner = ((spot["x"] * 4 + spot["z"]) * 4 + spot["y"]) * 2 + core
    return (owner * 10 + jnp.asarray(digits[4], jnp.int32)).reshape(1, D)


def backward_kernel(place, nt, keys, vals, q, g, fin, mine, theirs, s, pg, p, sg, query):
    grads = []
    keys_t = keys[...].T
    for j in range(2):
        head = slice(j * HD, (j + 1) * HD)
        s[j] = nt_dot(keys[:, head], q[:, head])
        pg[j] = nt_dot(vals[:, head], g[:, head])
        for tile in range(L // 128):
            at = slice(tile * 128, (tile + 1) * 128)
            probs = jnp.exp(s[j, :, at] * SCALE - fin[0, j : j + 1, at])
            p[j, :, at] = probs.astype(BF16)
            sg[j, :, at] = (probs * (pg[j, :, at] - fin[0, 2 + j : 3 + j, at]) * SCALE).astype(BF16)
        vgrad = dot(p[j], g[:, head]).astype(BF16)
        kgrad = dot(sg[j], q[:, head]).astype(BF16)
        query[:, head] = dot(keys_t[head, :], sg[j]).T
        grads.append((kgrad, vgrad))
    key_rows = dot(nt[...], jnp.concatenate([grads[0][0], grads[1][0]], axis=1))
    value_rows = dot(nt[...], jnp.concatenate([grads[0][1], grads[1][1]], axis=1))
    for half, out in enumerate((mine, theirs)):
        for k in range(4):
            rows = slice(half * 640 + k * 160, half * 640 + (k + 1) * 160)
            out[k, 0:160, :] = key_rows[rows]
            out[k, 160:320, :] = value_rows[rows]
            start = lax.rem(place[0] + half, 2) * 512 + lax.rem(place[1] + k, 4) * 128
            out[k, 320:448, :] = query[pl.ds(pl.multiple_of(start, 128), 128), :]


def backward(place, nt, keys, vals, q, g, fin, pairs):
    first, width = pairs[0], len(pairs) * PAIR
    cols = lambda rows: pl.BlockSpec((rows, PAIR), lambda i: (0, i + first))
    out = pl.BlockSpec((4, 448, PAIR), lambda i: (0, 0, i))
    return pl.pallas_call(
        backward_kernel,
        grid=(len(pairs),),
        in_specs=[SMEM, full((D, T)), cols(T), cols(T), cols(L), cols(L), pl.BlockSpec((1, 8, L), lambda i: (i + first, 0, 0))],
        out_specs=[out, out],
        out_shape=[jax.ShapeDtypeStruct((4, 448, width), F32)] * 2,
        scratch_shapes=[
            pltpu.VMEM((2, T, L), F32),
            pltpu.VMEM((2, T, L), F32),
            pltpu.VMEM((2, T, L), BF16),
            pltpu.VMEM((2, T, L), BF16),
            pltpu.VMEM((L, PAIR), F32),
        ],
        compiler_params=params(),
        cost_estimate=cost(3.2e9 * len(pairs), 4e6 * len(pairs)),
        name="backward",
    )(place, nt, keys, vals, q, g, fin)


def by_columns(kernel, ins, out_rows, name):
    width = ins[0].shape[-1]
    spec = lambda shape: pl.BlockSpec(shape[:-1] + (PAIR,), lambda i, n=len(shape): (0,) * (n - 1) + (i,))
    outs = [(rows, width) for rows in out_rows]
    return pl.pallas_call(
        kernel,
        grid=(width // PAIR,),
        in_specs=[spec(a.shape) for a in ins],
        out_specs=[spec(o) for o in outs],
        out_shape=[jax.ShapeDtypeStruct(o, F32) for o in outs],
        compiler_params=params(),
        cost_estimate=cost(1e6, 4 * (sum(a.size for a in ins) + sum(r for r in out_rows) * width)),
        name=name,
    )(*ins)


def pair_kernel(mine, other, *outs):
    for k, out in enumerate(outs):
        out[...] = mine[k] + other[k]


def four(a0, a1, a2, a3):
    return (a0[...] + a2[...]) + (a1[...] + a3[...])


def second_kernel(a0, a1, a2, a3, *outs):
    rows = four(a0, a1, a2, a3)
    for k, out in enumerate(outs):
        out[0:40, :] = rows[k * 40 : (k + 1) * 40]
        out[40:80, :] = rows[160 + k * 40 : 160 + (k + 1) * 40]
        out[80:208, :] = rows[320:448]


def third_kernel(a0, a1, a2, a3, *outs):
    rows = four(a0, a1, a2, a3)
    for k, out in enumerate(outs):
        out[0:128, :] = rows[80:208]
        out[128:138, :] = rows[k * 10 : (k + 1) * 10]
        out[138:148, :] = rows[40 + k * 10 : 40 + (k + 1) * 10]
        out[148:152, :] = jnp.zeros((4, PAIR), F32)


def last_kernel(a0, a1, a2, a3, query, key_rows, value_rows):
    rows = four(a0, a1, a2, a3)
    query[...] = rows[0:128]
    key_rows[...] = rows[128:138]
    value_rows[...] = rows[138:148]


def exchange(chunks, axis):
    far = {k: shift(chunks[k], axis, k) for k in (2, 1, 3)}
    return [chunks[0], far[1], far[2], far[3]]


def place_query_kernel(place, own, other, out):
    at = 0
    for i, (pairs, axes) in enumerate(PARTS):
        cols = slice(at, at + len(pairs) * PAIR)
        at = cols.stop
        for k in range(4):
            block = lax.rem(place[1 + i] + 4 - k, 4) * 128
            start = pl.multiple_of(place[0] * 512 + block, 128)
            out[pl.ds(start, 128), cols] = own[k, :, cols]
            start = pl.multiple_of((1 - place[0]) * 512 + block, 128)
            out[pl.ds(start, 128), cols] = other[k, :, cols]


def numer_x_kernel(place, n0, n1, n2, n3, s0, s1, s2, s3, fin, z0, z1, z2, z3, total):
    at = pl.ds(pl.multiple_of(place[0] * 256, 256), 256)
    for h in range(H):
        rows = slice(h * HD, (h + 1) * HD)
        pair, j = h // 2, h % 2
        top = fin[pair, 6 + j : 7 + j, at]
        acc = jnp.zeros((HD, 256), F32)
        for n, s in ((n0, s0), (n1, s1), (n2, s2), (n3, s3)):
            acc += n[rows, :] * jnp.exp(s[pair, j : j + 1, at] - top)
        total[rows, :] = acc
    for k, out in enumerate((z0, z1, z2, z3)):
        spot = lax.rem(place[1] + k, 4)
        row = pl.multiple_of(lax.rem(spot, 2) * 640, 640)
        lane = pl.multiple_of(lax.div(spot, 2) * 128, 128)
        out[...] = total[pl.ds(row, 640), pl.ds(lane, 128)]


def numer_z_kernel(place, z0, z1, z2, z3, fin, out):
    spot = place[1]
    at = pl.ds(pl.multiple_of(place[0] * 256 + lax.div(spot, 2) * 128, 128), 128)
    upper = lax.rem(spot, 2) == 1
    rows = four(z0, z1, z2, z3)
    for h in range(5):
        low = fin[h // 2, 4 + h % 2 : 5 + h % 2, at]
        high = fin[(5 + h) // 2, 4 + (5 + h) % 2 : 5 + (5 + h) % 2, at]
        total = jnp.where(upper, high, low)
        out[:, h * HD : (h + 1) * HD] = (rows[h * HD : (h + 1) * HD] / total).T


def round_kernel(x, out):
    out[...] = x[0].astype(BF16)


def on_device(tokens, queries, key_weight, value_weight, out_grad):
    seq, dp = lax.axis_index("seq"), lax.axis_index("dp")
    place = jnp.stack([seq // 4, seq % 4, dp // 2, dp % 2]).astype(jnp.int32)
    own = dict(x=place[0], z=place[1], y=place[2])
    core = place[3]
    grad = out_grad[0]
    vmem = pl.BlockSpec(memory_space=pltpu.VMEM)

    keys, vals, normed, n0, n1, n2, n3, stats = forward(place, tokens[0], key_weight, value_weight, queries, grad)
    near = exchange([stats] * 4, "x")
    numer = exchange([n0, n1, n2, n3], "x")
    orders = [reorder(row_order(place, axes), normed) for _, axes in PARTS]
    group = merged(merge_kernel, near, "merge")
    fin = merged(finish_kernel, exchange([group] * 4, "z"), "finish")

    sums = []
    for (pairs, axes), nt in zip(PARTS, orders):
        mine, theirs = backward(jnp.stack([core, own[axes[0]]]), nt, keys, vals, queries, grad, fin, pairs)
        other = shift(theirs, "c", 1)
        chunks = by_columns(pair_kernel, [mine, other], [448] * 4, "pair")
        sums.append(exchange(chunks, axes[0]))

    zs = pl.pallas_call(
        numer_x_kernel,
        in_specs=[SMEM] + [vmem] * 9,
        out_shape=[jax.ShapeDtypeStruct((640, 128), F32)] * 4,
        scratch_shapes=[pltpu.VMEM((D, 256), F32)],
        compiler_params=params(),
        cost_estimate=cost(1e7, 7e6),
        name="numer_x",
    )(place, *numer, *near, fin)
    share = pl.pallas_call(
        numer_z_kernel,
        in_specs=[SMEM] + [vmem] * 5,
        out_shape=jax.ShapeDtypeStruct((128, 640), F32),
        compiler_params=params(),
        cost_estimate=cost(1e6, 2e6),
        name="numer_z",
    )(place, *exchange(zs, "z"), fin)
    gathered = lax.all_gather(share, "seq")

    queries_out, key_rows, value_rows = [], [], []
    for i, (pairs, axes) in enumerate(PARTS):
        chunks = by_columns(second_kernel, sums[i], [208] * 4, "second")
        chunks = by_columns(third_kernel, exchange(chunks, axes[1]), [152] * 4, "third")
        query, key_part, value_part = by_columns(last_kernel, exchange(chunks, axes[2]), [128, 10, 10], "last")
        queries_out.append(jnp.stack(exchange([query] * 4, axes[0])))
        key_rows.append(key_part)
        value_rows.append(value_part)
    own_query = jnp.concatenate(queries_out, axis=2)
    other_query = shift(own_query, "c", 1)
    query_grad = pl.pallas_call(
        place_query_kernel,
        in_specs=[SMEM, vmem, vmem],
        out_shape=jax.ShapeDtypeStruct((L, D), F32),
        compiler_params=params(),
        cost_estimate=cost(1e6, 1e7),
        name="place_query",
    )(jnp.stack([core] + [own[axes[0]] for _, axes in PARTS]), own_query, other_query)

    attended = pl.pallas_call(
        round_kernel,
        grid=(16,),
        in_specs=[pl.BlockSpec((1, 128, 640), lambda i: (i, 0, 0))],
        out_specs=pl.BlockSpec((128, 640), lambda i: (i // 2, i % 2)),
        out_shape=jax.ShapeDtypeStruct((L, D), BF16),
        compiler_params=params(),
        cost_estimate=cost(1e6, 8e6),
        name="round",
    )(gathered)
    return (
        attended.reshape(1, L, D),
        query_grad,
        jnp.concatenate(key_rows, axis=1),
        jnp.concatenate(value_rows, axis=1),
    )


def solution(mesh):
    placed = (P("dp", "seq", None), P(), P(), P(), P("dp", None, None))
    return jax.shard_map(
        on_device,
        mesh=mesh,
        in_specs=placed,
        out_specs=(P("dp", None, None), P(), P(("seq", "dp"), None), P(("seq", "dp"), None)),
        check_vma=False,
    )
```

time: 528 us -> 354 us (0.67)
  blocking collectives: 120 us -> 0 us
  waiting for transfers between devices: 269 us -> 153 us
  Pallas kernels: 0 us -> 114 us
  matrix products: 78.9 us -> 0 us
  starting transfers between devices: 0.08 us -> 53.2 us
  other arithmetic: 18.4 us -> 4.63 us
  local copies, waits for them, and re-layouts: 27.7 us -> 14 us
    psum x2 -> x0, waiting for transfers between devices: 269 us -> none  [the longest x1 215 us: on_device(): query_grad = lax.psum(query_part, ('seq', 'dp'))]
    ppermute x0 -> x39, waiting for transfers between devices: none -> 153 us  [the longest x15 74.5 us: shift(): lax.ppermute(array, 'seq', [(a * 4 + b, a * 4 + (b + step) % 4) for a in...]
    pallas_call x0 -> x19, Pallas kernels: none -> 114 us  [the longest x8 31.5 us: by_columns(): pl.pallas_call(kernel, grid=(width // PAIR,), in_specs=[spec(a.shape) for...]
    dot_general x9 -> x0, matrix products: 78.9 us -> none  [the longest x1 13.9 us: on_device(): jnp.einsum('hlt,thd->lhd', weights, val_heads, preferred_element_type=jnp...]
    pmax x1 -> x0, blocking collectives: 62.4 us -> none  [on_device(): top = lax.pmax(block_top, 'seq')]
    psum x1 -> x0, blocking collectives: 57.4 us -> none  [on_device(): lax.psum((block_total * factor, block_numer * jnp.transpose(factor)[:, :,...]
    ppermute x0 -> x39, starting transfers between devices: none -> 53.2 us  [the longest x15 20 us: shift(): lax.ppermute(array, 'seq', [(a * 4 + b, a * 4 + (b + step) % 4) for a in...]
    reduce_sum x4 -> x0, other arithmetic: 18.4 us -> none  [the longest x1 9.84 us: on_device(): block_total = jnp.sum(shifted, axis=2)]
  transfers between devices with their start and end apart: 2 -> 40, of which waited for: 2 -> 17; matrix products, arithmetic and copies ran while one was open for 3% -> 1% of each run, Pallas kernels for 0% -> 24%
where the time goes in v1:
time: 354 us; the launch traced here: 353 us
  waiting for transfers between devices  153 us (43%)
  Pallas kernels  114 us (32%)
  starting transfers between devices  53.2 us (15%)
  between operations  14.3 us (4%)
  local copies, waits for them, and re-layouts  14 us (4%)
  other arithmetic  4.63 us (1%)
    ppermute x15, waiting for transfers between devices, shift(): lax.ppermute(array, 'seq', [(a * 4 + b, a * 4 + (b + step) % 4) for a in...  74.5 us
    ppermute x12, waiting for transfers between devices, shift(): lax.ppermute(array, 'seq', [(a * 4 + b, (a + step) % 4 * 4 + b) for a in...  58.9 us
    pallas_call x8, Pallas kernels, by_columns(): pl.pallas_call(kernel, grid=(width // PAIR,), in_specs=[spec(a.shape) for...  31.5 us
    pallas_call x2, Pallas kernels, backward(): pl.pallas_call(backward_kernel, grid=(len(pairs),), in_specs=[SMEM, full(...  27.2 us
    pallas_call x1, Pallas kernels, forward(): pl.pallas_call(forward_kernel, grid=(H // 2,), in_specs=[SMEM, full((T, D...  20.7 us
    ppermute x15, starting transfers between devices, shift(): lax.ppermute(array, 'seq', [(a * 4 + b, a * 4 + (b + step) % 4) for a in...  20 us
    ppermute x12, starting transfers between devices, shift(): lax.ppermute(array, 'seq', [(a * 4 + b, (a + step) % 4 * 4 + b) for a in...  19 us
    ppermute x9, waiting for transfers between devices, shift(): lax.ppermute(array, 'dp', [(a * 2 + b, (a + step) % 4 * 2 + b) for a in r...  16.8 us
  transfers between devices with their start and end apart: 40, of which 17 were waited for; matrix products, arithmetic and copies ran while one was open for 1% of the time, Pallas kernels for 24%

profile of v1, /device:TPU:1, one launch (start us, length us, event | category | flops | bytes accessed | tf_op | source)
XLA Modules:
  0.0 353.0 jit_solution(2889609900091317042)
XLA Ops:
  7.9 20.7 %forward.1 = (bf16[512,1280]{1,0:T(8,128)(2,1)}, bf16[512,1280]{1,0:T(8,128)(2,1)}, bf16[512,1280]{1,0:T(8,128)(2,1)}, f32[1280,256]{1,0:T(8,128)}, f32[1280,256...) custom-call(s32[4]{0:T(128)} %pad_add_fusion.place, bf16[512,1280]{1,0:T(8,128)(2,1)} %bitcast.29, ...), custom_call_target="tpu_custom_call" | custom-call | flops 12000000000 | bytes 24000000 | tf_op jit(solution)/shard_map/forward/pallas_call | solution.py:94
  28.6 3.4 collective-permute-start.5
  36.4 30.3 %collective-permute-done.5.s3 = f32[5,8,1024]{2,1,0:T(8,128)S(1)} collective-permute-done((f32[5,8,1024]{2,1,0:T(8,128)}, f32[5,8,1024]{2,1,0:T(8,128)S(1)}, u32[]{:S(2)}, u32[]{:S(2)}) %collective-permute-start.5) | collective-permute-done | bytes 163872 | tf_op jit(solution)/shard_map/ppermute | solution.py:26
  72.8 4.5 %reorder.2.nt = bf16[1280,512]{1,0:T(8,128)(2,1)} custom-call(s32[1,1280]{1,0:T(1,128)} %reshape.18.order, bf16[512,1280]{1,0:T(8,128)(2,1)} %get-tuple-element.59.normed), custom_call_target="tpu_custom_call" | custom-call | flops 1677721600 | bytes 3000000 | tf_op jit(solution)/shard_map/reorder/pallas_call | solution.py:160
  77.3 6.5 %collective-permute-start.2 = (f32[1280,256]{1,0:T(8,128)S(1)}, f32[1280,256]{1,0:T(8,128)S(1)}, u32[]{:S(2)}, u32[]{:S(2)}) collective-permute-start(f32[1280,256]{1,0:T(8,128)S(1)} %copy-done.41), channel_id=1, source_target_pairs={{0,96},{8,104},{16,112},{24,120},{32,0},{40,8},{48,16},{56,24},{64... | collective-permute-start | bytes 3932168 | tf_op jit(solution)/shard_map/ppermute | solution.py:26
  87.2 15.5 %backward.2 = (f32[4,448,768]{2,1,0:T(8,128)}, f32[4,448,768]{2,1,0:T(8,128)}) custom-call(s32[2]{0:T(128)} %get-tuple-element.98.place, bf16[1280,512]{1,0:T(8,128)(2,1)} %reorder.2.nt, bf16[512,1280]{1,0:T(8,128)(2,1)} %get-tuple-element.60.keys, bf16[512,1280]{1,0:T(8,128)(2,1)} %get-tuple-element.61.vals, bf16[1024,1280]{1,0:T(8,128)(2,1)} %q.5, ...), custom_call_target="tpu_custom_call" | custom-call | flops 9600000000 | bytes 12000000 | tf_op jit(solution)/shard_map/backward/pallas_call | solution.py:209
  106.1 4.3 %reorder.3.nt = bf16[1280,512]{1,0:T(8,128)(2,1)} custom-call(s32[1,1280]{1,0:T(1,128)} %reshape.19.order, bf16[512,1280]{1,0:T(8,128)(2,1)} %get-tuple-element.59.normed), custom_call_target="tpu_custom_call" | custom-call | flops 1677721600 | bytes 3000000 | tf_op jit(solution)/shard_map/reorder/pallas_call | solution.py:160
  110.4 11.7 %backward.3 = (f32[4,448,512]{2,1,0:T(8,128)}, f32[4,448,512]{2,1,0:T(8,128)}) custom-call(s32[2]{0:T(128)} %get-tuple-element.99.place, bf16[1280,512]{1,0:T(8,128)(2,1)} %reorder.3.nt, bf16[512,1280]{1,0:T(8,128)(2,1)} %get-tuple-element.60.keys, bf16[512,1280]{1,0:T(8,128)(2,1)} %get-tuple-element.61.vals, bf16[1024,1280]{1,0:T(8,128)(2,1)} %q.5, ...), custom_call_target="tpu_custom_call" | custom-call | flops 6400000000 | bytes 8000000 | tf_op jit(solution)/shard_map/backward/pallas_call | solution.py:209
  124.1 4.3 %numer_x.1 = (f32[640,128]{1,0:T(8,128)}, f32[640,128]{1,0:T(8,128)}, f32[640,128]{1,0:T(8,128)}, f32[640,128]{1,0:T(8,128)}) custom-call(s32[4]{0:T(128)} %pad_add_fusion.place, f32[1280,256]{1,0:T(8,128)} %get-tuple-element.50.n0, f32[1280,256]{1,0:T(8,128)} %copy-done.5, f32[1280,256]{1,0:T(8,128)} %copy-done.6, f32[1280,256]{1,0:T(8,128)} %copy-done.7, ...), custom_call_target="tpu_custom_call" | custom-call | flops 10000000 | bytes 7000000 | tf_op jit(solution)/shard_map/numer_x/pallas_call | solution.py:350
  132.7 5.8 %collective-permute-done.9.z1 = f32[640,128]{1,0:T(8,128)S(1)} collective-permute-done((f32[640,128]{1,0:T(8,128)}, f32[640,128]{1,0:T(8,128)S(1)}, u32[]{:S(2)}, u32[]{:S(2)}) %collective-permute-start.9) | collective-permute-done | bytes 327712 | tf_op jit(solution)/shard_map/ppermute | solution.py:28
  138.6 8.1 %collective-permute-done.10.z2 = f32[640,128]{1,0:T(8,128)S(1)} collective-permute-done((f32[640,128]{1,0:T(8,128)}, f32[640,128]{1,0:T(8,128)S(1)}, u32[]{:S(2)}, u32[]{:S(2)}) %collective-permute-start.10) | collective-permute-done | bytes 327712 | tf_op jit(solution)/shard_map/ppermute | solution.py:28
  149.8 4.6 %pair.3 = (f32[448,512]{1,0:T(8,128)}, f32[448,512]{1,0:T(8,128)}, f32[448,512]{1,0:T(8,128)}, f32[448,512]{1,0:T(8,128)}) custom-call(f32[4,448,512]{2,1,0:T(8,128)} %get-tuple-element.77.mine, f32[4,448,512]{2,1,0:T(8,128)} %collective-permute-done.25.other), custom_call_target="tpu_custom_call" | custom-call | flops 1000000 | bytes 11010048 | tf_op jit(solution)/shard_map/pair/pallas_call | solution.py:232
  155.9 7.6 %pair.2 = (f32[448,768]{1,0:T(8,128)}, f32[448,768]{1,0:T(8,128)}, f32[448,768]{1,0:T(8,128)}, f32[448,768]{1,0:T(8,128)}) custom-call(f32[4,448,768]{2,1,0:T(8,128)} %get-tuple-element.62.mine, f32[4,448,768]{2,1,0:T(8,128)} %collective-permute-done.12.other), custom_call_target="tpu_custom_call" | custom-call | flops 1000000 | bytes 16515072 | tf_op jit(solution)/shard_map/pair/pallas_call | solution.py:232
  170.7 10.9 %collective-permute-done.26.a1 = f32[448,512]{1,0:T(8,128)S(1)} collective-permute-done((f32[448,512]{1,0:T(8,128)}, f32[448,512]{1,0:T(8,128)S(1)}, u32[]{:S(2)}, u32[]{:S(2)}) %collective-permute-start.26) | collective-permute-done | bytes 917536 | tf_op jit(solution)/shard_map/ppermute | solution.py:28
  184.1 19.3 %collective-permute-done.27.a2 = f32[448,512]{1,0:T(8,128)S(1)} collective-permute-done((f32[448,512]{1,0:T(8,128)}, f32[448,512]{1,0:T(8,128)S(1)}, u32[]{:S(2)}, u32[]{:S(2)}) %collective-permute-start.27) | collective-permute-done | bytes 917536 | tf_op jit(solution)/shard_map/ppermute | solution.py:28
  203.3 19.5 %collective-permute-done.28.a3 = f32[448,512]{1,0:T(8,128)S(1)} collective-permute-done((f32[448,512]{1,0:T(8,128)S(1)}, f32[448,512]{1,0:T(8,128)S(1)}, u32[]{:S(2)}, u32[]{:S(2)}) %collective-permute-start.28) | collective-permute-done | bytes 917536 | tf_op jit(solution)/shard_map/ppermute | solution.py:28
  223.8 3.1 second.3
  231.2 4.8 %second.2 = (f32[208,768]{1,0:T(8,128)}, f32[208,768]{1,0:T(8,128)}, f32[208,768]{1,0:T(8,128)}, f32[208,768]{1,0:T(8,128)}) custom-call(f32[448,768]{1,0:T(8,128)} %get-tuple-element.64.a0, f32[448,768]{1,0:T(8,128)} %copy-done.2, f32[448,768]{1,0:T(8,128)} %copy-done.3, f32[448,768]{1,0:T(8,128)} %copy-done.4), custom_call_target="tpu_custom_call" | custom-call | flops 1000000 | bytes 8060928 | tf_op jit(solution)/shard_map/second/pallas_call | solution.py:232
  236.5 11.1 %collective-permute-done.29.a1 = f32[208,512]{1,0:T(8,128)S(1)} collective-permute-done((f32[208,512]{1,0:T(8,128)}, f32[208,512]{1,0:T(8,128)S(1)}, u32[]{:S(2)}, u32[]{:S(2)}) %collective-permute-start.29) | collective-permute-done | bytes 426016 | tf_op jit(solution)/shard_map/ppermute | solution.py:30
  254.1 8.5 %collective-permute-done.17.a2 = f32[208,768]{1,0:T(8,128)S(1)} collective-permute-done((f32[208,768]{1,0:T(8,128)}, f32[208,768]{1,0:T(8,128)S(1)}, u32[]{:S(2)}, u32[]{:S(2)}) %collective-permute-start.17) | collective-permute-done | bytes 639008 | tf_op jit(solution)/shard_map/ppermute | solution.py:26
  262.7 4.4 %collective-permute-done.18.a3 = f32[208,768]{1,0:T(8,128)S(1)} collective-permute-done((f32[208,768]{1,0:T(8,128)}, f32[208,768]{1,0:T(8,128)S(1)}, u32[]{:S(2)}, u32[]{:S(2)}) %collective-permute-start.18) | collective-permute-done | bytes 639008 | tf_op jit(solution)/shard_map/ppermute | solution.py:26
  267.9 3.8 %third.2 = (f32[152,768]{1,0:T(8,128)}, f32[152,768]{1,0:T(8,128)}, f32[152,768]{1,0:T(8,128)}, f32[152,768]{1,0:T(8,128)}) custom-call(f32[208,768]{1,0:T(8,128)} %get-tuple-element.68.a0, f32[208,768]{1,0:T(8,128)} %copy-done.14, f32[208,768]{1,0:T(8,128)} %copy-done.15, f32[208,768]{1,0:T(8,128)} %copy-done.16), custom_call_target="tpu_custom_call" | custom-call | flops 1000000 | bytes 4423680 | tf_op jit(solution)/shard_map/third/pallas_call | solution.py:232
  272.4 4.1 %collective-permute-start.20 = (f32[152,768]{1,0:T(8,128)}, f32[152,768]{1,0:T(8,128)S(1)}, u32[]{:S(2)}, u32[]{:S(2)}) collective-permute-start(f32[152,768]{1,0:T(8,128)} %get-tuple-element.74), channel_id=1, source_target_pairs={{0,16},{8,24},{16,0},{24,8},{32,48},{40,56},{48,32},{56,40},{64,80... | collective-permute-start | bytes 1400840 | tf_op jit(solution)/shard_map/ppermute | solution.py:28
  279.9 4.1 %collective-permute-done.33.a2 = f32[152,512]{1,0:T(8,128)S(1)} collective-permute-done((f32[152,512]{1,0:T(8,128)}, f32[152,512]{1,0:T(8,128)S(1)}, u32[]{:S(2)}, u32[]{:S(2)}) %collective-permute-start.33) | collective-permute-done | bytes 311328 | tf_op jit(solution)/shard_map/ppermute | solution.py:26
  283.9 9.8 %collective-permute-done.34.a3 = f32[152,512]{1,0:T(8,128)S(1)} collective-permute-done((f32[152,512]{1,0:T(8,128)}, f32[152,512]{1,0:T(8,128)S(1)}, u32[]{:S(2)}, u32[]{:S(2)}) %collective-permute-start.34) | collective-permute-done | bytes 311328 | tf_op jit(solution)/shard_map/ppermute | solution.py:26
  297.9 3.1 last.2
  304.1 3.0 collective-permute-start.36
  307.1 4.3 %collective-permute-done.36 = f32[128,512]{1,0:T(8,128)S(1)} collective-permute-done((f32[128,512]{1,0:T(8,128)}, f32[128,512]{1,0:T(8,128)S(1)}, u32[]{:S(2)}, u32[]{:S(2)}) %collective-permute-start.36) | collective-permute-done | bytes 262176 | tf_op jit(solution)/shard_map/ppermute | solution.py:28
  311.4 6.6 %collective-permute-done.35 = f32[128,512]{1,0:T(8,128)S(1)} collective-permute-done((f32[128,512]{1,0:T(8,128)}, f32[128,512]{1,0:T(8,128)S(1)}, u32[]{:S(2)}, u32[]{:S(2)}) %collective-permute-start.35) | collective-permute-done | bytes 262176 | tf_op jit(solution)/shard_map/ppermute | solution.py:28
  318.0 4.9 %collective-permute-done.22 = f32[128,768]{1,0:T(8,128)S(1)} collective-permute-done((f32[128,768]{1,0:T(8,128)}, f32[128,768]{1,0:T(8,128)S(1)}, u32[]{:S(2)}, u32[]{:S(2)}) %collective-permute-start.22) | collective-permute-done | bytes 393248 | tf_op jit(solution)/shard_map/ppermute | solution.py:30
  330.8 5.2 %place_query.1 = f32[1024,1280]{1,0:T(8,128)} custom-call(s32[3]{0:T(128)} %pad_add_fusion.1.place, f32[4,128,1280]{2,1,0:T(8,128)} %copy-done, f32[4,128,1280]{2,1,0:T(8,128)} %copy-done.1), custom_call_target="tpu_custom_call" | custom-call | flops 1000000 | bytes 10000000 | tf_op jit(solution)/shard_map/place_query/pallas_call | solution.py:379
  336.1 10.0 %round.1 = bf16[1024,1280]{1,0:T(8,128)(2,1)} custom-call(f32[16,128,640]{2,1,0:T(8,128)} %bitcast.16), custom_call_target="tpu_custom_call" | custom-call | flops 1000000 | bytes 8000000 | tf_op jit(solution)/shard_map/round/pallas_call | solution.py:388
  (163 shorter events, 70.8 us)
Async XLA Ops:
  7.2 328.9 %all-gather.3.cloned.1.call-start = ((), (), s32[]{:S(2)}) async-start(), calls=%async_computation | async-start | bytes 5570560 | tf_op jit(solution)/shard_map/all_gather | solution.py:367
  28.6 38.2 %collective-permute-start.5 = (f32[5,8,1024]{2,1,0:T(8,128)}, f32[5,8,1024]{2,1,0:T(8,128)S(1)}, u32[]{:S(2)}, u32[]{:S(2)}) collective-permute-start(f32[5,8,1024]{2,1,0:T(8,128)} %get-tuple-element.54.s0), channel_id=1, source_target_pairs={{0,96},{8,104},{16,112},{24,120},{32,0},{40,8},{48,16},{56,24},{64... | collective-permute-start | bytes 491528 | tf_op jit(solution)/shard_map/ppermute | solution.py:26
  32.0 34.8 %collective-permute-start.4 = (f32[5,8,1024]{2,1,0:T(8,128)}, f32[5,8,1024]{2,1,0:T(8,128)S(1)}, u32[]{:S(2)}, u32[]{:S(2)}) collective-permute-start(f32[5,8,1024]{2,1,0:T(8,128)} %get-tuple-element.54.s0), channel_id=1, source_target_pairs={{0,64},{8,72},{16,80},{24,88},{32,96},{40,104},{48,112},{56,120},{... | collective-permute-start | bytes 491528 | tf_op jit(solution)/shard_map/ppermute | solution.py:26
  32.5 34.3 %collective-permute-start.3 = (f32[5,8,1024]{2,1,0:T(8,128)}, f32[5,8,1024]{2,1,0:T(8,128)S(1)}, u32[]{:S(2)}, u32[]{:S(2)}) collective-permute-start(f32[5,8,1024]{2,1,0:T(8,128)} %get-tuple-element.54.s0), channel_id=1, source_target_pairs={{0,32},{8,40},{16,48},{24,56},{32,64},{40,72},{48,80},{56,88},{64,... | collective-permute-start | bytes 491528 | tf_op jit(solution)/shard_map/ppermute | solution.py:26
  33.1 89.0 %collective-permute-start = (f32[1280,256]{1,0:T(8,128)}, f32[1280,256]{1,0:T(8,128)S(1)}, u32[]{:S(2)}, u32[]{:S(2)}) collective-permute-start(f32[1280,256]{1,0:T(8,128)} %get-tuple-element.51), channel_id=1, source_target_pairs={{0,32},{8,40},{16,48},{24,56},{32,64},{40,72},{48,80},{56,88},{64,... | collective-permute-start | bytes 3932168 | tf_op jit(solution)/shard_map/ppermute | solution.py:26
  34.6 87.5 %collective-permute-start.1 = (f32[1280,256]{1,0:T(8,128)}, f32[1280,256]{1,0:T(8,128)S(1)}, u32[]{:S(2)}, u32[]{:S(2)}) collective-permute-start(f32[1280,256]{1,0:T(8,128)} %get-tuple-element.52), channel_id=1, source_target_pairs={{0,64},{8,72},{16,80},{24,88},{32,96},{40,104},{48,112},{56,120},{... | collective-permute-start | bytes 3932168 | tf_op jit(solution)/shard_map/ppermute | solution.py:26
  70.2 13.7 %collective-permute-start.6 = (f32[5,8,1024]{2,1,0:T(8,128)}, f32[5,8,1024]{2,1,0:T(8,128)S(1)}, u32[]{:S(2)}, u32[]{:S(2)}) collective-permute-start(f32[5,8,1024]{2,1,0:T(8,128)} %merge.1.s0), channel_id=1, source_target_pairs={{0,8},{8,16},{16,24},{24,0},{32,40},{40,48},{48,56},{56,32},{64,72... | collective-permute-start | bytes 491528 | tf_op jit(solution)/shard_map/ppermute | solution.py:28
  77.3 44.8 %collective-permute-start.2 = (f32[1280,256]{1,0:T(8,128)S(1)}, f32[1280,256]{1,0:T(8,128)S(1)}, u32[]{:S(2)}, u32[]{:S(2)}) collective-permute-start(f32[1280,256]{1,0:T(8,128)S(1)} %copy-done.41), channel_id=1, source_target_pairs={{0,96},{8,104},{16,112},{24,120},{32,0},{40,8},{48,16},{56,24},{64... | collective-permute-start | bytes 3932168 | tf_op jit(solution)/shard_map/ppermute | solution.py:26
  102.8 53.1 %collective-permute-start.12 = (f32[4,448,768]{2,1,0:T(8,128)}, f32[4,448,768]{2,1,0:T(8,128)}, u32[]{:S(2)}, u32[]{:S(2)}) collective-permute-start(f32[4,448,768]{2,1,0:T(8,128)} %get-tuple-element.63), channel_id=1, source_target_pairs={{0,1},{1,0},{2,3},{3,2},{4,5},{5,4},{6,7},{7,6},{8,9},{9,8},{10,11... | collective-permute-start | bytes 16515080 | tf_op jit(solution)/shard_map/ppermute | solution.py:31
  122.1 27.7 %collective-permute-start.25 = (f32[4,448,512]{2,1,0:T(8,128)}, f32[4,448,512]{2,1,0:T(8,128)}, u32[]{:S(2)}, u32[]{:S(2)}) collective-permute-start(f32[4,448,512]{2,1,0:T(8,128)} %get-tuple-element.78), channel_id=1, source_target_pairs={{0,1},{1,0},{2,3},{3,2},{4,5},{5,4},{6,7},{7,6},{8,9},{9,8},{10,11... | collective-permute-start | bytes 11010056 | tf_op jit(solution)/shard_map/ppermute | solution.py:31
  130.3 16.3 %collective-permute-start.10 = (f32[640,128]{1,0:T(8,128)}, f32[640,128]{1,0:T(8,128)S(1)}, u32[]{:S(2)}, u32[]{:S(2)}) collective-permute-start(f32[640,128]{1,0:T(8,128)} %get-tuple-element.57), channel_id=1, source_target_pairs={{0,16},{8,24},{16,0},{24,8},{32,48},{40,56},{48,32},{56,40},{64,80... | collective-permute-start | bytes 983048 | tf_op jit(solution)/shard_map/ppermute | solution.py:28
  132.1 14.6 %collective-permute-start.11 = (f32[640,128]{1,0:T(8,128)}, f32[640,128]{1,0:T(8,128)S(1)}, u32[]{:S(2)}, u32[]{:S(2)}) collective-permute-start(f32[640,128]{1,0:T(8,128)} %get-tuple-element.58), channel_id=1, source_target_pairs={{0,24},{8,0},{16,8},{24,16},{32,56},{40,32},{48,40},{56,48},{64,88... | collective-permute-start | bytes 983048 | tf_op jit(solution)/shard_map/ppermute | solution.py:28
  154.4 27.2 %collective-permute-start.26 = (f32[448,512]{1,0:T(8,128)}, f32[448,512]{1,0:T(8,128)S(1)}, u32[]{:S(2)}, u32[]{:S(2)}) collective-permute-start(f32[448,512]{1,0:T(8,128)} %get-tuple-element.80), channel_id=1, source_target_pairs={{0,8},{8,16},{16,24},{24,0},{32,40},{40,48},{48,56},{56,32},{64,72... | collective-permute-start | bytes 2752520 | tf_op jit(solution)/shard_map/ppermute | solution.py:28
  163.4 63.7 %collective-permute-start.13 = (f32[448,768]{1,0:T(8,128)}, f32[448,768]{1,0:T(8,128)S(1)}, u32[]{:S(2)}, u32[]{:S(2)}) collective-permute-start(f32[448,768]{1,0:T(8,128)} %get-tuple-element.65), channel_id=1, source_target_pairs={{0,2},{1,3},{2,4},{3,5},{4,6},{5,7},{6,0},{7,1},{8,10},{9,11},{10,... | collective-permute-start | bytes 4128776 | tf_op jit(solution)/shard_map/ppermute | solution.py:30
  164.7 64.9 %collective-permute-start.14 = (f32[448,768]{1,0:T(8,128)}, f32[448,768]{1,0:T(8,128)S(1)}, u32[]{:S(2)}, u32[]{:S(2)}) collective-permute-start(f32[448,768]{1,0:T(8,128)} %get-tuple-element.66), channel_id=1, source_target_pairs={{0,4},{1,5},{2,6},{3,7},{4,0},{5,1},{6,2},{7,3},{8,12},{9,13},{10,... | collective-permute-start | bytes 4128776 | tf_op jit(solution)/shard_map/ppermute | solution.py:30
  167.4 62.3 %collective-permute-start.15 = (f32[448,768]{1,0:T(8,128)}, f32[448,768]{1,0:T(8,128)S(1)}, u32[]{:S(2)}, u32[]{:S(2)}) collective-permute-start(f32[448,768]{1,0:T(8,128)} %get-tuple-element.67), channel_id=1, source_target_pairs={{0,6},{1,7},{2,0},{3,1},{4,2},{5,3},{6,4},{7,5},{8,14},{9,15},{10,... | collective-permute-start | bytes 4128776 | tf_op jit(solution)/shard_map/ppermute | solution.py:30
  168.4 34.9 %collective-permute-start.27 = (f32[448,512]{1,0:T(8,128)}, f32[448,512]{1,0:T(8,128)S(1)}, u32[]{:S(2)}, u32[]{:S(2)}) collective-permute-start(f32[448,512]{1,0:T(8,128)} %get-tuple-element.81), channel_id=1, source_target_pairs={{0,16},{8,24},{16,0},{24,8},{32,48},{40,56},{48,32},{56,40},{64,80... | collective-permute-start | bytes 2752520 | tf_op jit(solution)/shard_map/ppermute | solution.py:28
  181.6 41.2 %collective-permute-start.28 = (f32[448,512]{1,0:T(8,128)S(1)}, f32[448,512]{1,0:T(8,128)S(1)}, u32[]{:S(2)}, u32[]{:S(2)}) collective-permute-start(f32[448,512]{1,0:T(8,128)S(1)} %copy-done.42), channel_id=1, source_target_pairs={{0,24},{8,0},{16,8},{24,16},{32,56},{40,32},{48,40},{56,48},{64,88... | collective-permute-start | bytes 2752520 | tf_op jit(solution)/shard_map/ppermute | solution.py:28
  226.9 20.7 %collective-permute-start.29 = (f32[208,512]{1,0:T(8,128)}, f32[208,512]{1,0:T(8,128)S(1)}, u32[]{:S(2)}, u32[]{:S(2)}) collective-permute-start(f32[208,512]{1,0:T(8,128)} %get-tuple-element.84), channel_id=1, source_target_pairs={{0,2},{1,3},{2,4},{3,5},{4,6},{5,7},{6,0},{7,1},{8,10},{9,11},{10,... | collective-permute-start | bytes 1277960 | tf_op jit(solution)/shard_map/ppermute | solution.py:30
  227.1 20.5 %collective-permute-start.30 = (f32[208,512]{1,0:T(8,128)}, f32[208,512]{1,0:T(8,128)S(1)}, u32[]{:S(2)}, u32[]{:S(2)}) collective-permute-start(f32[208,512]{1,0:T(8,128)} %get-tuple-element.85), channel_id=1, source_target_pairs={{0,4},{1,5},{2,6},{3,7},{4,0},{5,1},{6,2},{7,3},{8,12},{9,13},{10,... | collective-permute-start | bytes 1277960 | tf_op jit(solution)/shard_map/ppermute | solution.py:30
  227.1 21.3 %collective-permute-start.31 = (f32[208,512]{1,0:T(8,128)}, f32[208,512]{1,0:T(8,128)S(1)}, u32[]{:S(2)}, u32[]{:S(2)}) collective-permute-start(f32[208,512]{1,0:T(8,128)} %get-tuple-element.86), channel_id=1, source_target_pairs={{0,6},{1,7},{2,0},{3,1},{4,2},{5,3},{6,4},{7,5},{8,14},{9,15},{10,... | collective-permute-start | bytes 1277960 | tf_op jit(solution)/shard_map/ppermute | solution.py:30
  236.0 18.2 %collective-permute-start.16 = (f32[208,768]{1,0:T(8,128)}, f32[208,768]{1,0:T(8,128)S(1)}, u32[]{:S(2)}, u32[]{:S(2)}) collective-permute-start(f32[208,768]{1,0:T(8,128)} %get-tuple-element.69), channel_id=1, source_target_pairs={{0,32},{8,40},{16,48},{24,56},{32,64},{40,72},{48,80},{56,88},{64,... | collective-permute-start | bytes 1916936 | tf_op jit(solution)/shard_map/ppermute | solution.py:26
  236.0 26.7 %collective-permute-start.17 = (f32[208,768]{1,0:T(8,128)}, f32[208,768]{1,0:T(8,128)S(1)}, u32[]{:S(2)}, u32[]{:S(2)}) collective-permute-start(f32[208,768]{1,0:T(8,128)} %get-tuple-element.70), channel_id=1, source_target_pairs={{0,64},{8,72},{16,80},{24,88},{32,96},{40,104},{48,112},{56,120},{... | collective-permute-start | bytes 1916936 | tf_op jit(solution)/shard_map/ppermute | solution.py:26
  247.6 19.4 %collective-permute-start.18 = (f32[208,768]{1,0:T(8,128)}, f32[208,768]{1,0:T(8,128)S(1)}, u32[]{:S(2)}, u32[]{:S(2)}) collective-permute-start(f32[208,768]{1,0:T(8,128)} %get-tuple-element.71), channel_id=1, source_target_pairs={{0,96},{8,104},{16,112},{24,120},{32,0},{40,8},{48,16},{56,24},{64... | collective-permute-start | bytes 1916936 | tf_op jit(solution)/shard_map/ppermute | solution.py:26
  251.6 25.5 %collective-permute-start.32 = (f32[152,512]{1,0:T(8,128)}, f32[152,512]{1,0:T(8,128)S(1)}, u32[]{:S(2)}, u32[]{:S(2)}) collective-permute-start(f32[152,512]{1,0:T(8,128)} %get-tuple-element.88), channel_id=1, source_target_pairs={{0,32},{8,40},{16,48},{24,56},{32,64},{40,72},{48,80},{56,88},{64,... | collective-permute-start | bytes 933896 | tf_op jit(solution)/shard_map/ppermute | solution.py:26
  271.7 25.0 %collective-permute-start.19 = (f32[152,768]{1,0:T(8,128)}, f32[152,768]{1,0:T(8,128)S(1)}, u32[]{:S(2)}, u32[]{:S(2)}) collective-permute-start(f32[152,768]{1,0:T(8,128)} %get-tuple-element.73), channel_id=1, source_target_pairs={{0,8},{8,16},{16,24},{24,0},{32,40},{40,48},{48,56},{56,32},{64,72... | collective-permute-start | bytes 1400840 | tf_op jit(solution)/shard_map/ppermute | solution.py:28
  272.4 24.4 %collective-permute-start.20 = (f32[152,768]{1,0:T(8,128)}, f32[152,768]{1,0:T(8,128)S(1)}, u32[]{:S(2)}, u32[]{:S(2)}) collective-permute-start(f32[152,768]{1,0:T(8,128)} %get-tuple-element.74), channel_id=1, source_target_pairs={{0,16},{8,24},{16,0},{24,8},{32,48},{40,56},{48,32},{56,40},{64,80... | collective-permute-start | bytes 1400840 | tf_op jit(solution)/shard_map/ppermute | solution.py:28
  276.5 20.3 %collective-permute-start.21 = (f32[152,768]{1,0:T(8,128)}, f32[152,768]{1,0:T(8,128)S(1)}, u32[]{:S(2)}, u32[]{:S(2)}) collective-permute-start(f32[152,768]{1,0:T(8,128)} %get-tuple-element.75), channel_id=1, source_target_pairs={{0,24},{8,0},{16,8},{24,16},{32,56},{40,32},{48,40},{56,48},{64,88... | collective-permute-start | bytes 1400840 | tf_op jit(solution)/shard_map/ppermute | solution.py:28
  277.1 16.6 %collective-permute-start.34 = (f32[152,512]{1,0:T(8,128)}, f32[152,512]{1,0:T(8,128)S(1)}, u32[]{:S(2)}, u32[]{:S(2)}) collective-permute-start(f32[152,512]{1,0:T(8,128)} %get-tuple-element.90), channel_id=1, source_target_pairs={{0,96},{8,104},{16,112},{24,120},{32,0},{40,8},{48,16},{56,24},{64... | collective-permute-start | bytes 933896 | tf_op jit(solution)/shard_map/ppermute | solution.py:26
  301.0 17.0 %collective-permute-start.24 = (f32[128,768]{1,0:T(8,128)}, f32[128,768]{1,0:T(8,128)S(1)}, u32[]{:S(2)}, u32[]{:S(2)}) collective-permute-start(f32[128,768]{1,0:T(8,128)} %get-tuple-element.76), channel_id=1, source_target_pairs={{0,6},{1,7},{2,0},{3,1},{4,2},{5,3},{6,4},{7,5},{8,14},{9,15},{10,... | collective-permute-start | bytes 1179656 | tf_op jit(solution)/shard_map/ppermute | solution.py:30
  301.8 16.3 %collective-permute-start.23 = (f32[128,768]{1,0:T(8,128)}, f32[128,768]{1,0:T(8,128)S(1)}, u32[]{:S(2)}, u32[]{:S(2)}) collective-permute-start(f32[128,768]{1,0:T(8,128)} %get-tuple-element.76), channel_id=1, source_target_pairs={{0,4},{1,5},{2,6},{3,7},{4,0},{5,1},{6,2},{7,3},{8,12},{9,13},{10,... | collective-permute-start | bytes 1179656 | tf_op jit(solution)/shard_map/ppermute | solution.py:30
  303.8 19.2 %collective-permute-start.22 = (f32[128,768]{1,0:T(8,128)}, f32[128,768]{1,0:T(8,128)S(1)}, u32[]{:S(2)}, u32[]{:S(2)}) collective-permute-start(f32[128,768]{1,0:T(8,128)} %get-tuple-element.76), channel_id=1, source_target_pairs={{0,2},{1,3},{2,4},{3,5},{4,6},{5,7},{6,0},{7,1},{8,10},{9,11},{10,... | collective-permute-start | bytes 1179656 | tf_op jit(solution)/shard_map/ppermute | solution.py:30
  (51 other events, 405.4 us)
Sparse Core Ops, SparseCore 0:
  149.9 83.5 all-gather.2

commit v2 on v1

v2 whole, which is shorter than its diff:
```python
import functools

import jax
import jax.numpy as jnp
import numpy as np
from jax import lax
from jax.experimental import pallas as pl
from jax.experimental.pallas import tpu as pltpu
from jax.sharding import PartitionSpec as P

H = 10
HD = 128
T = 512
L = 1024
D = 1280
PAIR = 2 * HD
SCALE = HD ** (-0.5)
VMEM_LIMIT = 56 * 1024 * 1024
PAIRS = H // 2
Z_GROUPS = [[a * 4 + b for b in range(4)] for a in range(4)]
Y_GROUPS = [[a * 2 + b for a in range(4)] for b in range(2)]
F32 = jnp.float32
BF16 = jnp.bfloat16


def shift(array, axis, step):
    if axis == "x":
        return lax.ppermute(array, "seq", [(a * 4 + b, (a + step) % 4 * 4 + b) for a in range(4) for b in range(4)])
    if axis == "z":
        return lax.ppermute(array, "seq", [(a * 4 + b, a * 4 + (b + step) % 4) for a in range(4) for b in range(4)])
    if axis == "y":
        return lax.ppermute(array, "dp", [(a * 2 + b, (a + step) % 4 * 2 + b) for a in range(4) for b in range(2)])
    return lax.ppermute(array, "dp", [(a * 2 + b, a * 2 + 1 - b) for a in range(4) for b in range(2)])


def nt_dot(a, b):
    return lax.dot_general(a, b, (((1,), (1,)), ((), ())), preferred_element_type=F32)


def dot(a, b):
    return jnp.dot(a, b, preferred_element_type=F32)


def params():
    return pltpu.CompilerParams(vmem_limit_bytes=VMEM_LIMIT)


def cost(flops, moved):
    return pl.CostEstimate(flops=int(flops), bytes_accessed=int(moved), transcendentals=0)


def full(shape):
    return pl.BlockSpec(shape, lambda *_: (0,) * len(shape))


SMEM = pl.BlockSpec(memory_space=pltpu.SMEM)


def forward_kernel(place, tok, kw, vw, q, g, k_out, v_out, normed_out, n0, n1, n2, n3, stats, normed, s, w, numer):
    @pl.when(pl.program_id(0) == 0)
    def _():
        values = tok[...].astype(F32)
        centre = values - jnp.mean(values, axis=-1, keepdims=True)
        spread = jnp.mean(centre * centre, axis=-1, keepdims=True)
        normed[...] = (centre * lax.rsqrt(spread + 1e-05)).astype(BF16)
        normed_out[...] = normed[...]

    keys = dot(normed[...], kw[...]).astype(BF16)
    vals = dot(normed[...], vw[...]).astype(BF16)
    k_out[...] = keys
    v_out[...] = vals
    vals_t = vals.T
    grad_t = g[...].T
    for j in range(2):
        head = slice(j * HD, (j + 1) * HD)
        s[j] = nt_dot(keys[:, head], q[:, head])
        tops, totals = [], []
        for tile in range(L // 128):
            at = slice(tile * 128, (tile + 1) * 128)
            scores = s[j, :, at] * SCALE
            high = jnp.max(scores, axis=0, keepdims=True)
            shifted = jnp.exp(scores - high)
            tops.append(high)
            totals.append(jnp.sum(shifted, axis=0, keepdims=True))
            w[j, :, at] = shifted.astype(BF16)
        total = jnp.concatenate(totals, axis=1)
        part = dot(vals_t[head, :], w[j]) * (1.0 / total)
        numer[head, :] = part
        stats[0, j : j + 1, :] = jnp.concatenate(tops, axis=1) + jnp.log(total)
        stats[0, 2 + j : 3 + j, :] = jnp.sum(part * grad_t[head, :].astype(F32), axis=0, keepdims=True)
    for k, out in enumerate((n0, n1, n2, n3)):
        start = pl.multiple_of(lax.rem(place[0] + k, 4) * 256, 256)
        out[...] = numer[:, pl.ds(start, 256)]


def forward(place, tokens, kw, vw, q, g):
    cols = lambda rows: pl.BlockSpec((rows, PAIR), lambda i: (0, i))
    return pl.pallas_call(
        forward_kernel,
        grid=(PAIRS,),
        in_specs=[SMEM, full((T, D)), cols(D), cols(D), cols(L), cols(L)],
        out_specs=[cols(T), cols(T), full((T, D))]
        + [pl.BlockSpec((PAIR, 256), lambda i: (i, 0))] * 4
        + [pl.BlockSpec((1, 4, L), lambda i: (i, 0, 0))],
        out_shape=[jax.ShapeDtypeStruct((T, D), BF16)] * 3
        + [jax.ShapeDtypeStruct((D, 256), F32)] * 4
        + [jax.ShapeDtypeStruct((PAIRS, 4, L), F32)],
        scratch_shapes=[
            pltpu.VMEM((T, D), BF16),
            pltpu.VMEM((2, T, L), F32),
            pltpu.VMEM((2, T, L), BF16),
            pltpu.VMEM((PAIR, L), F32),
        ],
        compiler_params=params(),
        cost_estimate=cost(1.2e10, 2.4e7),
        name="forward",
    )(place, tokens, kw, vw, q, g)


def merge_kernel(s0, s1, s2, s3, out):
    blocks = (s0, s1, s2, s3)
    top = functools.reduce(jnp.maximum, [b[:, 0:2, :] for b in blocks])
    total = jnp.zeros_like(top)
    inner = jnp.zeros_like(top)
    for b in blocks:
        factor = jnp.exp(b[:, 0:2, :] - top)
        total += factor
        inner += b[:, 2:4, :] * factor
    out[:, 0:2, :] = top + jnp.log(total)
    out[:, 2:4, :] = inner / total


def simple(kernel, ins, outs, name, scalars=None, scratch=(), moved=4e6, flops=1e6):
    specs = [pl.BlockSpec(memory_space=pltpu.VMEM)] * len(ins)
    several = isinstance(outs, list)
    shapes = [jax.ShapeDtypeStruct(o, F32) for o in (outs if several else [outs])]
    return pl.pallas_call(
        kernel,
        in_specs=([] if scalars is None else [SMEM]) + specs,
        out_shape=shapes if several else shapes[0],
        scratch_shapes=list(scratch),
        compiler_params=params(),
        cost_estimate=cost(flops, moved),
        name=name,
    )(*([] if scalars is None else [scalars]), *ins)


def reorder_kernel(order, normed, out):
    feature = lax.broadcasted_iota(jnp.int32, (D, D), 0)
    choose = jnp.where(feature == order[...], 1.0, 0.0).astype(BF16)
    out[...] = dot(normed[...], choose).astype(BF16).T


def reorder(order, normed):
    return pl.pallas_call(
        reorder_kernel,
        out_shape=jax.ShapeDtypeStruct((D, T), BF16),
        compiler_params=params(),
        cost_estimate=cost(2 * T * D * D, 3e6),
        name="reorder",
    )(order, normed)


def row_order(place):
    digits = [jnp.asarray(d, jnp.int32) for d in np.indices((2, 4, 4, 4, 10)).reshape(5, D)]
    core = (place[3] + digits[0]) % 2
    x = (place[0] + digits[2]) % 4
    z = (place[1] + digits[3]) % 4
    owner = ((x * 4 + z) * 4 + digits[1]) * 2 + core
    return (owner * 10 + digits[4]).reshape(1, D)


def pair_cols(rows):
    return pl.BlockSpec((rows, PAIR), lambda i: (0, i))


def value_kernel(nt, keys, q, g, fin, mine, theirs, s, p):
    grads = []
    for j in range(2):
        head = slice(j * HD, (j + 1) * HD)
        s[j] = nt_dot(keys[:, head], q[:, head])
        for tile in range(L // 128):
            at = slice(tile * 128, (tile + 1) * 128)
            p[j, :, at] = jnp.exp(s[j, :, at] * SCALE - fin[0, j : j + 1, at]).astype(BF16)
        grads.append(dot(p[j], g[:, head]).astype(BF16))
    rows = dot(nt[...], jnp.concatenate(grads, axis=1))
    mine[...] = rows[0:640]
    theirs[...] = rows[640:1280]


def key_kernel(place, nt, keys, vals, q, g, fin, mine, theirs, q_mine, q_theirs, s, pg, sg, query):
    grads = []
    keys_t = keys[...].T
    for j in range(2):
        head = slice(j * HD, (j + 1) * HD)
        s[j] = nt_dot(keys[:, head], q[:, head])
        pg[j] = nt_dot(vals[:, head], g[:, head])
        for tile in range(L // 128):
            at = slice(tile * 128, (tile + 1) * 128)
            probs = jnp.exp(s[j, :, at] * SCALE - fin[0, j : j + 1, at])
            sg[j, :, at] = (probs * (pg[j, :, at] - fin[0, 2 + j : 3 + j, at]) * SCALE).astype(BF16)
        query[:, head] = dot(keys_t[head, :], sg[j]).T
        grads.append(dot(sg[j], q[:, head]).astype(BF16))
    rows = dot(nt[...], jnp.concatenate(grads, axis=1))
    mine[...] = rows[0:640]
    theirs[...] = rows[640:1280]
    start = pl.multiple_of(place[3] * 512, 512)
    q_mine[...] = query[pl.ds(start, 512), :]
    q_theirs[...] = query[pl.ds(512 - start, 512), :]


def backward_specs():
    return [full((D, T)), pair_cols(T)], [pair_cols(L), pair_cols(L), pl.BlockSpec((1, 4, L), lambda i: (i, 0, 0))]


def value_grad(nt, keys, q, g, fin):
    first, rest = backward_specs()
    return pl.pallas_call(
        value_kernel,
        grid=(PAIRS,),
        in_specs=first + rest,
        out_specs=[pair_cols(640)] * 2,
        out_shape=[jax.ShapeDtypeStruct((640, D), F32)] * 2,
        scratch_shapes=[pltpu.VMEM((2, T, L), F32), pltpu.VMEM((2, T, L), BF16)],
        compiler_params=params(),
        cost_estimate=cost(8e9, 1.6e7),
        name="value_grad",
    )(nt, keys, q, g, fin)


def key_grad(place, nt, keys, vals, q, g, fin):
    first, rest = backward_specs()
    return pl.pallas_call(
        key_kernel,
        grid=(PAIRS,),
        in_specs=[SMEM] + first + [pair_cols(T)] + rest,
        out_specs=[pair_cols(640)] * 2 + [pair_cols(512)] * 2,
        out_shape=[jax.ShapeDtypeStruct((640, D), F32)] * 2 + [jax.ShapeDtypeStruct((512, D), F32)] * 2,
        scratch_shapes=[
            pltpu.VMEM((2, T, L), F32),
            pltpu.VMEM((2, T, L), F32),
            pltpu.VMEM((2, T, L), BF16),
            pltpu.VMEM((L, PAIR), F32),
        ],
        compiler_params=params(),
        cost_estimate=cost(1.6e10, 2.4e7),
        name="key_grad",
    )(place, nt, keys, vals, q, g, fin)


def four(a0, a1, a2, a3):
    return (a0[...] + a2[...]) + (a1[...] + a3[...])


def exchange(chunks, axis):
    far = {k: shift(chunks[k], axis, k) for k in (2, 1, 3)}
    return [chunks[0], far[1], far[2], far[3]]


def pair_kernel(place, mine, other, *outs):
    for k, out in enumerate(outs):
        start = pl.multiple_of(lax.rem(place[2] + k, 4) * 160, 160)
        out[...] = mine[pl.ds(start, 160), :] + other[pl.ds(start, 160), :]


def pair_chunks(place, mine, other):
    return pl.pallas_call(
        pair_kernel,
        grid=(PAIRS,),
        in_specs=[SMEM, pair_cols(640), pair_cols(640)],
        out_specs=[pair_cols(160)] * 4,
        out_shape=[jax.ShapeDtypeStruct((160, D), F32)] * 4,
        compiler_params=params(),
        cost_estimate=cost(1e6, 1e7),
        name="pair",
    )(place, mine, other)


def rows_x_kernel(value, a0, a1, a2, a3, *outs):
    rows = four(a0, a1, a2, a3)
    for k, out in enumerate(outs):
        out[0:40, :] = rows[k * 40 : (k + 1) * 40]
        out[40:80, :] = value[k * 40 : (k + 1) * 40, :]


def rows_z_kernel(a0, a1, a2, a3, *outs):
    rows = four(a0, a1, a2, a3)
    for k, out in enumerate(outs):
        out[0:10, :] = rows[k * 10 : (k + 1) * 10]
        out[10:20, :] = rows[40 + k * 10 : 40 + (k + 1) * 10]
        out[20:24, :] = jnp.zeros((4, D), F32)


def rows_last_kernel(a0, a1, a2, a3, key_rows, value_rows):
    rows = four(a0, a1, a2, a3)
    key_rows[...] = rows[0:10]
    value_rows[...] = rows[10:20]


def query_x_kernel(place, parts, *outs):
    rows = (parts[0] + parts[1]) + (parts[2] + parts[3])
    total = outs[-1]
    total[...] = rows
    for k, out in enumerate(outs[:-1]):
        start = pl.multiple_of(lax.rem(place[0] + k, 4) * 32, 32)
        out[...] = total[pl.ds(start, 32), :]


def query_sum_kernel(a0, a1, a2, a3, out):
    out[...] = four(a0, a1, a2, a3)


def query_halves_kernel(a0, a1, a2, a3, left, right):
    rows = four(a0, a1, a2, a3)
    left[...] = rows[:, 0:640]
    right[...] = rows[:, 640:1280]


def place_query_kernel(place, own, other, out):
    for half, block in ((place[3], own), (1 - place[3], other)):
        for i in range(4):
            for k in range(4):
                first = lax.rem(place[1] + 4 - i, 4) * 128 + lax.rem(place[0] + 4 - k, 4) * 32
                out[pl.ds(pl.multiple_of(half * 512 + first, 32), 32), 0:640] = block[i, k, :, 0:640]
                first = lax.rem(place[1] + 4 - k, 4) * 128 + lax.rem(place[0] + 4 - i, 4) * 32
                out[pl.ds(pl.multiple_of(half * 512 + first, 32), 32), 640:1280] = block[i, k, :, 640:1280]


def numer_x_kernel(place, n0, n1, n2, n3, s0, s1, s2, s3, fin, z0, z1, z2, z3, total):
    at = pl.ds(pl.multiple_of(place[0] * 256, 256), 256)
    for h in range(H):
        rows = slice(h * HD, (h + 1) * HD)
        pair, j = h // 2, h % 2
        acc = jnp.zeros((HD, 256), F32)
        for n, s in ((n0, s0), (n1, s1), (n2, s2), (n3, s3)):
            acc += n[rows, :] * jnp.exp(s[pair, j : j + 1, at] - fin[pair, j : j + 1, at])
        total[rows, :] = acc
    for k, out in enumerate((z0, z1, z2, z3)):
        spot = lax.rem(place[1] + k, 4)
        row = pl.multiple_of(lax.rem(spot, 2) * 640, 640)
        lane = pl.multiple_of(lax.div(spot, 2) * 128, 128)
        out[...] = total[pl.ds(row, 640), pl.ds(lane, 128)]


def numer_z_kernel(z0, z1, z2, z3, out):
    out[...] = four(z0, z1, z2, z3).T


def round_kernel(x, out):
    for k in range(2):
        rows = slice(k * 128, (k + 1) * 128)
        out[rows, 0:640] = x[2 * k].astype(BF16)
        out[rows, 640:1280] = x[2 * k + 1].astype(BF16)


def on_device(tokens, queries, key_weight, value_weight, out_grad):
    seq, dp = lax.axis_index("seq"), lax.axis_index("dp")
    place = jnp.stack([seq // 4, seq % 4, dp // 2, dp % 2]).astype(jnp.int32)
    grad = out_grad[0]

    keys, vals, normed, n0, n1, n2, n3, stats = forward(place, tokens[0], key_weight, value_weight, queries, grad)
    near = exchange([stats] * 4, "x")
    nt = reorder(row_order(place), normed)
    near, nt, n1, n2, n3 = lax.optimization_barrier((near, nt, n1, n2, n3))
    group = simple(merge_kernel, near, (PAIRS, 4, L), "merge")
    blocks = exchange([group] * 4, "z")
    numer = exchange([n0, n1, n2, n3], "x")
    fin = simple(merge_kernel, blocks, (PAIRS, 4, L), "finish")

    v_mine, v_theirs = value_grad(nt, keys, queries, grad, fin)
    v_other = shift(v_theirs, "c", 1)
    k_mine, k_theirs, q_mine, q_theirs = key_grad(place, nt, keys, vals, queries, grad, fin)
    q_other = shift(q_theirs, "c", 1)
    k_other = shift(k_theirs, "c", 1)

    v_rows = lax.psum_scatter(
        (v_mine + v_other).reshape(4, 160, D), "dp", scatter_dimension=0, axis_index_groups=Y_GROUPS, tiled=False
    )
    k_chunks = exchange(pair_chunks(place, k_mine, k_other), "y")

    q_parts = lax.all_to_all(
        (q_mine + q_other).reshape(4, 128, D), "seq", split_axis=0, concat_axis=0, axis_index_groups=Z_GROUPS
    )
    q_parts = simple(
        query_x_kernel, [q_parts], [(32, D)] * 4, "query_x", scalars=place, scratch=[pltpu.VMEM((128, D), F32)]
    )
    q_part = simple(query_sum_kernel, exchange(q_parts, "x"), (32, D), "query_sum")
    left, right = simple(query_halves_kernel, exchange([q_part] * 4, "y"), [(32, 640)] * 2, "query_halves")
    left = jnp.stack(exchange([left] * 4, "x"))
    right = jnp.stack(exchange([right] * 4, "z"))
    left = jnp.stack(exchange([left] * 4, "z"))
    right = jnp.stack(exchange([right] * 4, "x"))
    own_query = jnp.concatenate([left, right], axis=3)

    zs = simple(
        numer_x_kernel,
        [*numer, *near, fin],
        [(640, 128)] * 4,
        "numer_x",
        scalars=place,
        scratch=[pltpu.VMEM((D, 256), F32)],
        moved=7e6,
    )
    share = simple(numer_z_kernel, exchange(zs, "z"), (128, 640), "numer_z")
    gathered = lax.all_gather(share, "seq")
    attended = pl.pallas_call(
        round_kernel,
        grid=(4,),
        in_specs=[pl.BlockSpec((4, 128, 640), lambda i: (i, 0, 0))],
        out_specs=pl.BlockSpec((256, D), lambda i: (i, 0)),
        out_shape=jax.ShapeDtypeStruct((L, D), BF16),
        compiler_params=params(),
        cost_estimate=cost(1e6, 8e6),
        name="round",
    )(gathered)

    rows = simple(rows_x_kernel, [v_rows, *k_chunks], [(80, D)] * 4, "rows_x")
    rows = simple(rows_z_kernel, exchange(rows, "x"), [(24, D)] * 4, "rows_z")
    key_rows, value_rows = simple(rows_last_kernel, exchange(rows, "z"), [(10, D)] * 2, "rows_last")

    own_query, attended, key_rows, value_rows = lax.optimization_barrier((own_query, attended, key_rows, value_rows))
    other_query = shift(own_query, "c", 1)
    query_grad = simple(place_query_kernel, [own_query, other_query], (L, D), "place_query", scalars=place, moved=1e7)
    return attended.reshape(1, L, D), query_grad, key_rows, value_rows


def solution(mesh):
    placed = (P("dp", "seq", None), P(), P(), P(), P("dp", None, None))
    return jax.shard_map(
        on_device,
        mesh=mesh,
        in_specs=placed,
        out_specs=(P("dp", None, None), P(), P(("seq", "dp"), None), P(("seq", "dp"), None)),
        check_vma=False,
    )
```

time: 354 us -> 369 us (1.042)
  starting transfers between devices: 53.2 us -> 68.4 us
  Pallas kernels: 114 us -> 100 us
  waiting for transfers between devices: 153 us -> 166 us
  local copies, waits for them, and re-layouts: 14 us -> 9.46 us
  other arithmetic: 4.63 us -> 8.64 us
    ppermute x15, waiting for transfers between devices: 74.5 us -> 34.2 us  [shift(): lax.ppermute(array, 'seq', [(a * 4 + b, a * 4 + (b + step) % 4) for a in...]
    all_to_all x0 -> x1, waiting for transfers between devices: none -> 38 us  [on_device(): lax.all_to_all((q_mine + q_other).reshape(4, 128, D), 'seq', split_axis=0...]
    ppermute x3 -> x4, waiting for transfers between devices: 2.42 us -> 17.7 us  [shift(): lax.ppermute(array, 'dp', [(a * 2 + b, a * 2 + 1 - b) for a in range(4) f...]
    ppermute x3 -> x4, starting transfers between devices: 3.31 us -> 14.5 us  [shift(): lax.ppermute(array, 'dp', [(a * 2 + b, a * 2 + 1 - b) for a in range(4) f...]
    pallas_call x17 -> x16, Pallas kernels: 105 us -> 95.8 us  [the longest x11 28.7 us: simple(): pl.pallas_call(kernel, in_specs=([] if scalars is None else [SMEM]) + spe...]
    add x1 -> x3, other arithmetic: 0.04 us -> 7.67 us  [the longest x1 4.09 us: on_device(): v_mine + v_other]
    ppermute x12 -> x18, waiting for transfers between devices: 58.9 us -> 65.2 us  [shift(): lax.ppermute(array, 'seq', [(a * 4 + b, (a + step) % 4 * 4 + b) for a in...]
    ppermute x9 -> x6, waiting for transfers between devices: 16.8 us -> 10.7 us  [shift(): lax.ppermute(array, 'dp', [(a * 2 + b, (a + step) % 4 * 2 + b) for a in r...]
  transfers between devices with their start and end apart: 40 -> 46, of which waited for: 17 -> 25; matrix products, arithmetic and copies ran while one was open for 1% -> 1% of each run, Pallas kernels for 24% -> 14%
where the time goes in v2:
time: 369 us; the launch traced here: 368 us
  waiting for transfers between devices  166 us (45%)
  Pallas kernels  100 us (27%)
  starting transfers between devices  68.4 us (19%)
  between operations  15.7 us (4%)
  local copies, waits for them, and re-layouts  9.46 us (3%)
  other arithmetic  8.64 us (2%)
    ppermute x18, waiting for transfers between devices, shift(): lax.ppermute(array, 'seq', [(a * 4 + b, (a + step) % 4 * 4 + b) for a in...  65.2 us
    all_to_all x1, waiting for transfers between devices, on_device(): lax.all_to_all((q_mine + q_other).reshape(4, 128, D), 'seq', split_axis=0...  38 us
    ppermute x15, waiting for transfers between devices, shift(): lax.ppermute(array, 'seq', [(a * 4 + b, a * 4 + (b + step) % 4) for a in...  34.2 us
    pallas_call x11, Pallas kernels, simple(): pl.pallas_call(kernel, in_specs=([] if scalars is None else [SMEM]) + spe...  28.7 us
    ppermute x18, starting transfers between devices, shift(): lax.ppermute(array, 'seq', [(a * 4 + b, (a + step) % 4 * 4 + b) for a in...  25 us
    pallas_call x1, Pallas kernels, forward(): pl.pallas_call(forward_kernel, grid=(PAIRS,), in_specs=[SMEM, full((T, D)...  20.9 us
    pallas_call x1, Pallas kernels, key_grad(): pl.pallas_call(key_kernel, grid=(PAIRS,), in_specs=[SMEM] + first + [pair...  20.7 us
    ppermute x4, waiting for transfers between devices, shift(): lax.ppermute(array, 'dp', [(a * 2 + b, a * 2 + 1 - b) for a in range(4) f...  17.7 us
  transfers between devices with their start and end apart: 46, of which 25 were waited for; matrix products, arithmetic and copies ran while one was open for 1% of the time, Pallas kernels for 14%

profile of v2, /device:TPU:1, one launch (start us, length us, event | category | flops | bytes accessed | tf_op | source)
XLA Modules:
  0.0 368.2 jit_solution(11826711564621335273)
XLA Ops:
  8.8 20.9 %forward.1 = (bf16[512,1280]{1,0:T(8,128)(2,1)}, bf16[512,1280]{1,0:T(8,128)(2,1)}, bf16[512,1280]{1,0:T(8,128)(2,1)}, f32[1280,256]{1,0:T(8,128)}, f32[1280,256...) custom-call(s32[4]{0:T(128)} %pad_add_fusion.place, bf16[512,1280]{1,0:T(8,128)(2,1)} %bitcast.51, ...), custom_call_target="tpu_custom_call" | custom-call | flops 12000000000 | bytes 24000000 | tf_op jit(solution)/shard_map/forward/pallas_call | solution.py:98
  29.7 3.4 collective-permute-start.2
  34.9 4.4 %reorder.1.nt = bf16[1280,512]{1,0:T(8,128)(2,1)} custom-call(s32[1,1280]{1,0:T(1,128)} %reshape.20.order, bf16[512,1280]{1,0:T(8,128)(2,1)} %get-tuple-element.55.normed), custom_call_target="tpu_custom_call" | custom-call | flops 1677721600 | bytes 3000000 | tf_op jit(solution)/shard_map/reorder/pallas_call | solution.py:155
  41.9 3.8 %collective-permute-start.5 = (f32[5,4,1024]{2,1,0:T(4,128)}, f32[5,4,1024]{2,1,0:T(4,128)S(1)}, u32[]{:S(2)}, u32[]{:S(2)}) collective-permute-start(f32[5,4,1024]{2,1,0:T(4,128)} %merge.1.s0), channel_id=1, source_target_pairs={{0,24},{8,0},{16,8},{24,16},{32,56},{40,32},{48,40},{56,48},{64,88... | collective-permute-start | bytes 245768 | tf_op jit(solution)/shard_map/ppermute | solution.py:30
  53.8 14.6 %value_grad.1 = (f32[640,1280]{1,0:T(8,128)}, f32[640,1280]{1,0:T(8,128)}) custom-call(bf16[1280,512]{1,0:T(8,128)(2,1)} %reorder.1.nt, bf16[512,1280]{1,0:T(8,128)(2,1)} %get-tuple-element.60.keys, bf16[1024,1280]{1,0:T(8,128)(2,1)} %q.5, bf16[1024,1280]{1,0:T(8,128)(2,1)} %bitcast.49, f32[5,4,1024]{2,1,0:T(4,128)} %finish.1.fin), custom_call_target="tpu_custom_call" | custom-call | flops 8000000000 | bytes 16000000 | tf_op jit(solution)/shard_map/value_grad/pallas_call | solution.py:218
  68.5 3.3 collective-permute-start.31
  71.8 5.7 %collective-permute-done.31 = f32[640,1280]{1,0:T(8,128)S(1)} collective-permute-done((f32[640,1280]{1,0:T(8,128)}, f32[640,1280]{1,0:T(8,128)S(1)}, u32[]{:S(2)}, u32[]{:S(2)}) %collective-permute-start.31) | collective-permute-done | bytes 3276832 | tf_op jit(solution)/shard_map/ppermute | solution.py:33
  77.4 4.1 %add.77 = f32[640,1280]{1,0:T(8,128)} add(f32[640,1280]{1,0:T(8,128)} %get-tuple-element.82, f32[640,1280]{1,0:T(8,128)S(1)} %collective-permute-done.31) | non-fusion elementwise | flops 819200 | bytes 9830400 | tf_op jit(solution)/shard_map/add | solution.py:377
  86.2 27.0 %collective-permute-done.25.n1 = f32[1280,256]{1,0:T(8,128)S(1)} collective-permute-done((f32[1280,256]{1,0:T(8,128)}, f32[1280,256]{1,0:T(8,128)S(1)}, u32[]{:S(2)}, u32[]{:S(2)}) %collective-permute-start.25) | collective-permute-done | bytes 1310752 | tf_op jit(solution)/shard_map/ppermute | solution.py:28
  113.2 27.9 %collective-permute-done.26.n2 = f32[1280,256]{1,0:T(8,128)S(1)} collective-permute-done((f32[1280,256]{1,0:T(8,128)S(1)}, f32[1280,256]{1,0:T(8,128)S(1)}, u32[]{:S(2)}, u32[]{:S(2)}) %collective-permute-start.26) | collective-permute-done | bytes 1310752 | tf_op jit(solution)/shard_map/ppermute | solution.py:28
  142.7 4.1 %numer_x.1 = (f32[640,128]{1,0:T(8,128)}, f32[640,128]{1,0:T(8,128)}, f32[640,128]{1,0:T(8,128)}, f32[640,128]{1,0:T(8,128)}) custom-call(s32[4]{0:T(128)} %pad_add_fusion.place, f32[1280,256]{1,0:T(8,128)} %get-tuple-element.74.n0, f32[1280,256]{1,0:T(8,128)} %copy-done.3, f32[1280,256]{1,0:T(8,128)} %copy-done.4, f32[1280,256]{1,0:T(8,128)} %copy-done.5, ...), custom_call_target="tpu_custom_call" | custom-call | flops 1000000 | bytes 7000000 | tf_op jit(solution)/shard_map/numer_x/pallas_call | solution.py:137
  149.9 7.4 %collective-permute-done.28.z1 = f32[640,128]{1,0:T(8,128)S(1)} collective-permute-done((f32[640,128]{1,0:T(8,128)}, f32[640,128]{1,0:T(8,128)S(1)}, u32[]{:S(2)}, u32[]{:S(2)}) %collective-permute-start.28) | collective-permute-done | bytes 327712 | tf_op jit(solution)/shard_map/ppermute | solution.py:30
  157.2 5.0 %collective-permute-done.29.z2 = f32[640,128]{1,0:T(8,128)S(1)} collective-permute-done((f32[640,128]{1,0:T(8,128)}, f32[640,128]{1,0:T(8,128)S(1)}, u32[]{:S(2)}, u32[]{:S(2)}) %collective-permute-start.29) | collective-permute-done | bytes 327712 | tf_op jit(solution)/shard_map/ppermute | solution.py:30
  167.4 20.7 %key_grad.1 = (f32[640,1280]{1,0:T(8,128)}, f32[640,1280]{1,0:T(8,128)}, f32[512,1280]{1,0:T(8,128)}, f32[512,1280]{1,0:T(8,128)}) custom-call(s32[4]{0:T(128)} %pad_add_fusion.place, bf16[1280,512]{1,0:T(8,128)(2,1)} %reorder.1.nt, bf16[512,1280]{1,0:T(8,128)(2,1)} %get-tuple-element.60.keys, bf16[512,1280]{1,0:T(8,128)(2,1)} %get-tuple-element.61.vals, ...), custom_call_target="tpu_custom_call" | custom-call | flops 16000000000 | bytes 24000000 | tf_op jit(solution)/shard_map/key_grad/pallas_call | solution.py:233
  189.8 7.5 %collective-permute-done.6 = f32[512,1280]{1,0:T(8,128)S(1)} collective-permute-done((f32[512,1280]{1,0:T(8,128)}, f32[512,1280]{1,0:T(8,128)S(1)}, u32[]{:S(2)}, u32[]{:S(2)}) %collective-permute-start.6) | collective-permute-done | bytes 2621472 | tf_op jit(solution)/shard_map/ppermute | solution.py:33
  197.3 3.6 add.76
  200.8 3.7 all-to-all-start
  204.5 6.2 %pair.1 = (f32[160,1280]{1,0:T(8,128)}, f32[160,1280]{1,0:T(8,128)}, f32[160,1280]{1,0:T(8,128)}, f32[160,1280]{1,0:T(8,128)}) custom-call(s32[4]{0:T(128)} %pad_add_fusion.place, f32[640,1280]{1,0:T(8,128)} %get-tuple-element.84.mine, f32[640,1280]{1,0:T(8,128)} %collective-permute-done.32.other), custom_call_target="tpu_custom_call" | custom-call | flops 1000000 | bytes 10000000 | tf_op jit(solution)/shard_map/pair/pallas_call | solution.py:267
  215.7 38.0 %all-to-all-done.parts = f32[4,128,1280]{2,1,0:T(8,128)S(1)} async-done(((f32[4,128,1280]{2,1,0:T(8,128)}), f32[4,128,1280]{2,1,0:T(8,128)S(1)}, u32[]{:S(2)}, u32[]{:S(2)}) %all-to-all-start) | async-done | bytes 2621472 | tf_op jit(solution)/shard_map/all_to_all | solution.py:381
  261.6 2.8 collective-permute-done.7.a1
  265.6 3.2 collective-permute-done.8.a2
  274.5 3.8 %collective-permute-done.12.a3 = f32[32,1280]{1,0:T(8,128)S(1)} collective-permute-done((f32[32,1280]{1,0:T(8,128)}, f32[32,1280]{1,0:T(8,128)S(1)}, u32[]{:S(2)}, u32[]{:S(2)}) %collective-permute-start.12) | collective-permute-done | bytes 163872 | tf_op jit(solution)/shard_map/ppermute | solution.py:32
  279.9 5.3 %collective-permute-done.10.a1 = f32[32,1280]{1,0:T(8,128)S(1)} collective-permute-done((f32[32,1280]{1,0:T(8,128)}, f32[32,1280]{1,0:T(8,128)S(1)}, u32[]{:S(2)}, u32[]{:S(2)}) %collective-permute-start.10) | collective-permute-done | bytes 163872 | tf_op jit(solution)/shard_map/ppermute | solution.py:32
  287.7 2.9 collective-permute-start.15
  292.1 3.4 rows_x.1
  303.1 5.3 %collective-permute-done.20 = f32[32,640]{1,0:T(8,128)S(1)} collective-permute-done((f32[32,640]{1,0:T(8,128)S(1)}, f32[32,640]{1,0:T(8,128)S(1)}, u32[]{:S(2)}, u32[]{:S(2)}) %collective-permute-start.20) | collective-permute-done | bytes 81952 | tf_op jit(solution)/shard_map/ppermute | solution.py:30
  309.4 7.0 %collective-permute-done.19 = f32[32,640]{1,0:T(8,128)S(1)} collective-permute-done((f32[32,640]{1,0:T(8,128)S(1)}, f32[32,640]{1,0:T(8,128)S(1)}, u32[]{:S(2)}, u32[]{:S(2)}) %collective-permute-start.19) | collective-permute-done | bytes 81952 | tf_op jit(solution)/shard_map/ppermute | solution.py:30
  327.5 2.9 collective-permute-done.22
  335.4 4.6 %round.1 = bf16[1024,1280]{1,0:T(8,128)(2,1)} custom-call(f32[16,128,640]{2,1,0:T(8,128)} %bitcast.31), custom_call_target="tpu_custom_call" | custom-call | flops 1000000 | bytes 8000000 | tf_op jit(solution)/shard_map/round/pallas_call | solution.py:406
  340.0 9.6 %collective-permute-start.42 = (f32[4,4,32,1280]{3,2,1,0:T(8,128)S(1)}, f32[4,4,32,1280]{3,2,1,0:T(8,128)S(1)}, u32[]{:S(2)}, u32[]{:S(2)}) collective-permute-start(f32[4,4,32,1280]{3,2,1,0:T(8,128)S(1)} %maximum_maximum_fusion.own), channel_id=1, source_target_pairs={{0,1},{1,0},{2,3},{3,2},{4,5},{5,4},{6,7},{7,6},{8,9},{9,8},{10,11... | collective-permute-start | bytes 7864328 | tf_op jit(solution)/shard_map/ppermute | solution.py:33
  349.5 4.5 %collective-permute-done.42.other = f32[4,4,32,1280]{3,2,1,0:T(8,128)S(1)} collective-permute-done((f32[4,4,32,1280]{3,2,1,0:T(8,128)S(1)}, f32[4,4,32,1280]{3,2,1,0:T(8,128)S(1)}, u32[]{:S(2)}, u32[]{:S(2)}) %collective-permute-start.42) | collective-permute-done | bytes 2621472 | tf_op jit(solution)/shard_map/ppermute | solution.py:33
  355.5 5.3 %place_query.1 = f32[1024,1280]{1,0:T(8,128)} custom-call(s32[4]{0:T(128)} %pad_add_fusion.place, f32[4,4,32,1280]{3,2,1,0:T(8,128)} %copy-done.1, f32[4,4,32,1280]{3,2,1,0:T(8,128)} %copy-done.2), custom_call_target="tpu_custom_call" | custom-call | flops 1000000 | bytes 10000000 | tf_op jit(solution)/shard_map/place_query/pallas_call | solution.py:137
  (161 shorter events, 80.7 us)
Async XLA Ops:
  8.0 284.1 %reduce-scatter.2.cloned.1.call-start = ((), (), s32[]{:S(2)}) async-start(), calls=%async_computation.2 | async-start | bytes 4096000 | tf_op jit(solution)/shard_map/reduce_scatter | solution.py:376
  29.7 9.5 %collective-permute-start.2 = (f32[5,4,1024]{2,1,0:T(4,128)}, f32[5,4,1024]{2,1,0:T(4,128)S(1)}, u32[]{:S(2)}, u32[]{:S(2)}) collective-permute-start(f32[5,4,1024]{2,1,0:T(4,128)} %get-tuple-element.62.s0), channel_id=1, source_target_pairs={{0,96},{8,104},{16,112},{24,120},{32,0},{40,8},{48,16},{56,24},{64... | collective-permute-start | bytes 245768 | tf_op jit(solution)/shard_map/ppermute | solution.py:28
  68.5 9.0 %collective-permute-start.31 = (f32[640,1280]{1,0:T(8,128)}, f32[640,1280]{1,0:T(8,128)S(1)}, u32[]{:S(2)}, u32[]{:S(2)}) collective-permute-start(f32[640,1280]{1,0:T(8,128)} %get-tuple-element.83), channel_id=1, source_target_pairs={{0,1},{1,0},{2,3},{3,2},{4,5},{5,4},{6,7},{7,6},{8,9},{9,8},{10,11... | collective-permute-start | bytes 9830408 | tf_op jit(solution)/shard_map/ppermute | solution.py:33
  81.6 253.9 %all-gather.3.cloned.1.call-start = ((), (), s32[]{:S(2)}) async-start(), calls=%async_computation.3 | async-start | bytes 5570560 | tf_op jit(solution)/shard_map/all_gather | solution.py:405
  81.6 31.6 %collective-permute-start.25 = (f32[1280,256]{1,0:T(8,128)}, f32[1280,256]{1,0:T(8,128)S(1)}, u32[]{:S(2)}, u32[]{:S(2)}) collective-permute-start(f32[1280,256]{1,0:T(8,128)} %get-tuple-element.75), channel_id=1, source_target_pairs={{0,32},{8,40},{16,48},{24,56},{32,64},{40,72},{48,80},{56,88},{64,... | collective-permute-start | bytes 3932168 | tf_op jit(solution)/shard_map/ppermute | solution.py:28
  82.8 58.3 %collective-permute-start.26 = (f32[1280,256]{1,0:T(8,128)S(1)}, f32[1280,256]{1,0:T(8,128)S(1)}, u32[]{:S(2)}, u32[]{:S(2)}) collective-permute-start(f32[1280,256]{1,0:T(8,128)S(1)} %copy-done.36), channel_id=1, source_target_pairs={{0,64},{8,72},{16,80},{24,88},{32,96},{40,104},{48,112},{56,120},{... | collective-permute-start | bytes 3932168 | tf_op jit(solution)/shard_map/ppermute | solution.py:28
  84.3 56.9 %collective-permute-start.27 = (f32[1280,256]{1,0:T(8,128)S(1)}, f32[1280,256]{1,0:T(8,128)S(1)}, u32[]{:S(2)}, u32[]{:S(2)}) collective-permute-start(f32[1280,256]{1,0:T(8,128)S(1)} %copy-done.35), channel_id=1, source_target_pairs={{0,96},{8,104},{16,112},{24,120},{32,0},{40,8},{48,16},{56,24},{64... | collective-permute-start | bytes 3932168 | tf_op jit(solution)/shard_map/ppermute | solution.py:28
  146.8 10.4 %collective-permute-start.28 = (f32[640,128]{1,0:T(8,128)}, f32[640,128]{1,0:T(8,128)S(1)}, u32[]{:S(2)}, u32[]{:S(2)}) collective-permute-start(f32[640,128]{1,0:T(8,128)} %get-tuple-element.79), channel_id=1, source_target_pairs={{0,8},{8,16},{16,24},{24,0},{32,40},{40,48},{48,56},{56,32},{64,72... | collective-permute-start | bytes 983048 | tf_op jit(solution)/shard_map/ppermute | solution.py:30
  146.8 15.4 %collective-permute-start.29 = (f32[640,128]{1,0:T(8,128)}, f32[640,128]{1,0:T(8,128)S(1)}, u32[]{:S(2)}, u32[]{:S(2)}) collective-permute-start(f32[640,128]{1,0:T(8,128)} %get-tuple-element.80), channel_id=1, source_target_pairs={{0,16},{8,24},{16,0},{24,8},{32,48},{40,56},{48,32},{56,40},{64,80... | collective-permute-start | bytes 983048 | tf_op jit(solution)/shard_map/ppermute | solution.py:30
  148.4 16.1 %collective-permute-start.30 = (f32[640,128]{1,0:T(8,128)}, f32[640,128]{1,0:T(8,128)S(1)}, u32[]{:S(2)}, u32[]{:S(2)}) collective-permute-start(f32[640,128]{1,0:T(8,128)} %get-tuple-element.81), channel_id=1, source_target_pairs={{0,24},{8,0},{16,8},{24,16},{32,56},{40,32},{48,40},{56,48},{64,88... | collective-permute-start | bytes 983048 | tf_op jit(solution)/shard_map/ppermute | solution.py:30
  188.2 9.1 %collective-permute-start.6 = (f32[512,1280]{1,0:T(8,128)}, f32[512,1280]{1,0:T(8,128)S(1)}, u32[]{:S(2)}, u32[]{:S(2)}) collective-permute-start(f32[512,1280]{1,0:T(8,128)} %get-tuple-element.67), channel_id=1, source_target_pairs={{0,1},{1,0},{2,3},{3,2},{4,5},{5,4},{6,7},{7,6},{8,9},{9,8},{10,11... | collective-permute-start | bytes 7864328 | tf_op jit(solution)/shard_map/ppermute | solution.py:33
  189.7 14.8 %collective-permute-start.32 = (f32[640,1280]{1,0:T(8,128)}, f32[640,1280]{1,0:T(8,128)}, u32[]{:S(2)}, u32[]{:S(2)}) collective-permute-start(f32[640,1280]{1,0:T(8,128)} %get-tuple-element.85), channel_id=1, source_target_pairs={{0,1},{1,0},{2,3},{3,2},{4,5},{5,4},{6,7},{7,6},{8,9},{9,8},{10,11... | collective-permute-start | bytes 9830408 | tf_op jit(solution)/shard_map/ppermute | solution.py:33
  200.8 52.9 %all-to-all-start = ((f32[4,128,1280]{2,1,0:T(8,128)}), f32[4,128,1280]{2,1,0:T(8,128)S(1)}, u32[]{:S(2)}, u32[]{:S(2)}) async-start(f32[4,128,1280]{2,1,0:T(8,128)} %bitcast.30), calls=%async_computation | async-start | bytes 5242880 | tf_op jit(solution)/shard_map/all_to_all | solution.py:381
  210.7 79.9 %collective-permute-start.33 = (f32[160,1280]{1,0:T(8,128)}, f32[160,1280]{1,0:T(8,128)S(1)}, u32[]{:S(2)}, u32[]{:S(2)}) collective-permute-start(f32[160,1280]{1,0:T(8,128)} %get-tuple-element.87), channel_id=1, source_target_pairs={{0,2},{1,3},{2,4},{3,5},{4,6},{5,7},{6,0},{7,1},{8,10},{9,11},{10,... | collective-permute-start | bytes 2457608 | tf_op jit(solution)/shard_map/ppermute | solution.py:32
  212.0 79.3 %collective-permute-start.34 = (f32[160,1280]{1,0:T(8,128)}, f32[160,1280]{1,0:T(8,128)}, u32[]{:S(2)}, u32[]{:S(2)}) collective-permute-start(f32[160,1280]{1,0:T(8,128)} %get-tuple-element.88), channel_id=1, source_target_pairs={{0,4},{1,5},{2,6},{3,7},{4,0},{5,1},{6,2},{7,3},{8,12},{9,13},{10,... | collective-permute-start | bytes 2457608 | tf_op jit(solution)/shard_map/ppermute | solution.py:32
  214.7 77.5 %collective-permute-start.35 = (f32[160,1280]{1,0:T(8,128)}, f32[160,1280]{1,0:T(8,128)}, u32[]{:S(2)}, u32[]{:S(2)}) collective-permute-start(f32[160,1280]{1,0:T(8,128)} %get-tuple-element.89), channel_id=1, source_target_pairs={{0,6},{1,7},{2,0},{3,1},{4,2},{5,3},{6,4},{7,5},{8,14},{9,15},{10,... | collective-permute-start | bytes 2457608 | tf_op jit(solution)/shard_map/ppermute | solution.py:32
  259.2 9.6 %collective-permute-start.8 = (f32[32,1280]{1,0:T(8,128)}, f32[32,1280]{1,0:T(8,128)S(1)}, u32[]{:S(2)}, u32[]{:S(2)}) collective-permute-start(f32[32,1280]{1,0:T(8,128)} %get-tuple-element.70), channel_id=1, source_target_pairs={{0,64},{8,72},{16,80},{24,88},{32,96},{40,104},{48,112},{56,120},{... | collective-permute-start | bytes 491528 | tf_op jit(solution)/shard_map/ppermute | solution.py:28
  287.7 9.7 %collective-permute-start.15 = (f32[32,640]{1,0:T(8,128)}, f32[32,640]{1,0:T(8,128)S(1)}, u32[]{:S(2)}, u32[]{:S(2)}) collective-permute-start(f32[32,640]{1,0:T(8,128)} %get-tuple-element.72), channel_id=1, source_target_pairs={{0,96},{8,104},{16,112},{24,120},{32,0},{40,8},{48,16},{56,24},{64... | collective-permute-start | bytes 245768 | tf_op jit(solution)/shard_map/ppermute | solution.py:28
  290.7 8.1 %collective-permute-start.14 = (f32[32,640]{1,0:T(8,128)}, f32[32,640]{1,0:T(8,128)S(1)}, u32[]{:S(2)}, u32[]{:S(2)}) collective-permute-start(f32[32,640]{1,0:T(8,128)} %get-tuple-element.72), channel_id=1, source_target_pairs={{0,64},{8,72},{16,80},{24,88},{32,96},{40,104},{48,112},{56,120},{... | collective-permute-start | bytes 245768 | tf_op jit(solution)/shard_map/ppermute | solution.py:28
  290.7 9.3 %collective-permute-start.13 = (f32[32,640]{1,0:T(8,128)}, f32[32,640]{1,0:T(8,128)S(1)}, u32[]{:S(2)}, u32[]{:S(2)}) collective-permute-start(f32[32,640]{1,0:T(8,128)} %get-tuple-element.72), channel_id=1, source_target_pairs={{0,32},{8,40},{16,48},{24,56},{32,64},{40,72},{48,80},{56,88},{64,... | collective-permute-start | bytes 245768 | tf_op jit(solution)/shard_map/ppermute | solution.py:28
  291.3 10.1 %collective-permute-start.21 = (f32[32,640]{1,0:T(8,128)}, f32[32,640]{1,0:T(8,128)S(1)}, u32[]{:S(2)}, u32[]{:S(2)}) collective-permute-start(f32[32,640]{1,0:T(8,128)} %get-tuple-element.73), channel_id=1, source_target_pairs={{0,24},{8,0},{16,8},{24,16},{32,56},{40,32},{48,40},{56,48},{64,88... | collective-permute-start | bytes 245768 | tf_op jit(solution)/shard_map/ppermute | solution.py:30
  295.5 23.7 %collective-permute-start.36 = (f32[80,1280]{1,0:T(8,128)}, f32[80,1280]{1,0:T(8,128)S(1)}, u32[]{:S(2)}, u32[]{:S(2)}) collective-permute-start(f32[80,1280]{1,0:T(8,128)} %get-tuple-element.91), channel_id=1, source_target_pairs={{0,32},{8,40},{16,48},{24,56},{32,64},{40,72},{48,80},{56,88},{64,... | collective-permute-start | bytes 1228808 | tf_op jit(solution)/shard_map/ppermute | solution.py:28
  297.5 22.4 %collective-permute-start.37 = (f32[80,1280]{1,0:T(8,128)}, f32[80,1280]{1,0:T(8,128)S(1)}, u32[]{:S(2)}, u32[]{:S(2)}) collective-permute-start(f32[80,1280]{1,0:T(8,128)} %get-tuple-element.92), channel_id=1, source_target_pairs={{0,64},{8,72},{16,80},{24,88},{32,96},{40,104},{48,112},{56,120},{... | collective-permute-start | bytes 1228808 | tf_op jit(solution)/shard_map/ppermute | solution.py:28
  298.8 22.4 %collective-permute-start.38 = (f32[80,1280]{1,0:T(8,128)}, f32[80,1280]{1,0:T(8,128)S(1)}, u32[]{:S(2)}, u32[]{:S(2)}) collective-permute-start(f32[80,1280]{1,0:T(8,128)} %get-tuple-element.93), channel_id=1, source_target_pairs={{0,96},{8,104},{16,112},{24,120},{32,0},{40,8},{48,16},{56,24},{64... | collective-permute-start | bytes 1228808 | tf_op jit(solution)/shard_map/ppermute | solution.py:28
  300.0 16.4 %collective-permute-start.17 = (f32[4,32,640]{2,1,0:T(8,128)S(1)}, f32[4,32,640]{2,1,0:T(8,128)S(1)}, u32[]{:S(2)}, u32[]{:S(2)}) collective-permute-start(f32[4,32,640]{2,1,0:T(8,128)S(1)} %get-tuple-element.105), channel_id=1, source_target_pairs={{0,16},{8,24},{16,0},{24,8},{32,48},{40,56},{48,32},{56,40},{64,80... | collective-permute-start | bytes 983048 | tf_op jit(solution)/shard_map/ppermute | solution.py:30
  316.4 8.4 %collective-permute-start.16 = (f32[4,32,640]{2,1,0:T(8,128)S(1)}, f32[4,32,640]{2,1,0:T(8,128)S(1)}, u32[]{:S(2)}, u32[]{:S(2)}) collective-permute-start(f32[4,32,640]{2,1,0:T(8,128)S(1)} %get-tuple-element.105), channel_id=1, source_target_pairs={{0,8},{8,16},{16,24},{24,0},{32,40},{40,48},{48,56},{56,32},{64,72... | collective-permute-start | bytes 983048 | tf_op jit(solution)/shard_map/ppermute | solution.py:30
  316.4 8.3 %collective-permute-start.18 = (f32[4,32,640]{2,1,0:T(8,128)S(1)}, f32[4,32,640]{2,1,0:T(8,128)S(1)}, u32[]{:S(2)}, u32[]{:S(2)}) collective-permute-start(f32[4,32,640]{2,1,0:T(8,128)S(1)} %get-tuple-element.105), channel_id=1, source_target_pairs={{0,24},{8,0},{16,8},{24,16},{32,56},{40,32},{48,40},{56,48},{64,88... | collective-permute-start | bytes 983048 | tf_op jit(solution)/shard_map/ppermute | solution.py:30
  319.9 10.5 %collective-permute-start.22 = (f32[4,32,640]{2,1,0:T(8,128)S(1)}, f32[4,32,640]{2,1,0:T(8,128)S(1)}, u32[]{:S(2)}, u32[]{:S(2)}) collective-permute-start(f32[4,32,640]{2,1,0:T(8,128)S(1)} %get-tuple-element.107), channel_id=1, source_target_pairs={{0,32},{8,40},{16,48},{24,56},{32,64},{40,72},{48,80},{56,88},{64,... | collective-permute-start | bytes 983048 | tf_op jit(solution)/shard_map/ppermute | solution.py:28
  321.1 9.3 %collective-permute-start.24 = (f32[4,32,640]{2,1,0:T(8,128)S(1)}, f32[4,32,640]{2,1,0:T(8,128)S(1)}, u32[]{:S(2)}, u32[]{:S(2)}) collective-permute-start(f32[4,32,640]{2,1,0:T(8,128)S(1)} %get-tuple-element.107), channel_id=1, source_target_pairs={{0,96},{8,104},{16,112},{24,120},{32,0},{40,8},{48,16},{56,24},{64... | collective-permute-start | bytes 983048 | tf_op jit(solution)/shard_map/ppermute | solution.py:28
  324.8 8.1 %collective-permute-start.39 = (f32[24,1280]{1,0:T(8,128)}, f32[24,1280]{1,0:T(8,128)S(1)}, u32[]{:S(2)}, u32[]{:S(2)}) collective-permute-start(f32[24,1280]{1,0:T(8,128)} %get-tuple-element.95), channel_id=1, source_target_pairs={{0,8},{8,16},{16,24},{24,0},{32,40},{40,48},{48,56},{56,32},{64,72... | collective-permute-start | bytes 368648 | tf_op jit(solution)/shard_map/ppermute | solution.py:30
  324.8 8.1 %collective-permute-start.40 = (f32[24,1280]{1,0:T(8,128)}, f32[24,1280]{1,0:T(8,128)S(1)}, u32[]{:S(2)}, u32[]{:S(2)}) collective-permute-start(f32[24,1280]{1,0:T(8,128)} %get-tuple-element.96), channel_id=1, source_target_pairs={{0,16},{8,24},{16,0},{24,8},{32,48},{40,56},{48,32},{56,40},{64,80... | collective-permute-start | bytes 368648 | tf_op jit(solution)/shard_map/ppermute | solution.py:30
  340.0 14.1 %collective-permute-start.42 = (f32[4,4,32,1280]{3,2,1,0:T(8,128)S(1)}, f32[4,4,32,1280]{3,2,1,0:T(8,128)S(1)}, u32[]{:S(2)}, u32[]{:S(2)}) collective-permute-start(f32[4,4,32,1280]{3,2,1,0:T(8,128)S(1)} %maximum_maximum_fusion.own), channel_id=1, source_target_pairs={{0,1},{1,0},{2,3},{3,2},{4,5},{5,4},{6,7},{7,6},{8,9},{9,8},{10,11... | collective-permute-start | bytes 7864328 | tf_op jit(solution)/shard_map/ppermute | solution.py:33
  (51 other events, 335.2 us)
Sparse Core Ops, SparseCore 0:
  81.7 37.4 reduce-scatter.1
Sparse Core Ops, SparseCore 1:
  167.5 74.6 all-gather.2

commit v3 on v2

--- a/solution.py
+++ b/solution.py
@@ -17,8 +17,9 @@
 SCALE = HD ** (-0.5)
 VMEM_LIMIT = 56 * 1024 * 1024
 PAIRS = H // 2
-Z_GROUPS = [[a * 4 + b for b in range(4)] for a in range(4)]
-Y_GROUPS = [[a * 2 + b for a in range(4)] for b in range(2)]
+COST = 1.0
+PAIR_GROUPS = [[a * 2, a * 2 + 1] for a in range(4)]
+CORE_GROUPS = [[a * 2 + b for a in range(64)] for b in range(2)]
 F32 = jnp.float32
 BF16 = jnp.bfloat16
 
@@ -46,7 +47,7 @@
 
 
 def cost(flops, moved):
-    return pl.CostEstimate(flops=int(flops), bytes_accessed=int(moved), transcendentals=0)
+    return pl.CostEstimate(flops=int(flops * COST), bytes_accessed=int(moved * COST), transcendentals=0)
 
 
 def full(shape):
@@ -162,11 +163,10 @@
 
 
 def row_order(place):
-    digits = [jnp.asarray(d, jnp.int32) for d in np.indices((2, 4, 4, 4, 10)).reshape(5, D)]
-    core = (place[3] + digits[0]) % 2
-    x = (place[0] + digits[2]) % 4
-    z = (place[1] + digits[3]) % 4
-    owner = ((x * 4 + z) * 4 + digits[1]) * 2 + core
+    digits = [jnp.asarray(d, jnp.int32) for d in np.indices((4, 2, 4, 4, 10)).reshape(5, D)]
+    z = (place[1] + digits[2]) % 4
+    x = (place[0] + digits[3]) % 4
+    owner = ((x * 4 + z) * 4 + digits[0]) * 2 + digits[1]
     return (owner * 10 + digits[4]).reshape(1, D)
 
 
@@ -174,22 +174,7 @@
     return pl.BlockSpec((rows, PAIR), lambda i: (0, i))
 
 
-def value_kernel(nt, keys, q, g, fin, mine, theirs, s, p):
-    grads = []
-    for j in range(2):
-        head = slice(j * HD, (j + 1) * HD)
-        s[j] = nt_dot(keys[:, head], q[:, head])
-        for tile in range(L // 128):
-            at = slice(tile * 128, (tile + 1) * 128)
-            p[j, :, at] = jnp.exp(s[j, :, at] * SCALE - fin[0, j : j + 1, at]).astype(BF16)
-        grads.append(dot(p[j], g[:, head]).astype(BF16))
-    rows = dot(nt[...], jnp.concatenate(grads, axis=1))
-    mine[...] = rows[0:640]
-    theirs[...] = rows[640:1280]
-
-
-def key_kernel(place, nt, keys, vals, q, g, fin, mine, theirs, q_mine, q_theirs, s, pg, sg, query):
-    grads = []
+def backward_kernel(nt, keys, vals, q, g, fin, out, q_out, s, pg, p, sg, kgrad, vgrad):
     keys_t = keys[...].T
     for j in range(2):
         head = slice(j * HD, (j + 1) * HD)
@@ -198,54 +183,48 @@
         for tile in range(L // 128):
             at = slice(tile * 128, (tile + 1) * 128)
             probs = jnp.exp(s[j, :, at] * SCALE - fin[0, j : j + 1, at])
+            p[j, :, at] = probs.astype(BF16)
             sg[j, :, at] = (probs * (pg[j, :, at] - fin[0, 2 + j : 3 + j, at]) * SCALE).astype(BF16)
-        query[:, head] = dot(keys_t[head, :], sg[j]).T
-        grads.append(dot(sg[j], q[:, head]).astype(BF16))
-    rows = dot(nt[...], jnp.concatenate(grads, axis=1))
-    mine[...] = rows[0:640]
-    theirs[...] = rows[640:1280]
-    start = pl.multiple_of(place[3] * 512, 512)
-    q_mine[...] = query[pl.ds(start, 512), :]
-    q_theirs[...] = query[pl.ds(512 - start, 512), :]
-
-
-def backward_specs():
-    return [full((D, T)), pair_cols(T)], [pair_cols(L), pair_cols(L), pl.BlockSpec((1, 4, L), lambda i: (i, 0, 0))]
-
-
-def value_grad(nt, keys, q, g, fin):
-    first, rest = backward_specs()
-    return pl.pallas_call(
-        value_kernel,
+        query = dot(keys_t[head, :], sg[j]).T
+        for half in range(2):
+            for block in range(64):
+                row = half * 512 + block % 4 * 128 + block // 4 * 8
+                q_out[half, block, :, head] = query[row : row + 8, :]
+        kgrad[:, head] = dot(sg[j], q[:, head]).astype(BF16)
+        vgrad[:, head] = dot(p[j], g[:, head]).astype(BF16)
+    out[:, 0:PAIR] = dot(nt[...], kgrad[...])
+    out[:, PAIR:] = dot(nt[...], vgrad[...])
+
+
+def backward(nt, keys, vals, q, g, fin):
+    return pl.pallas_call(
+        backward_kernel,
         grid=(PAIRS,),
-        in_specs=first + rest,
-        out_specs=[pair_cols(640)] * 2,
-        out_shape=[jax.ShapeDtypeStruct((640, D), F32)] * 2,
-        scratch_shapes=[pltpu.VMEM((2, T, L), F32), pltpu.VMEM((2, T, L), BF16)],
-        compiler_params=params(),
-        cost_estimate=cost(8e9, 1.6e7),
-        name="value_grad",
-    )(nt, keys, q, g, fin)
-
-
-def key_grad(place, nt, keys, vals, q, g, fin):
-    first, rest = backward_specs()
-    return pl.pallas_call(
-        key_kernel,
-        grid=(PAIRS,),
-        in_specs=[SMEM] + first + [pair_cols(T)] + rest,
-        out_specs=[pair_cols(640)] * 2 + [pair_cols(512)] * 2,
-        out_shape=[jax.ShapeDtypeStruct((640, D), F32)] * 2 + [jax.ShapeDtypeStruct((512, D), F32)] * 2,
+        in_specs=[
+            full((D, T)),
+            pair_cols(T),
+            pair_cols(T),
+            pair_cols(L),
+            pair_cols(L),
+            pl.BlockSpec((1, 4, L), lambda i: (i, 0, 0)),
+        ],
+        out_specs=[
+            pl.BlockSpec((D, 2 * PAIR), lambda i: (0, i)),
+            pl.BlockSpec((2, 64, 8, PAIR), lambda i: (0, 0, 0, i)),
+        ],
+        out_shape=[jax.ShapeDtypeStruct((D, 2 * D), F32), jax.ShapeDtypeStruct((2, 64, 8, D), F32)],
         scratch_shapes=[
             pltpu.VMEM((2, T, L), F32),
             pltpu.VMEM((2, T, L), F32),
             pltpu.VMEM((2, T, L), BF16),
-            pltpu.VMEM((L, PAIR), F32),
+            pltpu.VMEM((2, T, L), BF16),
+            pltpu.VMEM((T, PAIR), BF16),
+            pltpu.VMEM((T, PAIR), BF16),
         ],
         compiler_params=params(),
-        cost_estimate=cost(1.6e10, 2.4e7),
-        name="key_grad",
-    )(place, nt, keys, vals, q, g, fin)
+        cost_estimate=cost(2e10, 3.0e7),
+        name="backward",
+    )(nt, keys, vals, q, g, fin)
 
 
 def four(a0, a1, a2, a3):
@@ -257,73 +236,69 @@
     return [chunks[0], far[1], far[2], far[3]]
 
 
-def pair_kernel(place, mine, other, *outs):
+def second_kernel(rows, *outs):
     for k, out in enumerate(outs):
-        start = pl.multiple_of(lax.rem(place[2] + k, 4) * 160, 160)
-        out[...] = mine[pl.ds(start, 160), :] + other[pl.ds(start, 160), :]
-
-
-def pair_chunks(place, mine, other):
-    return pl.pallas_call(
-        pair_kernel,
-        grid=(PAIRS,),
-        in_specs=[SMEM, pair_cols(640), pair_cols(640)],
-        out_specs=[pair_cols(160)] * 4,
-        out_shape=[jax.ShapeDtypeStruct((160, D), F32)] * 4,
-        compiler_params=params(),
-        cost_estimate=cost(1e6, 1e7),
-        name="pair",
-    )(place, mine, other)
-
-
-def rows_x_kernel(value, a0, a1, a2, a3, *outs):
-    rows = four(a0, a1, a2, a3)
-    for k, out in enumerate(outs):
-        out[0:40, :] = rows[k * 40 : (k + 1) * 40]
-        out[40:80, :] = value[k * 40 : (k + 1) * 40, :]
-
-
-def rows_z_kernel(a0, a1, a2, a3, *outs):
+        out[...] = rows[k * 40 : (k + 1) * 40]
+
+
+def third_kernel(a0, a1, a2, a3, *outs):
     rows = four(a0, a1, a2, a3)
     for k, out in enumerate(outs):
         out[0:10, :] = rows[k * 10 : (k + 1) * 10]
-        out[10:20, :] = rows[40 + k * 10 : 40 + (k + 1) * 10]
-        out[20:24, :] = jnp.zeros((4, D), F32)
-
-
-def rows_last_kernel(a0, a1, a2, a3, key_rows, value_rows):
+        out[10:16, :] = jnp.zeros((6, 2 * D), F32)
+
+
+def last_kernel(a0, a1, a2, a3, key_rows, value_rows):
     rows = four(a0, a1, a2, a3)
-    key_rows[...] = rows[0:10]
-    value_rows[...] = rows[10:20]
-
-
-def query_x_kernel(place, parts, *outs):
-    rows = (parts[0] + parts[1]) + (parts[2] + parts[3])
-    total = outs[-1]
-    total[...] = rows
-    for k, out in enumerate(outs[:-1]):
-        start = pl.multiple_of(lax.rem(place[0] + k, 4) * 32, 32)
-        out[...] = total[pl.ds(start, 32), :]
-
-
-def query_sum_kernel(a0, a1, a2, a3, out):
-    out[...] = four(a0, a1, a2, a3)
-
-
-def query_halves_kernel(a0, a1, a2, a3, left, right):
-    rows = four(a0, a1, a2, a3)
-    left[...] = rows[:, 0:640]
-    right[...] = rows[:, 640:1280]
+    for i in range(PAIRS):
+        cols = slice(i * PAIR, (i + 1) * PAIR)
+        key_rows[:, cols] = rows[0:10, 2 * i * PAIR : (2 * i + 1) * PAIR]
+        value_rows[:, cols] = rows[0:10, (2 * i + 1) * PAIR : (2 * i + 2) * PAIR]
+
+
+def query_sum_kernel(parts, out):
+    rows = parts[0]
+    for k in range(1, 64):
+        rows += parts[k]
+    for k in range(16):
+        out[k] = rows
+
+
+def query_sum(parts):
+    return pl.pallas_call(
+        query_sum_kernel,
+        grid=(PAIRS,),
+        in_specs=[pl.BlockSpec((64, 8, PAIR), lambda i: (0, 0, i))],
+        out_specs=pl.BlockSpec((16, 8, PAIR), lambda i: (0, 0, i)),
+        out_shape=jax.ShapeDtypeStruct((16, 8, D), F32),
+        compiler_params=params(),
+        cost_estimate=cost(1e6, 4e6),
+        name="query_sum",
+    )(parts)
 
 
 def place_query_kernel(place, own, other, out):
-    for half, block in ((place[3], own), (1 - place[3], other)):
-        for i in range(4):
-            for k in range(4):
-                first = lax.rem(place[1] + 4 - i, 4) * 128 + lax.rem(place[0] + 4 - k, 4) * 32
-                out[pl.ds(pl.multiple_of(half * 512 + first, 32), 32), 0:640] = block[i, k, :, 0:640]
-                first = lax.rem(place[1] + 4 - k, 4) * 128 + lax.rem(place[0] + 4 - i, 4) * 32
-                out[pl.ds(pl.multiple_of(half * 512 + first, 32), 32), 640:1280] = block[i, k, :, 640:1280]
+    for k in range(4):
+        block = lax.rem(place[2] + 4 - k, 4) * 128
+        out[pl.ds(pl.multiple_of(place[3] * 512 + block, 128), 128), :] = own[k]
+        out[pl.ds(pl.multiple_of((1 - place[3]) * 512 + block, 128), 128), :] = other[k]
+
+
+def place_query(place, own, other):
+    return pl.pallas_call(
+        place_query_kernel,
+        grid=(PAIRS,),
+        in_specs=[SMEM] + [pl.BlockSpec((4, 128, PAIR), lambda i: (0, 0, i))] * 2,
+        out_specs=pair_cols(L),
+        out_shape=jax.ShapeDtypeStruct((L, D), F32),
+        compiler_params=params(),
+        cost_estimate=cost(1e6, 1e7),
+        name="place_query",
+    )(place, own, other)
+
+
+def spread(blocks):
+    return lax.all_to_all(blocks, ("seq", "dp"), split_axis=0, concat_axis=0, axis_index_groups=CORE_GROUPS)
 
 
 def numer_x_kernel(place, n0, n1, n2, n3, s0, s1, s2, s3, fin, z0, z1, z2, z3, total):
@@ -353,6 +328,10 @@
         out[rows, 640:1280] = x[2 * k + 1].astype(BF16)
 
 
+def after(first, values):
+    return lax.optimization_barrier((first, values))[1]
+
+
 def on_device(tokens, queries, key_weight, value_weight, out_grad):
     seq, dp = lax.axis_index("seq"), lax.axis_index("dp")
     place = jnp.stack([seq // 4, seq % 4, dp // 2, dp % 2]).astype(jnp.int32)
@@ -367,30 +346,13 @@
     numer = exchange([n0, n1, n2, n3], "x")
     fin = simple(merge_kernel, blocks, (PAIRS, 4, L), "finish")
 
-    v_mine, v_theirs = value_grad(nt, keys, queries, grad, fin)
-    v_other = shift(v_theirs, "c", 1)
-    k_mine, k_theirs, q_mine, q_theirs = key_grad(place, nt, keys, vals, queries, grad, fin)
-    q_other = shift(q_theirs, "c", 1)
-    k_other = shift(k_theirs, "c", 1)
-
-    v_rows = lax.psum_scatter(
-        (v_mine + v_other).reshape(4, 160, D), "dp", scatter_dimension=0, axis_index_groups=Y_GROUPS, tiled=False
-    )
-    k_chunks = exchange(pair_chunks(place, k_mine, k_other), "y")
-
-    q_parts = lax.all_to_all(
-        (q_mine + q_other).reshape(4, 128, D), "seq", split_axis=0, concat_axis=0, axis_index_groups=Z_GROUPS
-    )
-    q_parts = simple(
-        query_x_kernel, [q_parts], [(32, D)] * 4, "query_x", scalars=place, scratch=[pltpu.VMEM((128, D), F32)]
-    )
-    q_part = simple(query_sum_kernel, exchange(q_parts, "x"), (32, D), "query_sum")
-    left, right = simple(query_halves_kernel, exchange([q_part] * 4, "y"), [(32, 640)] * 2, "query_halves")
-    left = jnp.stack(exchange([left] * 4, "x"))
-    right = jnp.stack(exchange([right] * 4, "z"))
-    left = jnp.stack(exchange([left] * 4, "z"))
-    right = jnp.stack(exchange([right] * 4, "x"))
-    own_query = jnp.concatenate([left, right], axis=3)
+    terms, q_terms = backward(nt, keys, vals, queries, grad, fin)
+    q_cores = lax.all_to_all(q_terms, "dp", split_axis=0, concat_axis=0, axis_index_groups=PAIR_GROUPS)
+    q_sum = q_cores[0] + q_cores[1]
+    q_parts = spread(q_sum)
+    numer, near = after(q_sum, (numer, near))
+    rows = lax.psum_scatter(after(numer, terms), "dp", scatter_dimension=0, tiled=True)
+    own_query = lax.all_to_all(query_sum(q_parts), "seq", split_axis=0, concat_axis=0).reshape(128, D)
 
     zs = simple(
         numer_x_kernel,
@@ -402,7 +364,10 @@
         moved=7e6,
     )
     share = simple(numer_z_kernel, exchange(zs, "z"), (128, 640), "numer_z")
-    gathered = lax.all_gather(share, "seq")
+    gathered = lax.all_gather(after(q_parts, share), "seq")
+    rows = after(own_query, rows)
+    own_query = jnp.stack(exchange([own_query] * 4, "y"))
+
     attended = pl.pallas_call(
         round_kernel,
         grid=(4,),
@@ -413,14 +378,11 @@
         cost_estimate=cost(1e6, 8e6),
         name="round",
     )(gathered)
-
-    rows = simple(rows_x_kernel, [v_rows, *k_chunks], [(80, D)] * 4, "rows_x")
-    rows = simple(rows_z_kernel, exchange(rows, "x"), [(24, D)] * 4, "rows_z")
-    key_rows, value_rows = simple(rows_last_kernel, exchange(rows, "z"), [(10, D)] * 2, "rows_last")
-
-    own_query, attended, key_rows, value_rows = lax.optimization_barrier((own_query, attended, key_rows, value_rows))
     other_query = shift(own_query, "c", 1)
-    query_grad = simple(place_query_kernel, [own_query, other_query], (L, D), "place_query", scalars=place, moved=1e7)
+    query_grad = place_query(place, own_query, other_query)
+    rows = exchange(simple(second_kernel, [rows], [(40, 2 * D)] * 4, "second"), "z")
+    rows = exchange(simple(third_kernel, after(attended, rows), [(16, 2 * D)] * 4, "third"), "x")
+    key_rows, value_rows = simple(last_kernel, after(query_grad, rows), [(10, D)] * 2, "last")
     return attended.reshape(1, L, D), query_grad, key_rows, value_rows
 
 

time: 369 us -> 287 us (0.78)
  waiting for transfers between devices: 166 us -> 101 us
  blocking collectives: 0 us -> 34.9 us
  starting transfers between devices: 68.4 us -> 42.6 us
  Pallas kernels: 100 us -> 82.4 us
  other arithmetic: 8.64 us -> 2.65 us
  local copies, waits for them, and re-layouts: 9.46 us -> 5 us
    ppermute x18 -> x9, waiting for transfers between devices: 65.2 us -> 13.6 us  [shift(): lax.ppermute(array, 'seq', [(a * 4 + b, (a + step) % 4 * 4 + b) for a in...]
    all_to_all x1, waiting for transfers between devices: 38 us -> 0.01 us  [spread(): lax.all_to_all(blocks, ('seq', 'dp'), split_axis=0, concat_axis=0, axis_i...]
    all_to_all x0 -> x2, blocking collectives: none -> 34.9 us  [the longest x1 22.6 us: on_device(): lax.all_to_all(query_sum(q_parts), 'seq', split_axis=0, concat_axis=0)]
    ppermute x6 -> x3, waiting for transfers between devices: 10.7 us -> 38 us  [shift(): lax.ppermute(array, 'dp', [(a * 2 + b, (a + step) % 4 * 2 + b) for a in r...]
    ppermute x4 -> x1, waiting for transfers between devices: 17.7 us -> 0.01 us  [shift(): lax.ppermute(array, 'dp', [(a * 2 + b, a * 2 + 1 - b) for a in range(4) f...]
    ppermute x15 -> x9, waiting for transfers between devices: 34.2 us -> 49.4 us  [shift(): lax.ppermute(array, 'seq', [(a * 4 + b, a * 4 + (b + step) % 4) for a in...]
    ppermute x4 -> x1, starting transfers between devices: 14.5 us -> 1.63 us  [shift(): lax.ppermute(array, 'dp', [(a * 2 + b, a * 2 + 1 - b) for a in range(4) f...]
    pallas_call x11 -> x7, Pallas kernels: 28.7 us -> 17 us  [simple(): pl.pallas_call(kernel, in_specs=([] if scalars is None else [SMEM]) + spe...]
  transfers between devices with their start and end apart: 46 -> 25, of which waited for: 25 -> 14; matrix products, arithmetic and copies ran while one was open for 1% -> 1% of each run, Pallas kernels for 14% -> 20%
where the time goes in v3:
time: 287 us; the launch traced here: 284 us
  waiting for transfers between devices  101 us (35%)
  Pallas kernels  82.4 us (29%)
  starting transfers between devices  42.6 us (15%)
  blocking collectives  34.9 us (12%)
  between operations  15.7 us (5%)
  local copies, waits for them, and re-layouts  5 us (2%)
    ppermute x9, waiting for transfers between devices, shift(): lax.ppermute(array, 'seq', [(a * 4 + b, a * 4 + (b + step) % 4) for a in...  49.4 us
    ppermute x3, waiting for transfers between devices, shift(): lax.ppermute(array, 'dp', [(a * 2 + b, (a + step) % 4 * 2 + b) for a in r...  38 us
    pallas_call x1, Pallas kernels, backward(): pl.pallas_call(backward_kernel, grid=(PAIRS,), in_specs=[full((D, T)), pa...  24.7 us
    all_to_all x1, blocking collectives, on_device(): lax.all_to_all(query_sum(q_parts), 'seq', split_axis=0, concat_axis=0)  22.6 us
    pallas_call x1, Pallas kernels, forward(): pl.pallas_call(forward_kernel, grid=(PAIRS,), in_specs=[SMEM, full((T, D)...  20.9 us
    pallas_call x7, Pallas kernels, simple(): pl.pallas_call(kernel, in_specs=([] if scalars is None else [SMEM]) + spe...  17 us
    ppermute x9, starting transfers between devices, shift(): lax.ppermute(array, 'seq', [(a * 4 + b, a * 4 + (b + step) % 4) for a in...  14.4 us
    ppermute x9, starting transfers between devices, shift(): lax.ppermute(array, 'seq', [(a * 4 + b, (a + step) % 4 * 4 + b) for a in...  14.3 us
  transfers between devices with their start and end apart: 25, of which 14 were waited for; matrix products, arithmetic and copies ran while one was open for 1% of the time, Pallas kernels for 20%

profile of v3, /device:TPU:1, one launch (start us, length us, event | category | flops | bytes accessed | tf_op | source)
XLA Modules:
  0.0 284.3 jit_solution(16064339652461940765)
XLA Ops:
  8.7 20.9 %forward.1 = (bf16[512,1280]{1,0:T(8,128)(2,1)}, bf16[512,1280]{1,0:T(8,128)(2,1)}, bf16[512,1280]{1,0:T(8,128)(2,1)}, f32[1280,256]{1,0:T(8,128)}, f32[1280,256...) custom-call(s32[4]{0:T(128)} %pad_add_fusion.place, bf16[512,1280]{1,0:T(8,128)(2,1)} %bitcast.26, ...), custom_call_target="tpu_custom_call" | custom-call | flops 12000000000 | bytes 24000000 | tf_op jit(solution)/shard_map/forward/pallas_call | solution.py:99
  29.7 3.4 %collective-permute-start.2 = (f32[5,4,1024]{2,1,0:T(4,128)}, f32[5,4,1024]{2,1,0:T(4,128)S(1)}, u32[]{:S(2)}, u32[]{:S(2)}) collective-permute-start(f32[5,4,1024]{2,1,0:T(4,128)} %get-tuple-element.76.s0), channel_id=1, source_target_pairs={{0,96},{8,104},{16,112},{24,120},{32,0},{40,8},{48,16},{56,24},{64... | collective-permute-start | bytes 245768 | tf_op jit(solution)/shard_map/ppermute | solution.py:29
  34.8 4.5 %reorder.1.nt = bf16[1280,512]{1,0:T(8,128)(2,1)} custom-call(s32[1,1280]{1,0:T(1,128)} %reshape.18.order, bf16[512,1280]{1,0:T(8,128)(2,1)} %get-tuple-element.56.normed), custom_call_target="tpu_custom_call" | custom-call | flops 1677721600 | bytes 3000000 | tf_op jit(solution)/shard_map/reorder/pallas_call | solution.py:156
  40.1 1.7 merge.1.s0
  41.9 3.8 %collective-permute-start.5 = (f32[5,4,1024]{2,1,0:T(4,128)}, f32[5,4,1024]{2,1,0:T(4,128)S(1)}, u32[]{:S(2)}, u32[]{:S(2)}) collective-permute-start(f32[5,4,1024]{2,1,0:T(4,128)} %merge.1.s0), channel_id=1, source_target_pairs={{0,24},{8,0},{16,8},{24,16},{32,56},{40,32},{48,40},{56,48},{64,88... | collective-permute-start | bytes 245768 | tf_op jit(solution)/shard_map/ppermute | solution.py:31
  47.7 1.7 collective-permute-start.7
  52.0 1.7 finish.1.fin
  53.7 24.7 %backward.1 = (f32[1280,2560]{1,0:T(8,128)}, f32[2,64,8,1280]{3,2,1,0:T(8,128)}) custom-call(bf16[1280,512]{1,0:T(8,128)(2,1)} %reorder.1.nt, bf16[512,1280]{1,0:T(8,128)(2,1)} %get-tuple-element.61.keys, bf16[512,1280]{1,0:T(8,128)(2,1)} %get-tuple-element.62.vals, bf16[1024,1280]{1,0:T(8,128)(2,1)} %q.3, bf16[1024,1280]{1,0:T(8,128)(2,1)} %bitcast.25, ...), custom_call_target="tpu_custom_call" | custom-call | flops 20000000000 | bytes 30000000 | tf_op jit(solution)/shard_map/backward/pallas_call | solution.py:200
  78.4 12.3 %all_to_all.15 = f32[2,64,8,1280]{3,2,1,0:T(8,128)S(1)} all-to-all(f32[2,64,8,1280]{3,2,1,0:T(8,128)} %get-tuple-element.67), channel_id=1, replica_groups={{0,1},{2,3},{4,5},{6,7},{8,9},{10,11},{12,13},{14,15},{16,17},{18,19},{..., dimensions={0} | all-to-all | bytes 10485760 | tf_op jit(solution)/shard_map/all_to_all | solution.py:350
  90.7 1.8 fusion
  92.5 11.6 %collective-permute-done.7.n2 = f32[1280,256]{1,0:T(8,128)} collective-permute-done((f32[1280,256]{1,0:T(8,128)S(1)}, f32[1280,256]{1,0:T(8,128)}, u32[]{:S(2)}, u32[]{:S(2)}) %collective-permute-start.7) | collective-permute-done | bytes 1310752 | tf_op jit(solution)/shard_map/ppermute | solution.py:29
  104.1 1.8 collective-permute-done.8.n3
  105.9 10.4 %all-to-all-start.1 = ((f32[64,8,1280]{2,1,0:T(8,128)}), f32[64,8,1280]{2,1,0:T(8,128)S(1)}, u32[]{:S(2)}, u32[]{:S(2)}) async-start(f32[64,8,1280]{2,1,0:T(8,128)} %fusion), calls=%async_computation.1 | async-start | bytes 5242880 | tf_op jit(solution)/shard_map/all_to_all | solution.py:301
  116.4 4.6 %numer_x.1 = (f32[640,128]{1,0:T(8,128)}, f32[640,128]{1,0:T(8,128)}, f32[640,128]{1,0:T(8,128)}, f32[640,128]{1,0:T(8,128)}) custom-call(s32[4]{0:T(128)} %pad_add_fusion.place, f32[1280,256]{1,0:T(8,128)} %get-tuple-element.72.n0, f32[1280,256]{1,0:T(8,128)} %collective-permute-done.6.n1, f32[1280,256]{1,0:T(8,128)} %collective-permute-done.7.n2, ...), custom_call_target="tpu_custom_call" | custom-call | flops 1000000 | bytes 7000000 | tf_op jit(solution)/shard_map/numer_x/pallas_call | solution.py:138
  122.4 2.6 collective-permute-start.10
  126.1 30.0 %collective-permute-done.9.z1 = f32[640,128]{1,0:T(8,128)S(1)} collective-permute-done((f32[640,128]{1,0:T(8,128)}, f32[640,128]{1,0:T(8,128)S(1)}, u32[]{:S(2)}, u32[]{:S(2)}) %collective-permute-start.9) | collective-permute-done | bytes 327712 | tf_op jit(solution)/shard_map/ppermute | solution.py:31
  156.1 6.8 %collective-permute-done.10.z2 = f32[640,128]{1,0:T(8,128)S(1)} collective-permute-done((f32[640,128]{1,0:T(8,128)}, f32[640,128]{1,0:T(8,128)S(1)}, u32[]{:S(2)}, u32[]{:S(2)}) %collective-permute-start.10) | collective-permute-done | bytes 327712 | tf_op jit(solution)/shard_map/ppermute | solution.py:31
  164.3 2.2 numer_z.1
  167.9 4.3 %query_sum.1 = f32[16,8,1280]{2,1,0:T(8,128)} custom-call(f32[64,8,1280]{2,1,0:T(8,128)} %copy-done), custom_call_target="tpu_custom_call" | custom-call | flops 1000000 | bytes 4000000 | tf_op jit(solution)/shard_map/query_sum/pallas_call | solution.py:268
  172.2 22.6 %all_to_all.16 = f32[16,8,1280]{2,1,0:T(8,128)S(1)} all-to-all(f32[16,8,1280]{2,1,0:T(8,128)} %query_sum.1), channel_id=1, replica_groups=mesh['seq'=16,'dp'=8] {'seq'}, dimensions={0} | all-to-all | bytes 1310720 | tf_op jit(solution)/shard_map/all_to_all | solution.py:355
  196.6 21.5 %collective-permute-done.14 = f32[128,1280]{1,0:T(8,128)S(1)} collective-permute-done((f32[128,1280]{1,0:T(8,128)S(1)}, f32[128,1280]{1,0:T(8,128)S(1)}, u32[]{:S(2)}, u32[]{:S(2)}) %collective-permute-start.14) | collective-permute-done | bytes 655392 | tf_op jit(solution)/shard_map/ppermute | solution.py:33
  219.7 14.8 %collective-permute-done.12 = f32[128,1280]{1,0:T(8,128)S(1)} collective-permute-done((f32[128,1280]{1,0:T(8,128)S(1)}, f32[128,1280]{1,0:T(8,128)S(1)}, u32[]{:S(2)}, u32[]{:S(2)}) %collective-permute-start.12) | collective-permute-done | bytes 655392 | tf_op jit(solution)/shard_map/ppermute | solution.py:33
  236.4 2.6 second.1
  239.4 2.5 collective-permute-start.17
  241.9 2.1 collective-permute-start.18
  244.0 4.6 %round.1 = bf16[1024,1280]{1,0:T(8,128)(2,1)} custom-call(f32[16,128,640]{2,1,0:T(8,128)} %bitcast.15), custom_call_target="tpu_custom_call" | custom-call | flops 1000000 | bytes 8000000 | tf_op jit(solution)/shard_map/round/pallas_call | solution.py:371
  249.1 7.5 %collective-permute-done.17.a2 = f32[40,2560]{1,0:T(8,128)S(1)} collective-permute-done((f32[40,2560]{1,0:T(8,128)}, f32[40,2560]{1,0:T(8,128)S(1)}, u32[]{:S(2)}, u32[]{:S(2)}) %collective-permute-start.17) | collective-permute-done | bytes 409632 | tf_op jit(solution)/shard_map/ppermute | solution.py:31
  256.6 3.1 %collective-permute-done.18.a3 = f32[40,2560]{1,0:T(8,128)} collective-permute-done((f32[40,2560]{1,0:T(8,128)}, f32[40,2560]{1,0:T(8,128)}, u32[]{:S(2)}, u32[]{:S(2)}) %collective-permute-start.18) | collective-permute-done | bytes 409632 | tf_op jit(solution)/shard_map/ppermute | solution.py:31
  259.7 2.3 third.1
  262.0 4.8 %collective-permute-start.20 = (f32[16,2560]{1,0:T(8,128)}, f32[16,2560]{1,0:T(8,128)S(1)}, u32[]{:S(2)}, u32[]{:S(2)}) collective-permute-start(f32[16,2560]{1,0:T(8,128)} %get-tuple-element.98), channel_id=1, source_target_pairs={{0,64},{8,72},{16,80},{24,88},{32,96},{40,104},{48,112},{56,120},{... | collective-permute-start | bytes 491528 | tf_op jit(solution)/shard_map/ppermute | solution.py:29
  267.7 6.5 %place_query.1 = f32[1024,1280]{1,0:T(8,128)} custom-call(s32[4]{0:T(128)} %pad_add_fusion.place, f32[4,128,1280]{2,1,0:T(8,128)} %copy-done.1, f32[4,128,1280]{2,1,0:T(8,128)} %collective-permute-done.15.other), custom_call_target="tpu_custom_call" | custom-call | flops 1000000 | bytes 10000000 | tf_op jit(solution)/shard_map/place_query/pallas_call | solution.py:288
  275.0 1.8 last.1
  (88 shorter events, 21.0 us)
Async XLA Ops:
  8.0 228.4 %reduce-scatter.2.cloned.1.call-start = ((), (), s32[]{:S(2)}) async-start(), calls=%async_computation.4 | async-start | bytes 14745600 | tf_op jit(solution)/shard_map/reduce_scatter | solution.py:354
  8.7 25.5 %copy-start.16 = (s32[1280]{0:T(1024)S(1)}, s32[1280]{0:T(1024)}, u32[]{:S(2)}) copy-start(s32[1280]{0:T(1024)} %constant.82.clone) | copy-start | bytes 15364
  8.7 25.5 %copy-start.17 = (s32[1280]{0:T(1024)S(1)}, s32[1280]{0:T(1024)}, u32[]{:S(2)}) copy-start(s32[1280]{0:T(1024)} %constant.81.clone) | copy-start | bytes 15364
  8.7 25.5 %copy-start.18 = (s32[1280]{0:T(1024)S(1)}, s32[1280]{0:T(1024)}, u32[]{:S(2)}) copy-start(s32[1280]{0:T(1024)} %constant.80.clone) | copy-start | bytes 15364
  8.7 25.5 %copy-start.19 = (s32[1280]{0:T(1024)S(1)}, s32[1280]{0:T(1024)}, u32[]{:S(2)}) copy-start(s32[1280]{0:T(1024)} %constant.79.clone) | copy-start | bytes 15364
  8.7 25.5 %copy-start.20 = (s32[1280]{0:T(1024)S(1)}, s32[1280]{0:T(1024)}, u32[]{:S(2)}) copy-start(s32[1280]{0:T(1024)} %constant.78.clone) | copy-start | bytes 15364
  29.7 9.7 %collective-permute-start.2 = (f32[5,4,1024]{2,1,0:T(4,128)}, f32[5,4,1024]{2,1,0:T(4,128)S(1)}, u32[]{:S(2)}, u32[]{:S(2)}) collective-permute-start(f32[5,4,1024]{2,1,0:T(4,128)} %get-tuple-element.76.s0), channel_id=1, source_target_pairs={{0,96},{8,104},{16,112},{24,120},{32,0},{40,8},{48,16},{56,24},{64... | collective-permute-start | bytes 245768 | tf_op jit(solution)/shard_map/ppermute | solution.py:29
  33.0 6.3 %collective-permute-start.1 = (f32[5,4,1024]{2,1,0:T(4,128)}, f32[5,4,1024]{2,1,0:T(4,128)S(1)}, u32[]{:S(2)}, u32[]{:S(2)}) collective-permute-start(f32[5,4,1024]{2,1,0:T(4,128)} %get-tuple-element.76.s0), channel_id=1, source_target_pairs={{0,64},{8,72},{16,80},{24,88},{32,96},{40,104},{48,112},{56,120},{... | collective-permute-start | bytes 245768 | tf_op jit(solution)/shard_map/ppermute | solution.py:29
  33.6 5.9 %collective-permute-start = (f32[5,4,1024]{2,1,0:T(4,128)}, f32[5,4,1024]{2,1,0:T(4,128)S(1)}, u32[]{:S(2)}, u32[]{:S(2)}) collective-permute-start(f32[5,4,1024]{2,1,0:T(4,128)} %get-tuple-element.76.s0), channel_id=1, source_target_pairs={{0,32},{8,40},{16,48},{24,56},{32,64},{40,72},{48,80},{56,88},{64,... | collective-permute-start | bytes 245768 | tf_op jit(solution)/shard_map/ppermute | solution.py:29
  34.8 14.7 %copy-start.21 = (f32[1280,256]{1,0:T(8,128)S(1)}, f32[1280,256]{1,0:T(8,128)}, u32[]{:S(2)}) copy-start(f32[1280,256]{1,0:T(8,128)} %get-tuple-element.71) | copy-start | bytes 3932164
  41.9 7.6 %collective-permute-start.5 = (f32[5,4,1024]{2,1,0:T(4,128)}, f32[5,4,1024]{2,1,0:T(4,128)S(1)}, u32[]{:S(2)}, u32[]{:S(2)}) collective-permute-start(f32[5,4,1024]{2,1,0:T(4,128)} %merge.1.s0), channel_id=1, source_target_pairs={{0,24},{8,0},{16,8},{24,16},{32,56},{40,32},{48,40},{56,48},{64,88... | collective-permute-start | bytes 245768 | tf_op jit(solution)/shard_map/ppermute | solution.py:31
  45.6 5.1 %collective-permute-start.4 = (f32[5,4,1024]{2,1,0:T(4,128)}, f32[5,4,1024]{2,1,0:T(4,128)S(1)}, u32[]{:S(2)}, u32[]{:S(2)}) collective-permute-start(f32[5,4,1024]{2,1,0:T(4,128)} %merge.1.s0), channel_id=1, source_target_pairs={{0,16},{8,24},{16,0},{24,8},{32,48},{40,56},{48,32},{56,40},{64,80... | collective-permute-start | bytes 245768 | tf_op jit(solution)/shard_map/ppermute | solution.py:31
  45.6 5.6 %collective-permute-start.3 = (f32[5,4,1024]{2,1,0:T(4,128)}, f32[5,4,1024]{2,1,0:T(4,128)S(1)}, u32[]{:S(2)}, u32[]{:S(2)}) collective-permute-start(f32[5,4,1024]{2,1,0:T(4,128)} %merge.1.s0), channel_id=1, source_target_pairs={{0,8},{8,16},{16,24},{24,0},{32,40},{40,48},{48,56},{56,32},{64,72... | collective-permute-start | bytes 245768 | tf_op jit(solution)/shard_map/ppermute | solution.py:31
  46.3 46.2 %collective-permute-start.6 = (f32[1280,256]{1,0:T(8,128)S(1)}, f32[1280,256]{1,0:T(8,128)}, u32[]{:S(2)}, u32[]{:S(2)}) collective-permute-start(f32[1280,256]{1,0:T(8,128)S(1)} %copy-done.23), channel_id=1, source_target_pairs={{0,32},{8,40},{16,48},{24,56},{32,64},{40,72},{48,80},{56,88},{64,... | collective-permute-start | bytes 3932168 | tf_op jit(solution)/shard_map/ppermute | solution.py:29
  47.7 56.4 %collective-permute-start.7 = (f32[1280,256]{1,0:T(8,128)S(1)}, f32[1280,256]{1,0:T(8,128)}, u32[]{:S(2)}, u32[]{:S(2)}) collective-permute-start(f32[1280,256]{1,0:T(8,128)S(1)} %copy-done.22), channel_id=1, source_target_pairs={{0,64},{8,72},{16,80},{24,88},{32,96},{40,104},{48,112},{56,120},{... | collective-permute-start | bytes 3932168 | tf_op jit(solution)/shard_map/ppermute | solution.py:29
  49.5 56.4 %collective-permute-start.8 = (f32[1280,256]{1,0:T(8,128)S(1)}, f32[1280,256]{1,0:T(8,128)}, u32[]{:S(2)}, u32[]{:S(2)}) collective-permute-start(f32[1280,256]{1,0:T(8,128)S(1)} %copy-done.21), channel_id=1, source_target_pairs={{0,96},{8,104},{16,112},{24,120},{32,0},{40,8},{48,16},{56,24},{64... | collective-permute-start | bytes 3932168 | tf_op jit(solution)/shard_map/ppermute | solution.py:29
  105.9 60.5 %all-to-all-start.1 = ((f32[64,8,1280]{2,1,0:T(8,128)}), f32[64,8,1280]{2,1,0:T(8,128)S(1)}, u32[]{:S(2)}, u32[]{:S(2)}) async-start(f32[64,8,1280]{2,1,0:T(8,128)} %fusion), calls=%async_computation.1 | async-start | bytes 5242880 | tf_op jit(solution)/shard_map/all_to_all | solution.py:301
  116.4 127.6 %all-gather.3.cloned.1.call-start = ((), (), s32[]{:S(2)}) async-start(), calls=%async_computation.5 | async-start | bytes 5570560 | tf_op jit(solution)/shard_map/all_gather | solution.py:367
  121.0 35.0 %collective-permute-start.9 = (f32[640,128]{1,0:T(8,128)}, f32[640,128]{1,0:T(8,128)S(1)}, u32[]{:S(2)}, u32[]{:S(2)}) collective-permute-start(f32[640,128]{1,0:T(8,128)} %get-tuple-element.81), channel_id=1, source_target_pairs={{0,8},{8,16},{16,24},{24,0},{32,40},{40,48},{48,56},{56,32},{64,72... | collective-permute-start | bytes 983048 | tf_op jit(solution)/shard_map/ppermute | solution.py:31
  122.4 40.4 %collective-permute-start.10 = (f32[640,128]{1,0:T(8,128)}, f32[640,128]{1,0:T(8,128)S(1)}, u32[]{:S(2)}, u32[]{:S(2)}) collective-permute-start(f32[640,128]{1,0:T(8,128)} %get-tuple-element.82), channel_id=1, source_target_pairs={{0,16},{8,24},{16,0},{24,8},{32,48},{40,56},{48,32},{56,40},{64,80... | collective-permute-start | bytes 983048 | tf_op jit(solution)/shard_map/ppermute | solution.py:31
  125.0 38.5 %collective-permute-start.11 = (f32[640,128]{1,0:T(8,128)}, f32[640,128]{1,0:T(8,128)S(1)}, u32[]{:S(2)}, u32[]{:S(2)}) collective-permute-start(f32[640,128]{1,0:T(8,128)} %get-tuple-element.83), channel_id=1, source_target_pairs={{0,24},{8,0},{16,8},{24,16},{32,56},{40,32},{48,40},{56,48},{64,88... | collective-permute-start | bytes 983048 | tf_op jit(solution)/shard_map/ppermute | solution.py:31
  194.8 23.3 %collective-permute-start.14 = (f32[128,1280]{1,0:T(8,128)S(1)}, f32[128,1280]{1,0:T(8,128)S(1)}, u32[]{:S(2)}, u32[]{:S(2)}) collective-permute-start(f32[128,1280]{1,0:T(8,128)S(1)} %bitcast.16), channel_id=1, source_target_pairs={{0,6},{1,7},{2,0},{3,1},{4,2},{5,3},{6,4},{7,5},{8,14},{9,15},{10,... | collective-permute-start | bytes 1966088 | tf_op jit(solution)/shard_map/ppermute | solution.py:33
  195.5 24.2 %collective-permute-start.13 = (f32[128,1280]{1,0:T(8,128)S(1)}, f32[128,1280]{1,0:T(8,128)S(1)}, u32[]{:S(2)}, u32[]{:S(2)}) collective-permute-start(f32[128,1280]{1,0:T(8,128)S(1)} %bitcast.17), channel_id=1, source_target_pairs={{0,4},{1,5},{2,6},{3,7},{4,0},{5,1},{6,2},{7,3},{8,12},{9,13},{10,... | collective-permute-start | bytes 1966088 | tf_op jit(solution)/shard_map/ppermute | solution.py:33
  195.8 38.7 %collective-permute-start.12 = (f32[128,1280]{1,0:T(8,128)S(1)}, f32[128,1280]{1,0:T(8,128)S(1)}, u32[]{:S(2)}, u32[]{:S(2)}) collective-permute-start(f32[128,1280]{1,0:T(8,128)S(1)} %bitcast.18), channel_id=1, source_target_pairs={{0,2},{1,3},{2,4},{3,5},{4,6},{5,7},{6,0},{7,1},{8,10},{9,11},{10,... | collective-permute-start | bytes 1966088 | tf_op jit(solution)/shard_map/ppermute | solution.py:33
  234.7 13.8 %copy-start.1 = (f32[4,128,1280]{2,1,0:T(8,128)}, f32[4,128,1280]{2,1,0:T(8,128)S(1)}, u32[]{:S(2)}) copy-start(f32[4,128,1280]{2,1,0:T(8,128)S(1)} %pad_maximum_fusion.own) | copy-start | bytes 7864324
  234.8 32.9 %collective-permute-start.15 = (f32[4,128,1280]{2,1,0:T(8,128)S(1)}, f32[4,128,1280]{2,1,0:T(8,128)}, u32[]{:S(2)}, u32[]{:S(2)}) collective-permute-start(f32[4,128,1280]{2,1,0:T(8,128)S(1)} %pad_maximum_fusion.own), channel_id=1, source_target_pairs={{0,1},{1,0},{2,3},{3,2},{4,5},{5,4},{6,7},{7,6},{8,9},{9,8},{10,11... | collective-permute-start | bytes 7864328 | tf_op jit(solution)/shard_map/ppermute | solution.py:34
  239.0 10.1 %collective-permute-start.16 = (f32[40,2560]{1,0:T(8,128)}, f32[40,2560]{1,0:T(8,128)S(1)}, u32[]{:S(2)}, u32[]{:S(2)}) collective-permute-start(f32[40,2560]{1,0:T(8,128)} %get-tuple-element.89), channel_id=1, source_target_pairs={{0,8},{8,16},{16,24},{24,0},{32,40},{40,48},{48,56},{56,32},{64,72... | collective-permute-start | bytes 1228808 | tf_op jit(solution)/shard_map/ppermute | solution.py:31
  239.4 17.2 %collective-permute-start.17 = (f32[40,2560]{1,0:T(8,128)}, f32[40,2560]{1,0:T(8,128)S(1)}, u32[]{:S(2)}, u32[]{:S(2)}) collective-permute-start(f32[40,2560]{1,0:T(8,128)} %get-tuple-element.90), channel_id=1, source_target_pairs={{0,16},{8,24},{16,0},{24,8},{32,48},{40,56},{48,32},{56,40},{64,80... | collective-permute-start | bytes 1228808 | tf_op jit(solution)/shard_map/ppermute | solution.py:31
  241.9 17.8 %collective-permute-start.18 = (f32[40,2560]{1,0:T(8,128)}, f32[40,2560]{1,0:T(8,128)}, u32[]{:S(2)}, u32[]{:S(2)}) collective-permute-start(f32[40,2560]{1,0:T(8,128)} %get-tuple-element.91), channel_id=1, source_target_pairs={{0,24},{8,0},{16,8},{24,16},{32,56},{40,32},{48,40},{56,48},{64,88... | collective-permute-start | bytes 1228808 | tf_op jit(solution)/shard_map/ppermute | solution.py:31
  262.0 12.2 %collective-permute-start.19 = (f32[16,2560]{1,0:T(8,128)}, f32[16,2560]{1,0:T(8,128)S(1)}, u32[]{:S(2)}, u32[]{:S(2)}) collective-permute-start(f32[16,2560]{1,0:T(8,128)} %get-tuple-element.97), channel_id=1, source_target_pairs={{0,32},{8,40},{16,48},{24,56},{32,64},{40,72},{48,80},{56,88},{64,... | collective-permute-start | bytes 491528 | tf_op jit(solution)/shard_map/ppermute | solution.py:29
  262.0 12.2 %collective-permute-start.20 = (f32[16,2560]{1,0:T(8,128)}, f32[16,2560]{1,0:T(8,128)S(1)}, u32[]{:S(2)}, u32[]{:S(2)}) collective-permute-start(f32[16,2560]{1,0:T(8,128)} %get-tuple-element.98), channel_id=1, source_target_pairs={{0,64},{8,72},{16,80},{24,88},{32,96},{40,104},{48,112},{56,120},{... | collective-permute-start | bytes 491528 | tf_op jit(solution)/shard_map/ppermute | solution.py:29
  266.8 7.4 %collective-permute-start.21 = (f32[16,2560]{1,0:T(8,128)}, f32[16,2560]{1,0:T(8,128)S(1)}, u32[]{:S(2)}, u32[]{:S(2)}) collective-permute-start(f32[16,2560]{1,0:T(8,128)} %get-tuple-element.99), channel_id=1, source_target_pairs={{0,96},{8,104},{16,112},{24,120},{32,0},{40,8},{48,16},{56,24},{64... | collective-permute-start | bytes 491528 | tf_op jit(solution)/shard_map/ppermute | solution.py:29
  (17 other events, 55.7 us)
Sparse Core Ops, SparseCore 0:
  106.0 125.0 reduce-scatter.1
Sparse Core Ops, SparseCore 1:
  166.6 60.0 all-gather.2

commit v4 on v3

--- a/solution.py
+++ b/solution.py
@@ -15,10 +15,12 @@
 D = 1280
 PAIR = 2 * HD
 SCALE = HD ** (-0.5)
+SCALE2 = SCALE * 1.4426950408889634
 VMEM_LIMIT = 56 * 1024 * 1024
 PAIRS = H // 2
 COST = 1.0
 PAIR_GROUPS = [[a * 2, a * 2 + 1] for a in range(4)]
+PLANE_GROUPS = [[a * 32 + b * 2 + c for b in range(16)] for a in range(4) for c in range(2)]
 CORE_GROUPS = [[a * 2 + b for a in range(64)] for b in range(2)]
 F32 = jnp.float32
 BF16 = jnp.bfloat16
@@ -74,20 +76,19 @@
     grad_t = g[...].T
     for j in range(2):
         head = slice(j * HD, (j + 1) * HD)
-        s[j] = nt_dot(keys[:, head], q[:, head])
         tops, totals = [], []
-        for tile in range(L // 128):
-            at = slice(tile * 128, (tile + 1) * 128)
-            scores = s[j, :, at] * SCALE
-            high = jnp.max(scores, axis=0, keepdims=True)
-            shifted = jnp.exp(scores - high)
+        for tile in range(L // 256):
+            at = slice(tile * 256, (tile + 1) * 256)
+            scores = nt_dot(keys[:, head], q[at, head])
+            high = jnp.max(scores, axis=0, keepdims=True) * SCALE2
+            shifted = jnp.exp2(scores * SCALE2 - high)
             tops.append(high)
             totals.append(jnp.sum(shifted, axis=0, keepdims=True))
             w[j, :, at] = shifted.astype(BF16)
         total = jnp.concatenate(totals, axis=1)
         part = dot(vals_t[head, :], w[j]) * (1.0 / total)
         numer[head, :] = part
-        stats[0, j : j + 1, :] = jnp.concatenate(tops, axis=1) + jnp.log(total)
+        stats[0, j : j + 1, :] = jnp.concatenate(tops, axis=1) + jnp.log2(total)
         stats[0, 2 + j : 3 + j, :] = jnp.sum(part * grad_t[head, :].astype(F32), axis=0, keepdims=True)
     for k, out in enumerate((n0, n1, n2, n3)):
         start = pl.multiple_of(lax.rem(place[0] + k, 4) * 256, 256)
@@ -124,10 +125,10 @@
     total = jnp.zeros_like(top)
     inner = jnp.zeros_like(top)
     for b in blocks:
-        factor = jnp.exp(b[:, 0:2, :] - top)
+        factor = jnp.exp2(b[:, 0:2, :] - top)
         total += factor
         inner += b[:, 2:4, :] * factor
-    out[:, 0:2, :] = top + jnp.log(total)
+    out[:, 0:2, :] = top + jnp.log2(total)
     out[:, 2:4, :] = inner / total
 
 
@@ -178,18 +179,13 @@
     keys_t = keys[...].T
     for j in range(2):
         head = slice(j * HD, (j + 1) * HD)
-        s[j] = nt_dot(keys[:, head], q[:, head])
-        pg[j] = nt_dot(vals[:, head], g[:, head])
-        for tile in range(L // 128):
-            at = slice(tile * 128, (tile + 1) * 128)
-            probs = jnp.exp(s[j, :, at] * SCALE - fin[0, j : j + 1, at])
+        for tile in range(L // 256):
+            at = slice(tile * 256, (tile + 1) * 256)
+            probs = jnp.exp2(nt_dot(keys[:, head], q[at, head]) * SCALE2 - fin[0, j : j + 1, at])
             p[j, :, at] = probs.astype(BF16)
-            sg[j, :, at] = (probs * (pg[j, :, at] - fin[0, 2 + j : 3 + j, at]) * SCALE).astype(BF16)
+            sg[j, :, at] = (probs * (nt_dot(vals[:, head], g[at, head]) - fin[0, 2 + j : 3 + j, at]) * SCALE).astype(BF16)
         query = dot(keys_t[head, :], sg[j]).T
-        for half in range(2):
-            for block in range(64):
-                row = half * 512 + block % 4 * 128 + block // 4 * 8
-                q_out[half, block, :, head] = query[row : row + 8, :]
+        q_out[:, :, :, head] = query.reshape(2, 64, 8, HD)
         kgrad[:, head] = dot(sg[j], q[:, head]).astype(BF16)
         vgrad[:, head] = dot(p[j], g[:, head]).astype(BF16)
     out[:, 0:PAIR] = dot(nt[...], kgrad[...])
@@ -279,7 +275,7 @@
 
 def place_query_kernel(place, own, other, out):
     for k in range(4):
-        block = lax.rem(place[2] + 4 - k, 4) * 128
+        block = lax.rem(place[0] + 4 - k, 4) * 128
         out[pl.ds(pl.multiple_of(place[3] * 512 + block, 128), 128), :] = own[k]
         out[pl.ds(pl.multiple_of((1 - place[3]) * 512 + block, 128), 128), :] = other[k]
 
@@ -308,7 +304,7 @@
         pair, j = h // 2, h % 2
         acc = jnp.zeros((HD, 256), F32)
         for n, s in ((n0, s0), (n1, s1), (n2, s2), (n3, s3)):
-            acc += n[rows, :] * jnp.exp(s[pair, j : j + 1, at] - fin[pair, j : j + 1, at])
+            acc += n[rows, :] * jnp.exp2(s[pair, j : j + 1, at] - fin[pair, j : j + 1, at])
         total[rows, :] = acc
     for k, out in enumerate((z0, z1, z2, z3)):
         spot = lax.rem(place[1] + k, 4)
@@ -352,7 +348,9 @@
     q_parts = spread(q_sum)
     numer, near = after(q_sum, (numer, near))
     rows = lax.psum_scatter(after(numer, terms), "dp", scatter_dimension=0, tiled=True)
-    own_query = lax.all_to_all(query_sum(q_parts), "seq", split_axis=0, concat_axis=0).reshape(128, D)
+    own_query = lax.all_to_all(
+        query_sum(q_parts), ("seq", "dp"), split_axis=0, concat_axis=0, axis_index_groups=PLANE_GROUPS
+    ).reshape(128, D)
 
     zs = simple(
         numer_x_kernel,
@@ -366,7 +364,10 @@
     share = simple(numer_z_kernel, exchange(zs, "z"), (128, 640), "numer_z")
     gathered = lax.all_gather(after(q_parts, share), "seq")
     rows = after(own_query, rows)
-    own_query = jnp.stack(exchange([own_query] * 4, "y"))
+    rows = exchange(simple(second_kernel, [rows], [(40, 2 * D)] * 4, "second"), "z")
+    rows = simple(third_kernel, rows, [(16, 2 * D)] * 4, "third")
+    own_query = jnp.stack(after(rows[0], exchange([own_query] * 4, "x")))
+    rows = exchange(rows, "x")
 
     attended = pl.pallas_call(
         round_kernel,
@@ -378,11 +379,9 @@
         cost_estimate=cost(1e6, 8e6),
         name="round",
     )(gathered)
-    other_query = shift(own_query, "c", 1)
+    other_query = after((attended, rows), shift(own_query, "c", 1))
     query_grad = place_query(place, own_query, other_query)
-    rows = exchange(simple(second_kernel, [rows], [(40, 2 * D)] * 4, "second"), "z")
-    rows = exchange(simple(third_kernel, after(attended, rows), [(16, 2 * D)] * 4, "third"), "x")
-    key_rows, value_rows = simple(last_kernel, after(query_grad, rows), [(10, D)] * 2, "last")
+    key_rows, value_rows = simple(last_kernel, rows, [(10, D)] * 2, "last")
     return attended.reshape(1, L, D), query_grad, key_rows, value_rows
 
 

time: 287 us -> 282 us (0.983)
  waiting for transfers between devices: 101 us -> 108 us
  Pallas kernels: 82.4 us -> 76.6 us
  starting transfers between devices: 42.6 us -> 39.6 us
    ppermute x3 -> x0, waiting for transfers between devices: 38 us -> none  [shift(): lax.ppermute(array, 'dp', [(a * 2 + b, (a + step) % 4 * 2 + b) for a in r...]
    reduce_scatter x1, waiting for transfers between devices: 0.01 us -> 24.5 us  [on_device(): lax.psum_scatter(after(numer, terms), 'dp', scatter_dimension=0, tiled=True)]
    ppermute x9 -> x12, waiting for transfers between devices: 13.6 us -> 27.2 us  [shift(): lax.ppermute(array, 'seq', [(a * 4 + b, (a + step) % 4 * 4 + b) for a in...]
    ppermute x9, waiting for transfers between devices: 49.4 us -> 56.4 us  [shift(): lax.ppermute(array, 'seq', [(a * 4 + b, a * 4 + (b + step) % 4) for a in...]
    pallas_call x1, Pallas kernels: 24.7 us -> 21.5 us  [backward(): pl.pallas_call(backward_kernel, grid=(PAIRS,), in_specs=[full((D, T)), pa...]
    ppermute x9 -> x12, starting transfers between devices: 14.3 us -> 15.5 us  [shift(): lax.ppermute(array, 'seq', [(a * 4 + b, (a + step) % 4 * 4 + b) for a in...]
  transfers between devices with their start and end apart: 25 -> 25, of which waited for: 14 -> 14; matrix products, arithmetic and copies ran while one was open for 1% -> 1% of each run, Pallas kernels for 20% -> 18%
where the time goes in v4:
time: 282 us; the launch traced here: 281 us
  waiting for transfers between devices  108 us (38%)
  Pallas kernels  76.6 us (27%)
  starting transfers between devices  39.6 us (14%)
  blocking collectives  32.8 us (12%)
  between operations  15.6 us (6%)
  local copies, waits for them, and re-layouts  5.92 us (2%)
    ppermute x9, waiting for transfers between devices, shift(): lax.ppermute(array, 'seq', [(a * 4 + b, a * 4 + (b + step) % 4) for a in...  56.4 us
    ppermute x12, waiting for transfers between devices, shift(): lax.ppermute(array, 'seq', [(a * 4 + b, (a + step) % 4 * 4 + b) for a in...  27.2 us
    reduce_scatter x1, waiting for transfers between devices, on_device(): lax.psum_scatter(after(numer, terms), 'dp', scatter_dimension=0, tiled=True)  24.5 us
    pallas_call x1, Pallas kernels, backward(): pl.pallas_call(backward_kernel, grid=(PAIRS,), in_specs=[full((D, T)), pa...  21.5 us
    all_to_all x1, blocking collectives, on_device(): lax.all_to_all(query_sum(q_parts), ('seq', 'dp'), split_axis=0, concat_ax...  20.4 us
    pallas_call x1, Pallas kernels, forward(): pl.pallas_call(forward_kernel, grid=(PAIRS,), in_specs=[SMEM, full((T, D)...  18.2 us
    pallas_call x7, Pallas kernels, simple(): pl.pallas_call(kernel, in_specs=([] if scalars is None else [SMEM]) + spe...  17 us
    ppermute x12, starting transfers between devices, shift(): lax.ppermute(array, 'seq', [(a * 4 + b, (a + step) % 4 * 4 + b) for a in...  15.5 us
  transfers between devices with their start and end apart: 25, of which 14 were waited for; matrix products, arithmetic and copies ran while one was open for 1% of the time, Pallas kernels for 18%

profile of v4, /device:TPU:1, one launch (start us, length us, event | category | flops | bytes accessed | tf_op | source)
XLA Modules:
  0.0 281.3 jit_solution(9051870803628040746)
XLA Ops:
  8.7 18.2 %forward.1 = (bf16[512,1280]{1,0:T(8,128)(2,1)}, bf16[512,1280]{1,0:T(8,128)(2,1)}, bf16[512,1280]{1,0:T(8,128)(2,1)}, f32[1280,256]{1,0:T(8,128)}, f32[1280,256...) custom-call(s32[4]{0:T(128)} %pad_add_fusion.place, bf16[512,1280]{1,0:T(8,128)(2,1)} %bitcast.26, ...), custom_call_target="tpu_custom_call" | custom-call | flops 12000000000 | bytes 24000000 | tf_op jit(solution)/shard_map/forward/pallas_call | solution.py:100
  27.0 3.4 %collective-permute-start.2 = (f32[5,4,1024]{2,1,0:T(4,128)}, f32[5,4,1024]{2,1,0:T(4,128)S(1)}, u32[]{:S(2)}, u32[]{:S(2)}) collective-permute-start(f32[5,4,1024]{2,1,0:T(4,128)} %get-tuple-element.73.s0), channel_id=1, source_target_pairs={{0,96},{8,104},{16,112},{24,120},{32,0},{40,8},{48,16},{56,24},{64... | collective-permute-start | bytes 245768 | tf_op jit(solution)/shard_map/ppermute | solution.py:31
  32.1 4.5 %reorder.1.nt = bf16[1280,512]{1,0:T(8,128)(2,1)} custom-call(s32[1,1280]{1,0:T(1,128)} %reshape.18.order, bf16[512,1280]{1,0:T(8,128)(2,1)} %get-tuple-element.53.normed), custom_call_target="tpu_custom_call" | custom-call | flops 1677721600 | bytes 3000000 | tf_op jit(solution)/shard_map/reorder/pallas_call | solution.py:157
  37.5 1.7 merge.1.s0
  39.2 3.8 %collective-permute-start.5 = (f32[5,4,1024]{2,1,0:T(4,128)}, f32[5,4,1024]{2,1,0:T(4,128)S(1)}, u32[]{:S(2)}, u32[]{:S(2)}) collective-permute-start(f32[5,4,1024]{2,1,0:T(4,128)} %merge.1.s0), channel_id=1, source_target_pairs={{0,24},{8,0},{16,8},{24,16},{32,56},{40,32},{48,40},{56,48},{64,88... | collective-permute-start | bytes 245768 | tf_op jit(solution)/shard_map/ppermute | solution.py:33
  49.3 1.7 finish.1.fin
  51.0 21.5 %backward.1 = (f32[1280,2560]{1,0:T(8,128)}, f32[2,64,8,1280]{3,2,1,0:T(8,128)}) custom-call(bf16[1280,512]{1,0:T(8,128)(2,1)} %reorder.1.nt, bf16[512,1280]{1,0:T(8,128)(2,1)} %get-tuple-element.58.keys, bf16[512,1280]{1,0:T(8,128)(2,1)} %get-tuple-element.59.vals, bf16[1024,1280]{1,0:T(8,128)(2,1)} %q.3, bf16[1024,1280]{1,0:T(8,128)(2,1)} %bitcast.25, ...), custom_call_target="tpu_custom_call" | custom-call | flops 20000000000 | bytes 30000000 | tf_op jit(solution)/shard_map/backward/pallas_call | solution.py:196
  72.5 12.4 %all_to_all.15 = f32[2,64,8,1280]{3,2,1,0:T(8,128)S(1)} all-to-all(f32[2,64,8,1280]{3,2,1,0:T(8,128)} %get-tuple-element.64), channel_id=1, replica_groups={{0,1},{2,3},{4,5},{6,7},{8,9},{10,11},{12,13},{14,15},{16,17},{18,19},{..., dimensions={0} | all-to-all | bytes 10485760 | tf_op jit(solution)/shard_map/all_to_all | solution.py:346
  84.9 1.8 fusion
  86.7 14.8 %collective-permute-done.7.n2 = f32[1280,256]{1,0:T(8,128)} collective-permute-done((f32[1280,256]{1,0:T(8,128)S(1)}, f32[1280,256]{1,0:T(8,128)}, u32[]{:S(2)}, u32[]{:S(2)}) %collective-permute-start.7) | collective-permute-done | bytes 1310752 | tf_op jit(solution)/shard_map/ppermute | solution.py:31
  101.4 1.8 collective-permute-done.8.n3
  103.2 10.4 %all-to-all-start.1 = ((f32[64,8,1280]{2,1,0:T(8,128)}), f32[64,8,1280]{2,1,0:T(8,128)S(1)}, u32[]{:S(2)}, u32[]{:S(2)}) async-start(f32[64,8,1280]{2,1,0:T(8,128)} %fusion), calls=%async_computation.1 | async-start | bytes 5242880 | tf_op jit(solution)/shard_map/all_to_all | solution.py:297
  113.7 4.6 %numer_x.1 = (f32[640,128]{1,0:T(8,128)}, f32[640,128]{1,0:T(8,128)}, f32[640,128]{1,0:T(8,128)}, f32[640,128]{1,0:T(8,128)}) custom-call(s32[4]{0:T(128)} %pad_add_fusion.place, f32[1280,256]{1,0:T(8,128)} %get-tuple-element.69.n0, f32[1280,256]{1,0:T(8,128)} %collective-permute-done.6.n1, f32[1280,256]{1,0:T(8,128)} %collective-permute-done.7.n2, ...), custom_call_target="tpu_custom_call" | custom-call | flops 1000000 | bytes 7000000 | tf_op jit(solution)/shard_map/numer_x/pallas_call | solution.py:139
  119.7 2.6 collective-permute-start.10
  123.4 30.0 %collective-permute-done.9.z1 = f32[640,128]{1,0:T(8,128)S(1)} collective-permute-done((f32[640,128]{1,0:T(8,128)}, f32[640,128]{1,0:T(8,128)S(1)}, u32[]{:S(2)}, u32[]{:S(2)}) %collective-permute-start.9) | collective-permute-done | bytes 327712 | tf_op jit(solution)/shard_map/ppermute | solution.py:33
  153.4 6.8 %collective-permute-done.10.z2 = f32[640,128]{1,0:T(8,128)S(1)} collective-permute-done((f32[640,128]{1,0:T(8,128)}, f32[640,128]{1,0:T(8,128)S(1)}, u32[]{:S(2)}, u32[]{:S(2)}) %collective-permute-start.10) | collective-permute-done | bytes 327712 | tf_op jit(solution)/shard_map/ppermute | solution.py:33
  161.5 2.2 numer_z.1
  165.2 4.3 %query_sum.1 = f32[16,8,1280]{2,1,0:T(8,128)} custom-call(f32[64,8,1280]{2,1,0:T(8,128)} %copy-done), custom_call_target="tpu_custom_call" | custom-call | flops 1000000 | bytes 4000000 | tf_op jit(solution)/shard_map/query_sum/pallas_call | solution.py:264
  169.5 20.4 %all_to_all.16 = f32[16,8,1280]{2,1,0:T(8,128)S(1)} all-to-all(f32[16,8,1280]{2,1,0:T(8,128)} %query_sum.1), channel_id=1, replica_groups={{0,2,4,6,8,10,12,14,16,18,20,22,24,26,28,30},{1,3,5,7,9,11,13,15,17,19,..., dimensions={0} | all-to-all | bytes 1310720 | tf_op jit(solution)/shard_map/all_to_all | solution.py:351
  189.9 24.5 %reduce-scatter.2.cloned.1.call-done.rows = f32[160,2560]{1,0:T(8,128)} async-done(((f32[1280,2560]{1,0:T(8,128)}), f32[160,2560]{1,0:T(8,128)}) %reduce-scatter.2.cloned.1.call-update) | async-done | bytes 1638416 | tf_op jit(solution)/shard_map/reduce_scatter | solution.py:350
  214.5 2.7 second.1
  217.8 2.8 %collective-permute-start.17 = (f32[128,1280]{1,0:T(8,128)S(1)}, f32[128,1280]{1,0:T(8,128)S(1)}, u32[]{:S(2)}, u32[]{:S(2)}) collective-permute-start(f32[128,1280]{1,0:T(8,128)S(1)} %bitcast.16), channel_id=1, source_target_pairs={{0,96},{8,104},{16,112},{24,120},{32,0},{40,8},{48,16},{56,24},{64... | collective-permute-start | bytes 1966088 | tf_op jit(solution)/shard_map/ppermute | solution.py:31
  221.9 2.0 collective-permute-start.13
  223.9 9.6 %collective-permute-done.12.a1 = f32[40,2560]{1,0:T(8,128)S(1)} collective-permute-done((f32[40,2560]{1,0:T(8,128)}, f32[40,2560]{1,0:T(8,128)S(1)}, u32[]{:S(2)}, u32[]{:S(2)}) %collective-permute-start.12) | collective-permute-done | bytes 409632 | tf_op jit(solution)/shard_map/ppermute | solution.py:33
  234.0 8.4 %collective-permute-done.13.a2 = f32[40,2560]{1,0:T(8,128)S(1)} collective-permute-done((f32[40,2560]{1,0:T(8,128)}, f32[40,2560]{1,0:T(8,128)S(1)}, u32[]{:S(2)}, u32[]{:S(2)}) %collective-permute-start.13) | collective-permute-done | bytes 409632 | tf_op jit(solution)/shard_map/ppermute | solution.py:33
  243.4 2.3 third.1
  245.6 7.1 %collective-permute-done.15 = f32[128,1280]{1,0:T(8,128)S(1)} collective-permute-done((f32[128,1280]{1,0:T(8,128)S(1)}, f32[128,1280]{1,0:T(8,128)S(1)}, u32[]{:S(2)}, u32[]{:S(2)}) %collective-permute-start.15) | collective-permute-done | bytes 655392 | tf_op jit(solution)/shard_map/ppermute | solution.py:31
  254.4 1.8 collective-permute-start.19
  256.8 4.6 %round.1 = bf16[1024,1280]{1,0:T(8,128)(2,1)} custom-call(f32[16,128,640]{2,1,0:T(8,128)} %bitcast.15), custom_call_target="tpu_custom_call" | custom-call | flops 1000000 | bytes 8000000 | tf_op jit(solution)/shard_map/round/pallas_call | solution.py:372
  261.3 2.9 %collective-permute-done.19.a2 = f32[16,2560]{1,0:T(8,128)S(1)} collective-permute-done((f32[16,2560]{1,0:T(8,128)}, f32[16,2560]{1,0:T(8,128)S(1)}, u32[]{:S(2)}, u32[]{:S(2)}) %collective-permute-start.19) | collective-permute-done | bytes 163872 | tf_op jit(solution)/shard_map/ppermute | solution.py:31
  265.5 1.8 last.1
  267.4 6.5 %place_query.1 = f32[1024,1280]{1,0:T(8,128)} custom-call(s32[4]{0:T(128)} %pad_add_fusion.place, f32[4,128,1280]{2,1,0:T(8,128)} %copy-done.1, f32[4,128,1280]{2,1,0:T(8,128)} %collective-permute-done.21.other), custom_call_target="tpu_custom_call" | custom-call | flops 1000000 | bytes 10000000 | tf_op jit(solution)/shard_map/place_query/pallas_call | solution.py:284
  (92 shorter events, 21.9 us)
Async XLA Ops:
  8.0 206.5 %reduce-scatter.2.cloned.1.call-start = ((), (), s32[]{:S(2)}) async-start(), calls=%async_computation.4 | async-start | bytes 14745600 | tf_op jit(solution)/shard_map/reduce_scatter | solution.py:350
  8.7 22.8 %copy-start.17 = (s32[1280]{0:T(1024)S(1)}, s32[1280]{0:T(1024)}, u32[]{:S(2)}) copy-start(s32[1280]{0:T(1024)} %constant.82.clone) | copy-start | bytes 15364
  8.7 22.8 %copy-start.18 = (s32[1280]{0:T(1024)S(1)}, s32[1280]{0:T(1024)}, u32[]{:S(2)}) copy-start(s32[1280]{0:T(1024)} %constant.81.clone) | copy-start | bytes 15364
  8.7 22.8 %copy-start.19 = (s32[1280]{0:T(1024)S(1)}, s32[1280]{0:T(1024)}, u32[]{:S(2)}) copy-start(s32[1280]{0:T(1024)} %constant.80.clone) | copy-start | bytes 15364
  8.7 22.8 %copy-start.20 = (s32[1280]{0:T(1024)S(1)}, s32[1280]{0:T(1024)}, u32[]{:S(2)}) copy-start(s32[1280]{0:T(1024)} %constant.79.clone) | copy-start | bytes 15364
  8.7 22.8 %copy-start.21 = (s32[1280]{0:T(1024)S(1)}, s32[1280]{0:T(1024)}, u32[]{:S(2)}) copy-start(s32[1280]{0:T(1024)} %constant.78.clone) | copy-start | bytes 15364
  27.0 9.7 %collective-permute-start.2 = (f32[5,4,1024]{2,1,0:T(4,128)}, f32[5,4,1024]{2,1,0:T(4,128)S(1)}, u32[]{:S(2)}, u32[]{:S(2)}) collective-permute-start(f32[5,4,1024]{2,1,0:T(4,128)} %get-tuple-element.73.s0), channel_id=1, source_target_pairs={{0,96},{8,104},{16,112},{24,120},{32,0},{40,8},{48,16},{56,24},{64... | collective-permute-start | bytes 245768 | tf_op jit(solution)/shard_map/ppermute | solution.py:31
  30.3 6.3 %collective-permute-start.1 = (f32[5,4,1024]{2,1,0:T(4,128)}, f32[5,4,1024]{2,1,0:T(4,128)S(1)}, u32[]{:S(2)}, u32[]{:S(2)}) collective-permute-start(f32[5,4,1024]{2,1,0:T(4,128)} %get-tuple-element.73.s0), channel_id=1, source_target_pairs={{0,64},{8,72},{16,80},{24,88},{32,96},{40,104},{48,112},{56,120},{... | collective-permute-start | bytes 245768 | tf_op jit(solution)/shard_map/ppermute | solution.py:31
  30.9 6.0 %collective-permute-start = (f32[5,4,1024]{2,1,0:T(4,128)}, f32[5,4,1024]{2,1,0:T(4,128)S(1)}, u32[]{:S(2)}, u32[]{:S(2)}) collective-permute-start(f32[5,4,1024]{2,1,0:T(4,128)} %get-tuple-element.73.s0), channel_id=1, source_target_pairs={{0,32},{8,40},{16,48},{24,56},{32,64},{40,72},{48,80},{56,88},{64,... | collective-permute-start | bytes 245768 | tf_op jit(solution)/shard_map/ppermute | solution.py:31
  32.1 13.0 %copy-start.23 = (f32[1280,256]{1,0:T(8,128)S(1)}, f32[1280,256]{1,0:T(8,128)}, u32[]{:S(2)}) copy-start(f32[1280,256]{1,0:T(8,128)} %get-tuple-element.67) | copy-start | bytes 3932164
  32.1 14.7 %copy-start.22 = (f32[1280,256]{1,0:T(8,128)S(1)}, f32[1280,256]{1,0:T(8,128)}, u32[]{:S(2)}) copy-start(f32[1280,256]{1,0:T(8,128)} %get-tuple-element.68) | copy-start | bytes 3932164
  39.2 7.6 %collective-permute-start.5 = (f32[5,4,1024]{2,1,0:T(4,128)}, f32[5,4,1024]{2,1,0:T(4,128)S(1)}, u32[]{:S(2)}, u32[]{:S(2)}) collective-permute-start(f32[5,4,1024]{2,1,0:T(4,128)} %merge.1.s0), channel_id=1, source_target_pairs={{0,24},{8,0},{16,8},{24,16},{32,56},{40,32},{48,40},{56,48},{64,88... | collective-permute-start | bytes 245768 | tf_op jit(solution)/shard_map/ppermute | solution.py:33
  42.9 5.1 %collective-permute-start.4 = (f32[5,4,1024]{2,1,0:T(4,128)}, f32[5,4,1024]{2,1,0:T(4,128)S(1)}, u32[]{:S(2)}, u32[]{:S(2)}) collective-permute-start(f32[5,4,1024]{2,1,0:T(4,128)} %merge.1.s0), channel_id=1, source_target_pairs={{0,16},{8,24},{16,0},{24,8},{32,48},{40,56},{48,32},{56,40},{64,80... | collective-permute-start | bytes 245768 | tf_op jit(solution)/shard_map/ppermute | solution.py:33
  42.9 5.6 %collective-permute-start.3 = (f32[5,4,1024]{2,1,0:T(4,128)}, f32[5,4,1024]{2,1,0:T(4,128)S(1)}, u32[]{:S(2)}, u32[]{:S(2)}) collective-permute-start(f32[5,4,1024]{2,1,0:T(4,128)} %merge.1.s0), channel_id=1, source_target_pairs={{0,8},{8,16},{16,24},{24,0},{32,40},{40,48},{48,56},{56,32},{64,72... | collective-permute-start | bytes 245768 | tf_op jit(solution)/shard_map/ppermute | solution.py:33
  43.6 43.0 %collective-permute-start.6 = (f32[1280,256]{1,0:T(8,128)S(1)}, f32[1280,256]{1,0:T(8,128)}, u32[]{:S(2)}, u32[]{:S(2)}) collective-permute-start(f32[1280,256]{1,0:T(8,128)S(1)} %copy-done.24), channel_id=1, source_target_pairs={{0,32},{8,40},{16,48},{24,56},{32,64},{40,72},{48,80},{56,88},{64,... | collective-permute-start | bytes 3932168 | tf_op jit(solution)/shard_map/ppermute | solution.py:31
  45.1 56.4 %collective-permute-start.7 = (f32[1280,256]{1,0:T(8,128)S(1)}, f32[1280,256]{1,0:T(8,128)}, u32[]{:S(2)}, u32[]{:S(2)}) collective-permute-start(f32[1280,256]{1,0:T(8,128)S(1)} %copy-done.23), channel_id=1, source_target_pairs={{0,64},{8,72},{16,80},{24,88},{32,96},{40,104},{48,112},{56,120},{... | collective-permute-start | bytes 3932168 | tf_op jit(solution)/shard_map/ppermute | solution.py:31
  46.8 56.4 %collective-permute-start.8 = (f32[1280,256]{1,0:T(8,128)S(1)}, f32[1280,256]{1,0:T(8,128)}, u32[]{:S(2)}, u32[]{:S(2)}) collective-permute-start(f32[1280,256]{1,0:T(8,128)S(1)} %copy-done.22), channel_id=1, source_target_pairs={{0,96},{8,104},{16,112},{24,120},{32,0},{40,8},{48,16},{56,24},{64... | collective-permute-start | bytes 3932168 | tf_op jit(solution)/shard_map/ppermute | solution.py:31
  103.2 60.5 %all-to-all-start.1 = ((f32[64,8,1280]{2,1,0:T(8,128)}), f32[64,8,1280]{2,1,0:T(8,128)S(1)}, u32[]{:S(2)}, u32[]{:S(2)}) async-start(f32[64,8,1280]{2,1,0:T(8,128)} %fusion), calls=%async_computation.1 | async-start | bytes 5242880 | tf_op jit(solution)/shard_map/all_to_all | solution.py:297
  113.7 143.1 %all-gather.3.cloned.1.call-start = ((), (), s32[]{:S(2)}) async-start(), calls=%async_computation.5 | async-start | bytes 5570560 | tf_op jit(solution)/shard_map/all_gather | solution.py:365
  118.3 35.0 %collective-permute-start.9 = (f32[640,128]{1,0:T(8,128)}, f32[640,128]{1,0:T(8,128)S(1)}, u32[]{:S(2)}, u32[]{:S(2)}) collective-permute-start(f32[640,128]{1,0:T(8,128)} %get-tuple-element.78), channel_id=1, source_target_pairs={{0,8},{8,16},{16,24},{24,0},{32,40},{40,48},{48,56},{56,32},{64,72... | collective-permute-start | bytes 983048 | tf_op jit(solution)/shard_map/ppermute | solution.py:33
  119.7 40.4 %collective-permute-start.10 = (f32[640,128]{1,0:T(8,128)}, f32[640,128]{1,0:T(8,128)S(1)}, u32[]{:S(2)}, u32[]{:S(2)}) collective-permute-start(f32[640,128]{1,0:T(8,128)} %get-tuple-element.79), channel_id=1, source_target_pairs={{0,16},{8,24},{16,0},{24,8},{32,48},{40,56},{48,32},{56,40},{64,80... | collective-permute-start | bytes 983048 | tf_op jit(solution)/shard_map/ppermute | solution.py:33
  122.3 38.5 %collective-permute-start.11 = (f32[640,128]{1,0:T(8,128)}, f32[640,128]{1,0:T(8,128)S(1)}, u32[]{:S(2)}, u32[]{:S(2)}) collective-permute-start(f32[640,128]{1,0:T(8,128)} %get-tuple-element.80), channel_id=1, source_target_pairs={{0,24},{8,0},{16,8},{24,16},{32,56},{40,32},{48,40},{56,48},{64,88... | collective-permute-start | bytes 983048 | tf_op jit(solution)/shard_map/ppermute | solution.py:33
  217.1 16.4 %collective-permute-start.12 = (f32[40,2560]{1,0:T(8,128)}, f32[40,2560]{1,0:T(8,128)S(1)}, u32[]{:S(2)}, u32[]{:S(2)}) collective-permute-start(f32[40,2560]{1,0:T(8,128)} %get-tuple-element.86), channel_id=1, source_target_pairs={{0,8},{8,16},{16,24},{24,0},{32,40},{40,48},{48,56},{56,32},{64,72... | collective-permute-start | bytes 1228808 | tf_op jit(solution)/shard_map/ppermute | solution.py:33
  217.8 27.8 %collective-permute-start.17 = (f32[128,1280]{1,0:T(8,128)S(1)}, f32[128,1280]{1,0:T(8,128)S(1)}, u32[]{:S(2)}, u32[]{:S(2)}) collective-permute-start(f32[128,1280]{1,0:T(8,128)S(1)} %bitcast.16), channel_id=1, source_target_pairs={{0,96},{8,104},{16,112},{24,120},{32,0},{40,8},{48,16},{56,24},{64... | collective-permute-start | bytes 1966088 | tf_op jit(solution)/shard_map/ppermute | solution.py:31
  220.7 25.0 %collective-permute-start.16 = (f32[128,1280]{1,0:T(8,128)S(1)}, f32[128,1280]{1,0:T(8,128)S(1)}, u32[]{:S(2)}, u32[]{:S(2)}) collective-permute-start(f32[128,1280]{1,0:T(8,128)S(1)} %bitcast.17), channel_id=1, source_target_pairs={{0,64},{8,72},{16,80},{24,88},{32,96},{40,104},{48,112},{56,120},{... | collective-permute-start | bytes 1966088 | tf_op jit(solution)/shard_map/ppermute | solution.py:31
  221.0 31.7 %collective-permute-start.15 = (f32[128,1280]{1,0:T(8,128)S(1)}, f32[128,1280]{1,0:T(8,128)S(1)}, u32[]{:S(2)}, u32[]{:S(2)}) collective-permute-start(f32[128,1280]{1,0:T(8,128)S(1)} %bitcast.18), channel_id=1, source_target_pairs={{0,32},{8,40},{16,48},{24,56},{32,64},{40,72},{48,80},{56,88},{64,... | collective-permute-start | bytes 1966088 | tf_op jit(solution)/shard_map/ppermute | solution.py:31
  221.9 20.5 %collective-permute-start.13 = (f32[40,2560]{1,0:T(8,128)}, f32[40,2560]{1,0:T(8,128)S(1)}, u32[]{:S(2)}, u32[]{:S(2)}) collective-permute-start(f32[40,2560]{1,0:T(8,128)} %get-tuple-element.87), channel_id=1, source_target_pairs={{0,16},{8,24},{16,0},{24,8},{32,48},{40,56},{48,32},{56,40},{64,80... | collective-permute-start | bytes 1228808 | tf_op jit(solution)/shard_map/ppermute | solution.py:33
  233.5 8.9 %collective-permute-start.14 = (f32[40,2560]{1,0:T(8,128)}, f32[40,2560]{1,0:T(8,128)S(1)}, u32[]{:S(2)}, u32[]{:S(2)}) collective-permute-start(f32[40,2560]{1,0:T(8,128)} %get-tuple-element.88), channel_id=1, source_target_pairs={{0,24},{8,0},{16,8},{24,16},{32,56},{40,32},{48,40},{56,48},{64,88... | collective-permute-start | bytes 1228808 | tf_op jit(solution)/shard_map/ppermute | solution.py:33
  253.0 14.4 %collective-permute-start.21 = (f32[4,128,1280]{2,1,0:T(8,128)S(1)}, f32[4,128,1280]{2,1,0:T(8,128)}, u32[]{:S(2)}, u32[]{:S(2)}) collective-permute-start(f32[4,128,1280]{2,1,0:T(8,128)S(1)} %pad_maximum_fusion.own), channel_id=1, source_target_pairs={{0,1},{1,0},{2,3},{3,2},{4,5},{5,4},{6,7},{7,6},{8,9},{9,8},{10,11... | collective-permute-start | bytes 7864328 | tf_op jit(solution)/shard_map/ppermute | solution.py:36
  253.8 7.5 %collective-permute-start.18 = (f32[16,2560]{1,0:T(8,128)}, f32[16,2560]{1,0:T(8,128)S(1)}, u32[]{:S(2)}, u32[]{:S(2)}) collective-permute-start(f32[16,2560]{1,0:T(8,128)} %get-tuple-element.94), channel_id=1, source_target_pairs={{0,32},{8,40},{16,48},{24,56},{32,64},{40,72},{48,80},{56,88},{64,... | collective-permute-start | bytes 491528 | tf_op jit(solution)/shard_map/ppermute | solution.py:31
  254.4 9.8 %collective-permute-start.19 = (f32[16,2560]{1,0:T(8,128)}, f32[16,2560]{1,0:T(8,128)S(1)}, u32[]{:S(2)}, u32[]{:S(2)}) collective-permute-start(f32[16,2560]{1,0:T(8,128)} %get-tuple-element.95), channel_id=1, source_target_pairs={{0,64},{8,72},{16,80},{24,88},{32,96},{40,104},{48,112},{56,120},{... | collective-permute-start | bytes 491528 | tf_op jit(solution)/shard_map/ppermute | solution.py:31
  256.2 8.6 %collective-permute-start.20 = (f32[16,2560]{1,0:T(8,128)S(1)}, f32[16,2560]{1,0:T(8,128)S(1)}, u32[]{:S(2)}, u32[]{:S(2)}) collective-permute-start(f32[16,2560]{1,0:T(8,128)S(1)} %copy-done.25), channel_id=1, source_target_pairs={{0,96},{8,104},{16,112},{24,120},{32,0},{40,8},{48,16},{56,24},{64... | collective-permute-start | bytes 491528 | tf_op jit(solution)/shard_map/ppermute | solution.py:31
  (19 other events, 54.1 us)
Sparse Core Ops, SparseCore 0:
  103.3 111.0 reduce-scatter.1
Sparse Core Ops, SparseCore 1:
  163.8 64.6 all-gather.2

commit v5 on v4

--- a/solution.py
+++ b/solution.py
@@ -18,7 +18,7 @@
 SCALE2 = SCALE * 1.4426950408889634
 VMEM_LIMIT = 56 * 1024 * 1024
 PAIRS = H // 2
-COST = 1.0
+COST = 0.02
 PAIR_GROUPS = [[a * 2, a * 2 + 1] for a in range(4)]
 PLANE_GROUPS = [[a * 32 + b * 2 + c for b in range(16)] for a in range(4) for c in range(2)]
 CORE_GROUPS = [[a * 2 + b for a in range(64)] for b in range(2)]
@@ -261,36 +261,33 @@
 
 
 def query_sum(parts):
-    return pl.pallas_call(
-        query_sum_kernel,
-        grid=(PAIRS,),
-        in_specs=[pl.BlockSpec((64, 8, PAIR), lambda i: (0, 0, i))],
-        out_specs=pl.BlockSpec((16, 8, PAIR), lambda i: (0, 0, i)),
-        out_shape=jax.ShapeDtypeStruct((16, 8, D), F32),
-        compiler_params=params(),
-        cost_estimate=cost(1e6, 4e6),
-        name="query_sum",
-    )(parts)
-
-
-def place_query_kernel(place, own, other, out):
-    for k in range(4):
-        block = lax.rem(place[0] + 4 - k, 4) * 128
-        out[pl.ds(pl.multiple_of(place[3] * 512 + block, 128), 128), :] = own[k]
-        out[pl.ds(pl.multiple_of((1 - place[3]) * 512 + block, 128), 128), :] = other[k]
-
-
-def place_query(place, own, other):
+    return simple(query_sum_kernel, [parts], (16, 8, D), "query_sum")
+
+
+def place_query_kernel(place, rows, *refs):
+    refs[-1][...] = rows[0]
+
+
+def place_query(place, rows, before=None):
+    def spot(k, p):
+        half = p[3] if before is None else 1 - p[3]
+        return half * 4 + lax.rem(p[0] + 4 - k, 4), 0
+
+    others = [] if before is None else [before]
     return pl.pallas_call(
         place_query_kernel,
-        grid=(PAIRS,),
-        in_specs=[SMEM] + [pl.BlockSpec((4, 128, PAIR), lambda i: (0, 0, i))] * 2,
-        out_specs=pair_cols(L),
+        grid_spec=pltpu.PrefetchScalarGridSpec(
+            num_scalar_prefetch=1,
+            grid=(4,),
+            in_specs=[pl.BlockSpec((1, 128, D), lambda k, p: (k, 0, 0))] + [pl.BlockSpec(memory_space=pl.ANY)] * len(others),
+            out_specs=pl.BlockSpec((128, D), spot),
+        ),
         out_shape=jax.ShapeDtypeStruct((L, D), F32),
-        compiler_params=params(),
-        cost_estimate=cost(1e6, 1e7),
+        input_output_aliases={} if before is None else {2: 0},
+        compiler_params=params(),
+        cost_estimate=cost(1e6, 6e6),
         name="place_query",
-    )(place, own, other)
+    )(place, rows, *others)
 
 
 def spread(blocks):
@@ -363,10 +360,11 @@
     )
     share = simple(numer_z_kernel, exchange(zs, "z"), (128, 640), "numer_z")
     gathered = lax.all_gather(after(q_parts, share), "seq")
-    rows = after(own_query, rows)
+    right, left = shift(own_query, "x", 1), shift(own_query, "x", 3)
+    rows = after((right, left), rows)
     rows = exchange(simple(second_kernel, [rows], [(40, 2 * D)] * 4, "second"), "z")
     rows = simple(third_kernel, rows, [(16, 2 * D)] * 4, "third")
-    own_query = jnp.stack(after(rows[0], exchange([own_query] * 4, "x")))
+    own_query = jnp.stack([own_query, right, after(rows[0], shift(own_query, "x", 2)), left])
     rows = exchange(rows, "x")
 
     attended = pl.pallas_call(
@@ -379,8 +377,9 @@
         cost_estimate=cost(1e6, 8e6),
         name="round",
     )(gathered)
-    other_query = after((attended, rows), shift(own_query, "c", 1))
-    query_grad = place_query(place, own_query, other_query)
+    half_placed = place_query(place, own_query)
+    other_query = after((attended, rows, half_placed), shift(own_query, "c", 1))
+    query_grad = place_query(place, other_query, half_placed)
     key_rows, value_rows = simple(last_kernel, rows, [(10, D)] * 2, "last")
     return attended.reshape(1, L, D), query_grad, key_rows, value_rows
 

time: 282 us -> 277 us (0.982)
  waiting for transfers between devices: 108 us -> 91.7 us
  starting transfers between devices: 39.6 us -> 47.9 us
    reduce_scatter x1, waiting for transfers between devices: 24.5 us -> 1.61 us  [on_device(): lax.psum_scatter(after(numer, terms), 'dp', scatter_dimension=0, tiled=True)]
    ppermute x9, waiting for transfers between devices: 56.4 us -> 66.2 us  [shift(): lax.ppermute(array, 'seq', [(a * 4 + b, a * 4 + (b + step) % 4) for a in...]
    ppermute x1, starting transfers between devices: 0.81 us -> 5.82 us  [shift(): lax.ppermute(array, 'dp', [(a * 2 + b, a * 2 + 1 - b) for a in range(4) f...]
    ppermute x12, waiting for transfers between devices: 27.2 us -> 23.9 us  [shift(): lax.ppermute(array, 'seq', [(a * 4 + b, (a + step) % 4 * 4 + b) for a in...]
    pallas_call x7 -> x8, Pallas kernels: 17 us -> 19.8 us  [simple(): pl.pallas_call(kernel, in_specs=([] if scalars is None else [SMEM]) + spe...]
    unnamed x52 -> x56, local copies, waits for them, and re-layouts: 5.32 us -> 5.93 us
  transfers between devices with their start and end apart: 25 -> 25, of which waited for: 14 -> 14; matrix products, arithmetic and copies ran while one was open for 1% -> 2% of each run, Pallas kernels for 18% -> 20%
where the time goes in v5:
time: 277 us; the launch traced here: 276 us
  waiting for transfers between devices  91.7 us (33%)
  Pallas kernels  77.8 us (28%)
  starting transfers between devices  47.9 us (17%)
  blocking collectives  32.1 us (12%)
  between operations  15.7 us (6%)
  local copies, waits for them, and re-layouts  6.53 us (2%)
  other arithmetic  4.17 us (2%)
    ppermute x9, waiting for transfers between devices, shift(): lax.ppermute(array, 'seq', [(a * 4 + b, a * 4 + (b + step) % 4) for a in...  66.2 us
    ppermute x12, waiting for transfers between devices, shift(): lax.ppermute(array, 'seq', [(a * 4 + b, (a + step) % 4 * 4 + b) for a in...  23.9 us
    pallas_call x1, Pallas kernels, backward(): pl.pallas_call(backward_kernel, grid=(PAIRS,), in_specs=[full((D, T)), pa...  21.4 us
    all_to_all x1, blocking collectives, on_device(): lax.all_to_all(query_sum(q_parts), ('seq', 'dp'), split_axis=0, concat_ax...  20.4 us
    pallas_call x8, Pallas kernels, simple(): pl.pallas_call(kernel, in_specs=([] if scalars is None else [SMEM]) + spe...  19.8 us
    pallas_call x1, Pallas kernels, forward(): pl.pallas_call(forward_kernel, grid=(PAIRS,), in_specs=[SMEM, full((T, D)...  18.3 us
    ppermute x12, starting transfers between devices, shift(): lax.ppermute(array, 'seq', [(a * 4 + b, (a + step) % 4 * 4 + b) for a in...  15.6 us
    ppermute x9, starting transfers between devices, shift(): lax.ppermute(array, 'seq', [(a * 4 + b, a * 4 + (b + step) % 4) for a in...  14.4 us
  transfers between devices with their start and end apart: 25, of which 14 were waited for; matrix products, arithmetic and copies ran while one was open for 2% of the time, Pallas kernels for 20%

profile of v5, /device:TPU:1, one launch (start us, length us, event | category | flops | bytes accessed | tf_op | source)
XLA Modules:
  0.0 275.8 jit_solution(7555268504635153705)
XLA Ops:
  8.7 18.3 %forward.1 = (bf16[512,1280]{1,0:T(8,128)(2,1)}, bf16[512,1280]{1,0:T(8,128)(2,1)}, bf16[512,1280]{1,0:T(8,128)(2,1)}, f32[1280,256]{1,0:T(8,128)}, f32[1280,256...) custom-call(s32[4]{0:T(128)} %pad_add_fusion.place, bf16[512,1280]{1,0:T(8,128)(2,1)} %bitcast.23, ...), custom_call_target="tpu_custom_call" | custom-call | flops 240000000 | bytes 480000 | tf_op jit(solution)/shard_map/forward/pallas_call | solution.py:100
  27.0 3.4 %collective-permute-start.2 = (f32[5,4,1024]{2,1,0:T(4,128)}, f32[5,4,1024]{2,1,0:T(4,128)S(1)}, u32[]{:S(2)}, u32[]{:S(2)}) collective-permute-start(f32[5,4,1024]{2,1,0:T(4,128)} %get-tuple-element.70.s0), channel_id=1, source_target_pairs={{0,96},{8,104},{16,112},{24,120},{32,0},{40,8},{48,16},{56,24},{64... | collective-permute-start | bytes 245768 | tf_op jit(solution)/shard_map/ppermute | solution.py:31
  32.1 4.4 %reorder.1.nt = bf16[1280,512]{1,0:T(8,128)(2,1)} custom-call(s32[1,1280]{1,0:T(1,128)} %reshape.18.order, bf16[512,1280]{1,0:T(8,128)(2,1)} %get-tuple-element.50.normed), custom_call_target="tpu_custom_call" | custom-call | flops 33554432 | bytes 60000 | tf_op jit(solution)/shard_map/reorder/pallas_call | solution.py:157
  42.4 3.8 %collective-permute-start.5 = (f32[5,4,1024]{2,1,0:T(4,128)}, f32[5,4,1024]{2,1,0:T(4,128)S(1)}, u32[]{:S(2)}, u32[]{:S(2)}) collective-permute-start(f32[5,4,1024]{2,1,0:T(4,128)} %merge.1.s0), channel_id=1, source_target_pairs={{0,24},{8,0},{16,8},{24,16},{32,56},{40,32},{48,40},{56,48},{64,88... | collective-permute-start | bytes 245768 | tf_op jit(solution)/shard_map/ppermute | solution.py:33
  46.2 2.1 collective-permute-done.5.s3
  48.3 2.9 %collective-permute-done.4.s2 = f32[5,4,1024]{2,1,0:T(4,128)S(1)} collective-permute-done((f32[5,4,1024]{2,1,0:T(4,128)}, f32[5,4,1024]{2,1,0:T(4,128)S(1)}, u32[]{:S(2)}, u32[]{:S(2)}) %collective-permute-start.4) | collective-permute-done | bytes 81952 | tf_op jit(solution)/shard_map/ppermute | solution.py:33
  51.2 4.1 %collective-permute-done.3.s1 = f32[5,4,1024]{2,1,0:T(4,128)S(1)} collective-permute-done((f32[5,4,1024]{2,1,0:T(4,128)}, f32[5,4,1024]{2,1,0:T(4,128)S(1)}, u32[]{:S(2)}, u32[]{:S(2)}) %collective-permute-start.3) | collective-permute-done | bytes 81952 | tf_op jit(solution)/shard_map/ppermute | solution.py:33
  57.7 21.4 %backward.1 = (f32[1280,2560]{1,0:T(8,128)}, f32[2,64,8,1280]{3,2,1,0:T(8,128)}) custom-call(bf16[1280,512]{1,0:T(8,128)(2,1)} %reorder.1.nt, bf16[512,1280]{1,0:T(8,128)(2,1)} %get-tuple-element.55.keys, bf16[512,1280]{1,0:T(8,128)(2,1)} %get-tuple-element.56.vals, bf16[1024,1280]{1,0:T(8,128)(2,1)} %q.3, bf16[1024,1280]{1,0:T(8,128)(2,1)} %bitcast.16, ...), custom_call_target="tpu_custom_call" | custom-call | flops 400000000 | bytes 600000 | tf_op jit(solution)/shard_map/backward/pallas_call | solution.py:196
  79.1 11.7 %all_to_all.15 = f32[2,64,8,1280]{3,2,1,0:T(8,128)S(1)} all-to-all(f32[2,64,8,1280]{3,2,1,0:T(8,128)} %get-tuple-element.61), channel_id=1, replica_groups={{0,1},{2,3},{4,5},{6,7},{8,9},{10,11},{12,13},{14,15},{16,17},{18,19},{..., dimensions={0} | all-to-all | bytes 10485760 | tf_op jit(solution)/shard_map/all_to_all | solution.py:343
  92.6 3.0 %collective-permute-done.7.n2 = f32[1280,256]{1,0:T(8,128)} collective-permute-done((f32[1280,256]{1,0:T(8,128)S(1)}, f32[1280,256]{1,0:T(8,128)}, u32[]{:S(2)}, u32[]{:S(2)}) %collective-permute-start.7) | collective-permute-done | bytes 1310752 | tf_op jit(solution)/shard_map/ppermute | solution.py:31
  96.4 11.9 %all-to-all-start.1 = ((f32[64,8,1280]{2,1,0:T(8,128)}), f32[64,8,1280]{2,1,0:T(8,128)S(1)}, u32[]{:S(2)}, u32[]{:S(2)}) async-start(f32[64,8,1280]{2,1,0:T(8,128)} %fusion), calls=%async_computation.1 | async-start | bytes 5242880 | tf_op jit(solution)/shard_map/all_to_all | solution.py:294
  108.4 4.6 %numer_x.1 = (f32[640,128]{1,0:T(8,128)}, f32[640,128]{1,0:T(8,128)}, f32[640,128]{1,0:T(8,128)}, f32[640,128]{1,0:T(8,128)}) custom-call(s32[4]{0:T(128)} %pad_add_fusion.place, f32[1280,256]{1,0:T(8,128)} %get-tuple-element.66.n0, f32[1280,256]{1,0:T(8,128)} %collective-permute-done.6.n1, f32[1280,256]{1,0:T(8,128)} %collective-permute-done.7.n2, ...), custom_call_target="tpu_custom_call" | custom-call | flops 20000 | bytes 140000 | tf_op jit(solution)/shard_map/numer_x/pallas_call | solution.py:139
  114.4 2.6 collective-permute-start.10
  118.1 30.0 %collective-permute-done.9.z1 = f32[640,128]{1,0:T(8,128)S(1)} collective-permute-done((f32[640,128]{1,0:T(8,128)}, f32[640,128]{1,0:T(8,128)S(1)}, u32[]{:S(2)}, u32[]{:S(2)}) %collective-permute-start.9) | collective-permute-done | bytes 327712 | tf_op jit(solution)/shard_map/ppermute | solution.py:33
  148.0 6.8 %collective-permute-done.10.z2 = f32[640,128]{1,0:T(8,128)S(1)} collective-permute-done((f32[640,128]{1,0:T(8,128)}, f32[640,128]{1,0:T(8,128)S(1)}, u32[]{:S(2)}, u32[]{:S(2)}) %collective-permute-start.10) | collective-permute-done | bytes 327712 | tf_op jit(solution)/shard_map/ppermute | solution.py:33
  156.2 2.2 numer_z.1
  159.9 2.8 %query_sum.1 = f32[16,8,1280]{2,1,0:T(8,128)} custom-call(f32[64,8,1280]{2,1,0:T(8,128)} %copy-done), custom_call_target="tpu_custom_call" | custom-call | flops 20000 | bytes 80000 | tf_op jit(solution)/shard_map/query_sum/pallas_call | solution.py:139
  162.7 20.4 %all_to_all.16 = f32[16,8,1280]{2,1,0:T(8,128)S(1)} all-to-all(f32[16,8,1280]{2,1,0:T(8,128)} %query_sum.1), channel_id=1, replica_groups={{0,2,4,6,8,10,12,14,16,18,20,22,24,26,28,30},{1,3,5,7,9,11,13,15,17,19,..., dimensions={0} | all-to-all | bytes 1310720 | tf_op jit(solution)/shard_map/all_to_all | solution.py:348
  183.1 3.4 %collective-permute-start.13 = (f32[128,1280]{1,0:T(8,128)S(1)}, f32[128,1280]{1,0:T(8,128)S(1)}, u32[]{:S(2)}, u32[]{:S(2)}) collective-permute-start(f32[128,1280]{1,0:T(8,128)S(1)} %bitcast.18), channel_id=1, source_target_pairs={{0,96},{8,104},{16,112},{24,120},{32,0},{40,8},{48,16},{56,24},{64... | collective-permute-start | bytes 1966088 | tf_op jit(solution)/shard_map/ppermute | solution.py:31
  187.7 16.2 %collective-permute-done.13 = f32[128,1280]{1,0:T(8,128)S(1)} collective-permute-done((f32[128,1280]{1,0:T(8,128)S(1)}, f32[128,1280]{1,0:T(8,128)S(1)}, u32[]{:S(2)}, u32[]{:S(2)}) %collective-permute-start.13) | collective-permute-done | bytes 655392 | tf_op jit(solution)/shard_map/ppermute | solution.py:31
  203.9 3.6 %collective-permute-done.12 = f32[128,1280]{1,0:T(8,128)S(1)} collective-permute-done((f32[128,1280]{1,0:T(8,128)S(1)}, f32[128,1280]{1,0:T(8,128)S(1)}, u32[]{:S(2)}, u32[]{:S(2)}) %collective-permute-start.12) | collective-permute-done | bytes 655392 | tf_op jit(solution)/shard_map/ppermute | solution.py:31
  209.1 2.6 second.1
  212.5 2.8 %collective-permute-start.15 = (f32[40,2560]{1,0:T(8,128)}, f32[40,2560]{1,0:T(8,128)S(1)}, u32[]{:S(2)}, u32[]{:S(2)}) collective-permute-start(f32[40,2560]{1,0:T(8,128)} %get-tuple-element.84), channel_id=1, source_target_pairs={{0,16},{8,24},{16,0},{24,8},{32,48},{40,56},{48,32},{56,40},{64,80... | collective-permute-start | bytes 1228808 | tf_op jit(solution)/shard_map/ppermute | solution.py:33
  215.3 2.1 collective-permute-start.16
  217.4 5.6 %collective-permute-done.14.a1 = f32[40,2560]{1,0:T(8,128)S(1)} collective-permute-done((f32[40,2560]{1,0:T(8,128)}, f32[40,2560]{1,0:T(8,128)S(1)}, u32[]{:S(2)}, u32[]{:S(2)}) %collective-permute-start.14) | collective-permute-done | bytes 409632 | tf_op jit(solution)/shard_map/ppermute | solution.py:33
  222.9 14.0 %collective-permute-done.15.a2 = f32[40,2560]{1,0:T(8,128)S(1)} collective-permute-done((f32[40,2560]{1,0:T(8,128)}, f32[40,2560]{1,0:T(8,128)S(1)}, u32[]{:S(2)}, u32[]{:S(2)}) %collective-permute-start.15) | collective-permute-done | bytes 409632 | tf_op jit(solution)/shard_map/ppermute | solution.py:33
  237.9 2.3 third.1
  242.8 5.8 %collective-permute-start.21 = (f32[4,128,1280]{2,1,0:T(8,128)S(1)}, f32[4,128,1280]{2,1,0:T(8,128)}, u32[]{:S(2)}, u32[]{:S(2)}) collective-permute-start(f32[4,128,1280]{2,1,0:T(8,128)S(1)} %pad_maximum_fusion.rows), channel_id=1, source_target_pairs={{0,1},{1,0},{2,3},{3,2},{4,5},{5,4},{6,7},{7,6},{8,9},{9,8},{10,11... | collective-permute-start | bytes 7864328 | tf_op jit(solution)/shard_map/ppermute | solution.py:36
  248.6 2.5 collective-permute-start.18
  251.3 4.6 %round.1 = bf16[1024,1280]{1,0:T(8,128)(2,1)} custom-call(f32[16,128,640]{2,1,0:T(8,128)} %bitcast.17), custom_call_target="tpu_custom_call" | custom-call | flops 20000 | bytes 160000 | tf_op jit(solution)/shard_map/round/pallas_call | solution.py:370
  255.8 4.7 %place_query.2.refs_0_ = f32[1024,1280]{1,0:T(8,128)} custom-call(s32[4]{0:T(128)} %pad_add_fusion.place, f32[4,128,1280]{2,1,0:T(8,128)} %copy-done.1), custom_call_target="tpu_custom_call" | custom-call | flops 20000 | bytes 120000 | tf_op jit(solution)/shard_map/place_query/pallas_call | solution.py:277
  263.7 4.7 %place_query.3 = f32[1024,1280]{1,0:T(8,128)} custom-call(s32[4]{0:T(128)} %pad_add_fusion.place, f32[4,128,1280]{2,1,0:T(8,128)} %collective-permute-done.21.rows, f32[1024,1280]{1,0:T(8,128)} %place_query.2.refs_0_), custom_call_target="tpu_custom_call", output_to_operand_aliasing={{}: (2, {})} | custom-call | flops 20000 | bytes 120000 | tf_op jit(solution)/shard_map/place_query/pallas_call | solution.py:277
  (97 shorter events, 29.1 us)
Async XLA Ops:
  8.0 201.1 %reduce-scatter.2.cloned.1.call-start = ((), (), s32[]{:S(2)}) async-start(), calls=%async_computation.4 | async-start | bytes 14745600 | tf_op jit(solution)/shard_map/reduce_scatter | solution.py:347
  8.7 22.8 %copy-start.20 = (s32[1280]{0:T(1024)S(1)}, s32[1280]{0:T(1024)}, u32[]{:S(2)}) copy-start(s32[1280]{0:T(1024)} %constant.82.clone) | copy-start | bytes 15364
  8.7 22.8 %copy-start.21 = (s32[1280]{0:T(1024)S(1)}, s32[1280]{0:T(1024)}, u32[]{:S(2)}) copy-start(s32[1280]{0:T(1024)} %constant.81.clone) | copy-start | bytes 15364
  8.7 22.8 %copy-start.22 = (s32[1280]{0:T(1024)S(1)}, s32[1280]{0:T(1024)}, u32[]{:S(2)}) copy-start(s32[1280]{0:T(1024)} %constant.80.clone) | copy-start | bytes 15364
  8.7 22.8 %copy-start.23 = (s32[1280]{0:T(1024)S(1)}, s32[1280]{0:T(1024)}, u32[]{:S(2)}) copy-start(s32[1280]{0:T(1024)} %constant.79.clone) | copy-start | bytes 15364
  8.7 22.8 %copy-start.24 = (s32[1280]{0:T(1024)S(1)}, s32[1280]{0:T(1024)}, u32[]{:S(2)}) copy-start(s32[1280]{0:T(1024)} %constant.78.clone) | copy-start | bytes 15364
  27.0 9.6 %collective-permute-start.2 = (f32[5,4,1024]{2,1,0:T(4,128)}, f32[5,4,1024]{2,1,0:T(4,128)S(1)}, u32[]{:S(2)}, u32[]{:S(2)}) collective-permute-start(f32[5,4,1024]{2,1,0:T(4,128)} %get-tuple-element.70.s0), channel_id=1, source_target_pairs={{0,96},{8,104},{16,112},{24,120},{32,0},{40,8},{48,16},{56,24},{64... | collective-permute-start | bytes 245768 | tf_op jit(solution)/shard_map/ppermute | solution.py:31
  30.4 6.2 %collective-permute-start.1 = (f32[5,4,1024]{2,1,0:T(4,128)}, f32[5,4,1024]{2,1,0:T(4,128)S(1)}, u32[]{:S(2)}, u32[]{:S(2)}) collective-permute-start(f32[5,4,1024]{2,1,0:T(4,128)} %get-tuple-element.70.s0), channel_id=1, source_target_pairs={{0,64},{8,72},{16,80},{24,88},{32,96},{40,104},{48,112},{56,120},{... | collective-permute-start | bytes 245768 | tf_op jit(solution)/shard_map/ppermute | solution.py:31
  30.9 6.0 %collective-permute-start = (f32[5,4,1024]{2,1,0:T(4,128)}, f32[5,4,1024]{2,1,0:T(4,128)S(1)}, u32[]{:S(2)}, u32[]{:S(2)}) collective-permute-start(f32[5,4,1024]{2,1,0:T(4,128)} %get-tuple-element.70.s0), channel_id=1, source_target_pairs={{0,32},{8,40},{16,48},{24,56},{32,64},{40,72},{48,80},{56,88},{64,... | collective-permute-start | bytes 245768 | tf_op jit(solution)/shard_map/ppermute | solution.py:31
  36.9 55.8 %collective-permute-start.6 = (f32[1280,256]{1,0:T(8,128)}, f32[1280,256]{1,0:T(8,128)}, u32[]{:S(2)}, u32[]{:S(2)}) collective-permute-start(f32[1280,256]{1,0:T(8,128)} %get-tuple-element.63), channel_id=1, source_target_pairs={{0,32},{8,40},{16,48},{24,56},{32,64},{40,72},{48,80},{56,88},{64,... | collective-permute-start | bytes 3932168 | tf_op jit(solution)/shard_map/ppermute | solution.py:31
  38.2 57.4 %collective-permute-start.7 = (f32[1280,256]{1,0:T(8,128)S(1)}, f32[1280,256]{1,0:T(8,128)}, u32[]{:S(2)}, u32[]{:S(2)}) collective-permute-start(f32[1280,256]{1,0:T(8,128)S(1)} %copy-done.26), channel_id=1, source_target_pairs={{0,64},{8,72},{16,80},{24,88},{32,96},{40,104},{48,112},{56,120},{... | collective-permute-start | bytes 3932168 | tf_op jit(solution)/shard_map/ppermute | solution.py:31
  39.9 56.5 %collective-permute-start.8 = (f32[1280,256]{1,0:T(8,128)S(1)}, f32[1280,256]{1,0:T(8,128)}, u32[]{:S(2)}, u32[]{:S(2)}) collective-permute-start(f32[1280,256]{1,0:T(8,128)S(1)} %copy-done.25), channel_id=1, source_target_pairs={{0,96},{8,104},{16,112},{24,120},{32,0},{40,8},{48,16},{56,24},{64... | collective-permute-start | bytes 3932168 | tf_op jit(solution)/shard_map/ppermute | solution.py:31
  42.4 5.8 %collective-permute-start.5 = (f32[5,4,1024]{2,1,0:T(4,128)}, f32[5,4,1024]{2,1,0:T(4,128)S(1)}, u32[]{:S(2)}, u32[]{:S(2)}) collective-permute-start(f32[5,4,1024]{2,1,0:T(4,128)} %merge.1.s0), channel_id=1, source_target_pairs={{0,24},{8,0},{16,8},{24,16},{32,56},{40,32},{48,40},{56,48},{64,88... | collective-permute-start | bytes 245768 | tf_op jit(solution)/shard_map/ppermute | solution.py:33
  46.2 5.0 %collective-permute-start.4 = (f32[5,4,1024]{2,1,0:T(4,128)}, f32[5,4,1024]{2,1,0:T(4,128)S(1)}, u32[]{:S(2)}, u32[]{:S(2)}) collective-permute-start(f32[5,4,1024]{2,1,0:T(4,128)} %merge.1.s0), channel_id=1, source_target_pairs={{0,16},{8,24},{16,0},{24,8},{32,48},{40,56},{48,32},{56,40},{64,80... | collective-permute-start | bytes 245768 | tf_op jit(solution)/shard_map/ppermute | solution.py:33
  48.3 7.0 %collective-permute-start.3 = (f32[5,4,1024]{2,1,0:T(4,128)}, f32[5,4,1024]{2,1,0:T(4,128)S(1)}, u32[]{:S(2)}, u32[]{:S(2)}) collective-permute-start(f32[5,4,1024]{2,1,0:T(4,128)} %merge.1.s0), channel_id=1, source_target_pairs={{0,8},{8,16},{16,24},{24,0},{32,40},{40,48},{48,56},{56,32},{64,72... | collective-permute-start | bytes 245768 | tf_op jit(solution)/shard_map/ppermute | solution.py:33
  96.4 62.0 %all-to-all-start.1 = ((f32[64,8,1280]{2,1,0:T(8,128)}), f32[64,8,1280]{2,1,0:T(8,128)S(1)}, u32[]{:S(2)}, u32[]{:S(2)}) async-start(f32[64,8,1280]{2,1,0:T(8,128)} %fusion), calls=%async_computation.1 | async-start | bytes 5242880 | tf_op jit(solution)/shard_map/all_to_all | solution.py:294
  108.4 142.9 %all-gather.3.cloned.1.call-start = ((), (), s32[]{:S(2)}) async-start(), calls=%async_computation.5 | async-start | bytes 5570560 | tf_op jit(solution)/shard_map/all_gather | solution.py:362
  113.0 35.0 %collective-permute-start.9 = (f32[640,128]{1,0:T(8,128)}, f32[640,128]{1,0:T(8,128)S(1)}, u32[]{:S(2)}, u32[]{:S(2)}) collective-permute-start(f32[640,128]{1,0:T(8,128)} %get-tuple-element.75), channel_id=1, source_target_pairs={{0,8},{8,16},{16,24},{24,0},{32,40},{40,48},{48,56},{56,32},{64,72... | collective-permute-start | bytes 983048 | tf_op jit(solution)/shard_map/ppermute | solution.py:33
  114.4 40.4 %collective-permute-start.10 = (f32[640,128]{1,0:T(8,128)}, f32[640,128]{1,0:T(8,128)S(1)}, u32[]{:S(2)}, u32[]{:S(2)}) collective-permute-start(f32[640,128]{1,0:T(8,128)} %get-tuple-element.76), channel_id=1, source_target_pairs={{0,16},{8,24},{16,0},{24,8},{32,48},{40,56},{48,32},{56,40},{64,80... | collective-permute-start | bytes 983048 | tf_op jit(solution)/shard_map/ppermute | solution.py:33
  117.0 38.5 %collective-permute-start.11 = (f32[640,128]{1,0:T(8,128)}, f32[640,128]{1,0:T(8,128)S(1)}, u32[]{:S(2)}, u32[]{:S(2)}) collective-permute-start(f32[640,128]{1,0:T(8,128)} %get-tuple-element.77), channel_id=1, source_target_pairs={{0,24},{8,0},{16,8},{24,16},{32,56},{40,32},{48,40},{56,48},{64,88... | collective-permute-start | bytes 983048 | tf_op jit(solution)/shard_map/ppermute | solution.py:33
  183.1 20.8 %collective-permute-start.13 = (f32[128,1280]{1,0:T(8,128)S(1)}, f32[128,1280]{1,0:T(8,128)S(1)}, u32[]{:S(2)}, u32[]{:S(2)}) collective-permute-start(f32[128,1280]{1,0:T(8,128)S(1)} %bitcast.18), channel_id=1, source_target_pairs={{0,96},{8,104},{16,112},{24,120},{32,0},{40,8},{48,16},{56,24},{64... | collective-permute-start | bytes 1966088 | tf_op jit(solution)/shard_map/ppermute | solution.py:31
  186.6 21.0 %collective-permute-start.12 = (f32[128,1280]{1,0:T(8,128)S(1)}, f32[128,1280]{1,0:T(8,128)S(1)}, u32[]{:S(2)}, u32[]{:S(2)}) collective-permute-start(f32[128,1280]{1,0:T(8,128)S(1)} %bitcast.19), channel_id=1, source_target_pairs={{0,32},{8,40},{16,48},{24,56},{32,64},{40,72},{48,80},{56,88},{64,... | collective-permute-start | bytes 1966088 | tf_op jit(solution)/shard_map/ppermute | solution.py:31
  186.6 53.6 %collective-permute-start.20 = (f32[128,1280]{1,0:T(8,128)S(1)}, f32[128,1280]{1,0:T(8,128)S(1)}, u32[]{:S(2)}, u32[]{:S(2)}) collective-permute-start(f32[128,1280]{1,0:T(8,128)S(1)} %bitcast.20), channel_id=1, source_target_pairs={{0,64},{8,72},{16,80},{24,88},{32,96},{40,104},{48,112},{56,120},{... | collective-permute-start | bytes 1966088 | tf_op jit(solution)/shard_map/ppermute | solution.py:31
  203.9 36.3 %copy-start.2 = (f32[128,1280]{1,0:T(8,128)}, f32[128,1280]{1,0:T(8,128)S(1)}, u32[]{:S(2)}) copy-start(f32[128,1280]{1,0:T(8,128)S(1)} %collective-permute-done.13) | copy-start | bytes 1966084
  207.5 32.6 %copy-start.3 = (f32[128,1280]{1,0:T(8,128)}, f32[128,1280]{1,0:T(8,128)S(1)}, u32[]{:S(2)}) copy-start(f32[128,1280]{1,0:T(8,128)S(1)} %collective-permute-done.12) | copy-start | bytes 1966084
  211.8 11.2 %collective-permute-start.14 = (f32[40,2560]{1,0:T(8,128)}, f32[40,2560]{1,0:T(8,128)S(1)}, u32[]{:S(2)}, u32[]{:S(2)}) collective-permute-start(f32[40,2560]{1,0:T(8,128)} %get-tuple-element.83), channel_id=1, source_target_pairs={{0,8},{8,16},{16,24},{24,0},{32,40},{40,48},{48,56},{56,32},{64,72... | collective-permute-start | bytes 1228808 | tf_op jit(solution)/shard_map/ppermute | solution.py:33
  212.5 24.5 %collective-permute-start.15 = (f32[40,2560]{1,0:T(8,128)}, f32[40,2560]{1,0:T(8,128)S(1)}, u32[]{:S(2)}, u32[]{:S(2)}) collective-permute-start(f32[40,2560]{1,0:T(8,128)} %get-tuple-element.84), channel_id=1, source_target_pairs={{0,16},{8,24},{16,0},{24,8},{32,48},{40,56},{48,32},{56,40},{64,80... | collective-permute-start | bytes 1228808 | tf_op jit(solution)/shard_map/ppermute | solution.py:33
  215.3 21.7 %collective-permute-start.16 = (f32[40,2560]{1,0:T(8,128)}, f32[40,2560]{1,0:T(8,128)S(1)}, u32[]{:S(2)}, u32[]{:S(2)}) collective-permute-start(f32[40,2560]{1,0:T(8,128)} %get-tuple-element.85), channel_id=1, source_target_pairs={{0,24},{8,0},{16,8},{24,16},{32,56},{40,32},{48,40},{56,48},{64,88... | collective-permute-start | bytes 1228808 | tf_op jit(solution)/shard_map/ppermute | solution.py:33
  242.8 21.0 %collective-permute-start.21 = (f32[4,128,1280]{2,1,0:T(8,128)S(1)}, f32[4,128,1280]{2,1,0:T(8,128)}, u32[]{:S(2)}, u32[]{:S(2)}) collective-permute-start(f32[4,128,1280]{2,1,0:T(8,128)S(1)} %pad_maximum_fusion.rows), channel_id=1, source_target_pairs={{0,1},{1,0},{2,3},{3,2},{4,5},{5,4},{6,7},{7,6},{8,9},{9,8},{10,11... | collective-permute-start | bytes 7864328 | tf_op jit(solution)/shard_map/ppermute | solution.py:36
  248.6 11.9 %collective-permute-start.17 = (f32[16,2560]{1,0:T(8,128)}, f32[16,2560]{1,0:T(8,128)S(1)}, u32[]{:S(2)}, u32[]{:S(2)}) collective-permute-start(f32[16,2560]{1,0:T(8,128)} %get-tuple-element.87), channel_id=1, source_target_pairs={{0,32},{8,40},{16,48},{24,56},{32,64},{40,72},{48,80},{56,88},{64,... | collective-permute-start | bytes 491528 | tf_op jit(solution)/shard_map/ppermute | solution.py:31
  248.6 11.9 %collective-permute-start.18 = (f32[16,2560]{1,0:T(8,128)}, f32[16,2560]{1,0:T(8,128)S(1)}, u32[]{:S(2)}, u32[]{:S(2)}) collective-permute-start(f32[16,2560]{1,0:T(8,128)} %get-tuple-element.88), channel_id=1, source_target_pairs={{0,64},{8,72},{16,80},{24,88},{32,96},{40,104},{48,112},{56,120},{... | collective-permute-start | bytes 491528 | tf_op jit(solution)/shard_map/ppermute | solution.py:31
  251.1 9.4 %collective-permute-start.19 = (f32[16,2560]{1,0:T(8,128)S(1)}, f32[16,2560]{1,0:T(8,128)S(1)}, u32[]{:S(2)}, u32[]{:S(2)}) collective-permute-start(f32[16,2560]{1,0:T(8,128)S(1)} %copy-done.27), channel_id=1, source_target_pairs={{0,96},{8,104},{16,112},{24,120},{32,0},{40,8},{48,16},{56,24},{64... | collective-permute-start | bytes 491528 | tf_op jit(solution)/shard_map/ppermute | solution.py:31
  (21 other events, 100.2 us)
Sparse Core Ops, SparseCore 0:
  96.6 112.5 reduce-scatter.1
Sparse Core Ops, SparseCore 1:
  158.5 81.4 all-gather.2

commit v6 on v5

--- a/solution.py
+++ b/solution.py
@@ -264,30 +264,33 @@
     return simple(query_sum_kernel, [parts], (16, 8, D), "query_sum")
 
 
-def place_query_kernel(place, rows, *refs):
-    refs[-1][...] = rows[0]
-
-
-def place_query(place, rows, before=None):
-    def spot(k, p):
-        half = p[3] if before is None else 1 - p[3]
-        return half * 4 + lax.rem(p[0] + 4 - k, 4), 0
-
-    others = [] if before is None else [before]
+def place_query_kernel(hops, place, own, other, *refs):
+    out, sems = refs[-2], refs[-1]
+    copies = []
+    for i, hop in enumerate(hops):
+        block = lax.rem(place[0] + 4 - hop, 4) * 128
+        for j, (half, rows) in enumerate(((place[3], own), (1 - place[3], other))):
+            start = pl.multiple_of(half * 512 + block, 128)
+            copies.append(pltpu.make_async_copy(rows.at[i], out.at[pl.ds(start, 128)], sems.at[2 * i + j]))
+    for copy in copies:
+        copy.start()
+    for copy in copies:
+        copy.wait()
+
+
+def place_query(place, hops, own, other, before=None):
+    arrays = [own, other] + ([] if before is None else [before])
     return pl.pallas_call(
-        place_query_kernel,
-        grid_spec=pltpu.PrefetchScalarGridSpec(
-            num_scalar_prefetch=1,
-            grid=(4,),
-            in_specs=[pl.BlockSpec((1, 128, D), lambda k, p: (k, 0, 0))] + [pl.BlockSpec(memory_space=pl.ANY)] * len(others),
-            out_specs=pl.BlockSpec((128, D), spot),
-        ),
+        functools.partial(place_query_kernel, hops),
+        in_specs=[SMEM] + [pl.BlockSpec(memory_space=pl.ANY)] * len(arrays),
+        out_specs=pl.BlockSpec(memory_space=pl.ANY),
         out_shape=jax.ShapeDtypeStruct((L, D), F32),
-        input_output_aliases={} if before is None else {2: 0},
+        input_output_aliases={} if before is None else {3: 0},
+        scratch_shapes=[pltpu.SemaphoreType.DMA((2 * len(hops),))],
         compiler_params=params(),
         cost_estimate=cost(1e6, 6e6),
         name="place_query",
-    )(place, rows, *others)
+    )(place, *arrays)
 
 
 def spread(blocks):
@@ -362,9 +365,12 @@
     gathered = lax.all_gather(after(q_parts, share), "seq")
     right, left = shift(own_query, "x", 1), shift(own_query, "x", 3)
     rows = after((right, left), rows)
+    far = shift(own_query, "x", 2)
     rows = exchange(simple(second_kernel, [rows], [(40, 2 * D)] * 4, "second"), "z")
-    rows = simple(third_kernel, rows, [(16, 2 * D)] * 4, "third")
-    own_query = jnp.stack([own_query, right, after(rows[0], shift(own_query, "x", 2)), left])
+    near_query = jnp.stack([own_query, right, left])
+    query_grad = place_query(place, (0, 1, 3), near_query, shift(near_query, "c", 1))
+    rows = simple(third_kernel, after(query_grad, rows), [(16, 2 * D)] * 4, "third")
+    far = after(rows[0], far).reshape(1, 128, D)
     rows = exchange(rows, "x")
 
     attended = pl.pallas_call(
@@ -377,9 +383,8 @@
         cost_estimate=cost(1e6, 8e6),
         name="round",
     )(gathered)
-    half_placed = place_query(place, own_query)
-    other_query = after((attended, rows, half_placed), shift(own_query, "c", 1))
-    query_grad = place_query(place, other_query, half_placed)
+    far_other = after(attended, shift(far, "c", 1))
+    query_grad = place_query(place, (2,), far, far_other, query_grad)
     key_rows, value_rows = simple(last_kernel, rows, [(10, D)] * 2, "last")
     return attended.reshape(1, L, D), query_grad, key_rows, value_rows
 

time: 277 us -> 410 us (1.48)
  Pallas kernels: 77.8 us -> 231 us
  waiting for transfers between devices: 91.7 us -> 72.3 us
    pallas_call x2, Pallas kernels: 9.32 us -> 162 us  [place_query(): pl.pallas_call(functools.partial(place_query_kernel, hops), in_specs=[SME...]
    ppermute x9, waiting for transfers between devices: 66.2 us -> 46.5 us  [shift(): lax.ppermute(array, 'seq', [(a * 4 + b, a * 4 + (b + step) % 4) for a in...]
    ppermute x1 -> x2, starting transfers between devices: 5.82 us -> 8.38 us  [shift(): lax.ppermute(array, 'dp', [(a * 2 + b, a * 2 + 1 - b) for a in range(4) f...]
  transfers between devices with their start and end apart: 25 -> 26, of which waited for: 14 -> 12; matrix products, arithmetic and copies ran while one was open for 2% -> 1% of each run, Pallas kernels for 20% -> 42%
where the time goes in v6:
time: 410 us; the launch traced here: 409 us
  Pallas kernels  231 us (56%)
  waiting for transfers between devices  72.3 us (18%)
  starting transfers between devices  48.4 us (12%)
  blocking collectives  32.1 us (8%)
  between operations  15.7 us (4%)
  local copies, waits for them, and re-layouts  6.62 us (2%)
    pallas_call x2, Pallas kernels, place_query(): pl.pallas_call(functools.partial(place_query_kernel, hops), in_specs=[SME...  162 us
    ppermute x9, waiting for transfers between devices, shift(): lax.ppermute(array, 'seq', [(a * 4 + b, a * 4 + (b + step) % 4) for a in...  46.5 us
    ppermute x12, waiting for transfers between devices, shift(): lax.ppermute(array, 'seq', [(a * 4 + b, (a + step) % 4 * 4 + b) for a in...  25.7 us
    pallas_call x1, Pallas kernels, backward(): pl.pallas_call(backward_kernel, grid=(PAIRS,), in_specs=[full((D, T)), pa...  21.4 us
    all_to_all x1, blocking collectives, on_device(): lax.all_to_all(query_sum(q_parts), ('seq', 'dp'), split_axis=0, concat_ax...  20.4 us
    pallas_call x8, Pallas kernels, simple(): pl.pallas_call(kernel, in_specs=([] if scalars is None else [SMEM]) + spe...  19.9 us
    pallas_call x1, Pallas kernels, forward(): pl.pallas_call(forward_kernel, grid=(PAIRS,), in_specs=[SMEM, full((T, D)...  18.3 us
    ppermute x12, starting transfers between devices, shift(): lax.ppermute(array, 'seq', [(a * 4 + b, (a + step) % 4 * 4 + b) for a in...  16.5 us
  transfers between devices with their start and end apart: 26, of which 12 were waited for; matrix products, arithmetic and copies ran while one was open for 1% of the time, Pallas kernels for 42%

profile of v6, /device:TPU:1, one launch (start us, length us, event | category | flops | bytes accessed | tf_op | source)
XLA Modules:
  0.0 408.5 jit_solution(348752582137096057)
XLA Ops:
  8.7 18.3 %forward.1 = (bf16[512,1280]{1,0:T(8,128)(2,1)}, bf16[512,1280]{1,0:T(8,128)(2,1)}, bf16[512,1280]{1,0:T(8,128)(2,1)}, f32[1280,256]{1,0:T(8,128)}, f32[1280,256...) custom-call(s32[4]{0:T(128)} %pad_add_fusion.place, bf16[512,1280]{1,0:T(8,128)(2,1)} %bitcast.23, ...), custom_call_target="tpu_custom_call" | custom-call | flops 240000000 | bytes 480000 | tf_op jit(solution)/shard_map/forward/pallas_call | solution.py:100
  27.0 3.4 collective-permute-start.2
  32.1 4.3 %reorder.1.nt = bf16[1280,512]{1,0:T(8,128)(2,1)} custom-call(s32[1,1280]{1,0:T(1,128)} %reshape.21.order, bf16[512,1280]{1,0:T(8,128)(2,1)} %get-tuple-element.54.normed), custom_call_target="tpu_custom_call" | custom-call | flops 33554432 | bytes 60000 | tf_op jit(solution)/shard_map/reorder/pallas_call | solution.py:157
  42.3 3.8 collective-permute-start.5
  46.1 2.1 collective-permute-done.5.s3
  48.2 2.9 collective-permute-done.4.s2
  51.1 4.1 %collective-permute-done.3.s1 = f32[5,4,1024]{2,1,0:T(4,128)S(1)} collective-permute-done((f32[5,4,1024]{2,1,0:T(4,128)}, f32[5,4,1024]{2,1,0:T(4,128)S(1)}, u32[]{:S(2)}, u32[]{:S(2)}) %collective-permute-start.3) | collective-permute-done | bytes 81952 | tf_op jit(solution)/shard_map/ppermute | solution.py:33
  57.6 21.4 %backward.1 = (f32[1280,2560]{1,0:T(8,128)}, f32[2,64,8,1280]{3,2,1,0:T(8,128)}) custom-call(bf16[1280,512]{1,0:T(8,128)(2,1)} %reorder.1.nt, bf16[512,1280]{1,0:T(8,128)(2,1)} %get-tuple-element.59.keys, bf16[512,1280]{1,0:T(8,128)(2,1)} %get-tuple-element.60.vals, bf16[1024,1280]{1,0:T(8,128)(2,1)} %q.3, bf16[1024,1280]{1,0:T(8,128)(2,1)} %bitcast.16, ...), custom_call_target="tpu_custom_call" | custom-call | flops 400000000 | bytes 600000 | tf_op jit(solution)/shard_map/backward/pallas_call | solution.py:196
  79.0 11.7 %all_to_all.15 = f32[2,64,8,1280]{3,2,1,0:T(8,128)S(1)} all-to-all(f32[2,64,8,1280]{3,2,1,0:T(8,128)} %get-tuple-element.65), channel_id=1, replica_groups={{0,1},{2,3},{4,5},{6,7},{8,9},{10,11},{12,13},{14,15},{16,17},{18,19},{..., dimensions={0} | all-to-all | bytes 10485760 | tf_op jit(solution)/shard_map/all_to_all | solution.py:346
  90.7 1.8 fusion
  92.5 3.0 collective-permute-done.7.n2
  96.4 11.9 %all-to-all-start.1 = ((f32[64,8,1280]{2,1,0:T(8,128)}), f32[64,8,1280]{2,1,0:T(8,128)S(1)}, u32[]{:S(2)}, u32[]{:S(2)}) async-start(f32[64,8,1280]{2,1,0:T(8,128)} %fusion), calls=%async_computation.1 | async-start | bytes 5242880 | tf_op jit(solution)/shard_map/all_to_all | solution.py:297
  108.4 4.7 %numer_x.1 = (f32[640,128]{1,0:T(8,128)}, f32[640,128]{1,0:T(8,128)}, f32[640,128]{1,0:T(8,128)}, f32[640,128]{1,0:T(8,128)}) custom-call(s32[4]{0:T(128)} %pad_add_fusion.place, f32[1280,256]{1,0:T(8,128)} %get-tuple-element.70.n0, f32[1280,256]{1,0:T(8,128)} %collective-permute-done.6.n1, f32[1280,256]{1,0:T(8,128)} %collective-permute-done.7.n2, ...), custom_call_target="tpu_custom_call" | custom-call | flops 20000 | bytes 140000 | tf_op jit(solution)/shard_map/numer_x/pallas_call | solution.py:139
  114.4 2.6 collective-permute-start.10
  118.1 29.9 %collective-permute-done.9.z1 = f32[640,128]{1,0:T(8,128)S(1)} collective-permute-done((f32[640,128]{1,0:T(8,128)}, f32[640,128]{1,0:T(8,128)S(1)}, u32[]{:S(2)}, u32[]{:S(2)}) %collective-permute-start.9) | collective-permute-done | bytes 327712 | tf_op jit(solution)/shard_map/ppermute | solution.py:33
  148.0 6.7 %collective-permute-done.10.z2 = f32[640,128]{1,0:T(8,128)S(1)} collective-permute-done((f32[640,128]{1,0:T(8,128)}, f32[640,128]{1,0:T(8,128)S(1)}, u32[]{:S(2)}, u32[]{:S(2)}) %collective-permute-start.10) | collective-permute-done | bytes 327712 | tf_op jit(solution)/shard_map/ppermute | solution.py:33
  156.2 2.2 numer_z.1
  159.9 2.8 query_sum.1
  162.7 20.4 %all_to_all.16 = f32[16,8,1280]{2,1,0:T(8,128)S(1)} all-to-all(f32[16,8,1280]{2,1,0:T(8,128)} %query_sum.1), channel_id=1, replica_groups={{0,2,4,6,8,10,12,14,16,18,20,22,24,26,28,30},{1,3,5,7,9,11,13,15,17,19,..., dimensions={0} | all-to-all | bytes 1310720 | tf_op jit(solution)/shard_map/all_to_all | solution.py:351
  183.1 3.4 collective-permute-start.13
  186.5 16.9 %collective-permute-done.13 = f32[128,1280]{1,0:T(8,128)S(1)} collective-permute-done((f32[128,1280]{1,0:T(8,128)S(1)}, f32[128,1280]{1,0:T(8,128)S(1)}, u32[]{:S(2)}, u32[]{:S(2)}) %collective-permute-start.13) | collective-permute-done | bytes 655392 | tf_op jit(solution)/shard_map/ppermute | solution.py:31
  203.4 3.0 collective-permute-done.12
  206.6 7.1 %collective-permute-start.14 = (f32[3,128,1280]{2,1,0:T(8,128)S(1)}, f32[3,128,1280]{2,1,0:T(8,128)}, u32[]{:S(2)}, u32[]{:S(2)}) collective-permute-start(f32[3,128,1280]{2,1,0:T(8,128)S(1)} %pad_maximum_fusion.own), channel_id=1, source_target_pairs={{0,1},{1,0},{2,3},{3,2},{4,5},{5,4},{6,7},{7,6},{8,9},{9,8},{10,11... | collective-permute-start | bytes 5898248 | tf_op jit(solution)/shard_map/ppermute | solution.py:36
  213.7 2.7 second.1
  216.4 2.7 collective-permute-start.17
  219.1 120.9 %place_query.2.refs_0_ = f32[1024,1280]{1,0:T(8,128)} custom-call(s32[4]{0:T(128)} %pad_add_fusion.place, f32[3,128,1280]{2,1,0:T(8,128)} %copy-done.1, f32[3,128,1280]{2,1,0:T(8,128)} %collective-permute-done.14.other), custom_call_target="tpu_custom_call" | custom-call | flops 20000 | bytes 120000 | tf_op jit(solution)/shard_map/place_query/pallas_call | solution.py:283
  341.1 2.2 third.1
  344.6 2.7 collective-permute-start.21
  347.4 2.1 collective-permute-start.22
  349.4 4.6 %round.1 = bf16[1024,1280]{1,0:T(8,128)(2,1)} custom-call(f32[16,128,640]{2,1,0:T(8,128)} %bitcast.17), custom_call_target="tpu_custom_call" | custom-call | flops 20000 | bytes 160000 | tf_op jit(solution)/shard_map/round/pallas_call | solution.py:376
  356.9 1.8 last.1
  359.6 41.5 %place_query.3 = f32[1024,1280]{1,0:T(8,128)} custom-call(s32[4]{0:T(128)} %pad_add_fusion.place, f32[1,128,1280]{2,1,0:T(8,128)} %bitcast.25, f32[1,128,1280]{2,1,0:T(8,128)} %copy-done.3, f32[1024,1280]{1,0:T(8,128)} %place_query.2.refs_0_), custom_call_target="tpu_custom_call", output_to_operand_aliasing={{}: (3, {})} | custom-call | flops 20000 | bytes 120000 | tf_op jit(solution)/shard_map/place_query/pallas_call | solution.py:283
  (95 shorter events, 23.0 us)
Async XLA Ops:
  8.0 205.7 %reduce-scatter.2.cloned.1.call-start = ((), (), s32[]{:S(2)}) async-start(), calls=%async_computation.4 | async-start | bytes 14745600 | tf_op jit(solution)/shard_map/reduce_scatter | solution.py:350
  8.6 22.8 %copy-start.19 = (s32[1280]{0:T(1024)S(1)}, s32[1280]{0:T(1024)}, u32[]{:S(2)}) copy-start(s32[1280]{0:T(1024)} %constant.82.clone) | copy-start | bytes 15364
  8.6 22.8 %copy-start.20 = (s32[1280]{0:T(1024)S(1)}, s32[1280]{0:T(1024)}, u32[]{:S(2)}) copy-start(s32[1280]{0:T(1024)} %constant.81.clone) | copy-start | bytes 15364
  8.6 22.8 %copy-start.21 = (s32[1280]{0:T(1024)S(1)}, s32[1280]{0:T(1024)}, u32[]{:S(2)}) copy-start(s32[1280]{0:T(1024)} %constant.80.clone) | copy-start | bytes 15364
  8.6 22.8 %copy-start.22 = (s32[1280]{0:T(1024)S(1)}, s32[1280]{0:T(1024)}, u32[]{:S(2)}) copy-start(s32[1280]{0:T(1024)} %constant.79.clone) | copy-start | bytes 15364
  8.7 22.8 %copy-start.23 = (s32[1280]{0:T(1024)S(1)}, s32[1280]{0:T(1024)}, u32[]{:S(2)}) copy-start(s32[1280]{0:T(1024)} %constant.78.clone) | copy-start | bytes 15364
  26.9 12.9 %copy-start.24 = (f32[1280,256]{1,0:T(8,128)S(1)}, f32[1280,256]{1,0:T(8,128)}, u32[]{:S(2)}) copy-start(f32[1280,256]{1,0:T(8,128)} %get-tuple-element.69) | copy-start | bytes 3932164
  27.0 9.5 %collective-permute-start.2 = (f32[5,4,1024]{2,1,0:T(4,128)}, f32[5,4,1024]{2,1,0:T(4,128)S(1)}, u32[]{:S(2)}, u32[]{:S(2)}) collective-permute-start(f32[5,4,1024]{2,1,0:T(4,128)} %get-tuple-element.74.s0), channel_id=1, source_target_pairs={{0,96},{8,104},{16,112},{24,120},{32,0},{40,8},{48,16},{56,24},{64... | collective-permute-start | bytes 245768 | tf_op jit(solution)/shard_map/ppermute | solution.py:31
  30.3 6.1 %collective-permute-start.1 = (f32[5,4,1024]{2,1,0:T(4,128)}, f32[5,4,1024]{2,1,0:T(4,128)S(1)}, u32[]{:S(2)}, u32[]{:S(2)}) collective-permute-start(f32[5,4,1024]{2,1,0:T(4,128)} %get-tuple-element.74.s0), channel_id=1, source_target_pairs={{0,64},{8,72},{16,80},{24,88},{32,96},{40,104},{48,112},{56,120},{... | collective-permute-start | bytes 245768 | tf_op jit(solution)/shard_map/ppermute | solution.py:31
  30.9 5.9 %collective-permute-start = (f32[5,4,1024]{2,1,0:T(4,128)}, f32[5,4,1024]{2,1,0:T(4,128)S(1)}, u32[]{:S(2)}, u32[]{:S(2)}) collective-permute-start(f32[5,4,1024]{2,1,0:T(4,128)} %get-tuple-element.74.s0), channel_id=1, source_target_pairs={{0,32},{8,40},{16,48},{24,56},{32,64},{40,72},{48,80},{56,88},{64,... | collective-permute-start | bytes 245768 | tf_op jit(solution)/shard_map/ppermute | solution.py:31
  36.8 55.7 %collective-permute-start.6 = (f32[1280,256]{1,0:T(8,128)}, f32[1280,256]{1,0:T(8,128)}, u32[]{:S(2)}, u32[]{:S(2)}) collective-permute-start(f32[1280,256]{1,0:T(8,128)} %get-tuple-element.67), channel_id=1, source_target_pairs={{0,32},{8,40},{16,48},{24,56},{32,64},{40,72},{48,80},{56,88},{64,... | collective-permute-start | bytes 3932168 | tf_op jit(solution)/shard_map/ppermute | solution.py:31
  38.1 57.4 %collective-permute-start.7 = (f32[1280,256]{1,0:T(8,128)S(1)}, f32[1280,256]{1,0:T(8,128)}, u32[]{:S(2)}, u32[]{:S(2)}) collective-permute-start(f32[1280,256]{1,0:T(8,128)S(1)} %copy-done.25), channel_id=1, source_target_pairs={{0,64},{8,72},{16,80},{24,88},{32,96},{40,104},{48,112},{56,120},{... | collective-permute-start | bytes 3932168 | tf_op jit(solution)/shard_map/ppermute | solution.py:31
  39.8 56.5 %collective-permute-start.8 = (f32[1280,256]{1,0:T(8,128)S(1)}, f32[1280,256]{1,0:T(8,128)}, u32[]{:S(2)}, u32[]{:S(2)}) collective-permute-start(f32[1280,256]{1,0:T(8,128)S(1)} %copy-done.24), channel_id=1, source_target_pairs={{0,96},{8,104},{16,112},{24,120},{32,0},{40,8},{48,16},{56,24},{64... | collective-permute-start | bytes 3932168 | tf_op jit(solution)/shard_map/ppermute | solution.py:31
  42.3 5.9 %collective-permute-start.5 = (f32[5,4,1024]{2,1,0:T(4,128)}, f32[5,4,1024]{2,1,0:T(4,128)S(1)}, u32[]{:S(2)}, u32[]{:S(2)}) collective-permute-start(f32[5,4,1024]{2,1,0:T(4,128)} %merge.1.s0), channel_id=1, source_target_pairs={{0,24},{8,0},{16,8},{24,16},{32,56},{40,32},{48,40},{56,48},{64,88... | collective-permute-start | bytes 245768 | tf_op jit(solution)/shard_map/ppermute | solution.py:33
  46.1 5.0 %collective-permute-start.4 = (f32[5,4,1024]{2,1,0:T(4,128)}, f32[5,4,1024]{2,1,0:T(4,128)S(1)}, u32[]{:S(2)}, u32[]{:S(2)}) collective-permute-start(f32[5,4,1024]{2,1,0:T(4,128)} %merge.1.s0), channel_id=1, source_target_pairs={{0,16},{8,24},{16,0},{24,8},{32,48},{40,56},{48,32},{56,40},{64,80... | collective-permute-start | bytes 245768 | tf_op jit(solution)/shard_map/ppermute | solution.py:33
  48.2 7.0 %collective-permute-start.3 = (f32[5,4,1024]{2,1,0:T(4,128)}, f32[5,4,1024]{2,1,0:T(4,128)S(1)}, u32[]{:S(2)}, u32[]{:S(2)}) collective-permute-start(f32[5,4,1024]{2,1,0:T(4,128)} %merge.1.s0), channel_id=1, source_target_pairs={{0,8},{8,16},{16,24},{24,0},{32,40},{40,48},{48,56},{56,32},{64,72... | collective-permute-start | bytes 245768 | tf_op jit(solution)/shard_map/ppermute | solution.py:33
  96.4 62.0 %all-to-all-start.1 = ((f32[64,8,1280]{2,1,0:T(8,128)}), f32[64,8,1280]{2,1,0:T(8,128)S(1)}, u32[]{:S(2)}, u32[]{:S(2)}) async-start(f32[64,8,1280]{2,1,0:T(8,128)} %fusion), calls=%async_computation.1 | async-start | bytes 5242880 | tf_op jit(solution)/shard_map/all_to_all | solution.py:297
  108.3 241.1 %all-gather.3.cloned.1.call-start = ((), (), s32[]{:S(2)}) async-start(), calls=%async_computation.5 | async-start | bytes 5570560 | tf_op jit(solution)/shard_map/all_gather | solution.py:365
  113.0 35.0 %collective-permute-start.9 = (f32[640,128]{1,0:T(8,128)}, f32[640,128]{1,0:T(8,128)S(1)}, u32[]{:S(2)}, u32[]{:S(2)}) collective-permute-start(f32[640,128]{1,0:T(8,128)} %get-tuple-element.79), channel_id=1, source_target_pairs={{0,8},{8,16},{16,24},{24,0},{32,40},{40,48},{48,56},{56,32},{64,72... | collective-permute-start | bytes 983048 | tf_op jit(solution)/shard_map/ppermute | solution.py:33
  114.4 40.3 %collective-permute-start.10 = (f32[640,128]{1,0:T(8,128)}, f32[640,128]{1,0:T(8,128)S(1)}, u32[]{:S(2)}, u32[]{:S(2)}) collective-permute-start(f32[640,128]{1,0:T(8,128)} %get-tuple-element.80), channel_id=1, source_target_pairs={{0,16},{8,24},{16,0},{24,8},{32,48},{40,56},{48,32},{56,40},{64,80... | collective-permute-start | bytes 983048 | tf_op jit(solution)/shard_map/ppermute | solution.py:33
  117.0 38.5 %collective-permute-start.11 = (f32[640,128]{1,0:T(8,128)}, f32[640,128]{1,0:T(8,128)S(1)}, u32[]{:S(2)}, u32[]{:S(2)}) collective-permute-start(f32[640,128]{1,0:T(8,128)} %get-tuple-element.81), channel_id=1, source_target_pairs={{0,24},{8,0},{16,8},{24,16},{32,56},{40,32},{48,40},{56,48},{64,88... | collective-permute-start | bytes 983048 | tf_op jit(solution)/shard_map/ppermute | solution.py:33
  183.1 20.4 %collective-permute-start.13 = (f32[128,1280]{1,0:T(8,128)S(1)}, f32[128,1280]{1,0:T(8,128)S(1)}, u32[]{:S(2)}, u32[]{:S(2)}) collective-permute-start(f32[128,1280]{1,0:T(8,128)S(1)} %bitcast.19), channel_id=1, source_target_pairs={{0,96},{8,104},{16,112},{24,120},{32,0},{40,8},{48,16},{56,24},{64... | collective-permute-start | bytes 1966088 | tf_op jit(solution)/shard_map/ppermute | solution.py:31
  186.5 19.9 %collective-permute-start.12 = (f32[128,1280]{1,0:T(8,128)S(1)}, f32[128,1280]{1,0:T(8,128)S(1)}, u32[]{:S(2)}, u32[]{:S(2)}) collective-permute-start(f32[128,1280]{1,0:T(8,128)S(1)} %bitcast.20), channel_id=1, source_target_pairs={{0,32},{8,40},{16,48},{24,56},{32,64},{40,72},{48,80},{56,88},{64,... | collective-permute-start | bytes 1966088 | tf_op jit(solution)/shard_map/ppermute | solution.py:31
  206.6 12.5 %collective-permute-start.14 = (f32[3,128,1280]{2,1,0:T(8,128)S(1)}, f32[3,128,1280]{2,1,0:T(8,128)}, u32[]{:S(2)}, u32[]{:S(2)}) collective-permute-start(f32[3,128,1280]{2,1,0:T(8,128)S(1)} %pad_maximum_fusion.own), channel_id=1, source_target_pairs={{0,1},{1,0},{2,3},{3,2},{4,5},{5,4},{6,7},{7,6},{8,9},{9,8},{10,11... | collective-permute-start | bytes 5898248 | tf_op jit(solution)/shard_map/ppermute | solution.py:36
  213.7 129.6 %collective-permute-start.18 = (f32[128,1280]{1,0:T(8,128)S(1)}, f32[128,1280]{1,0:T(8,128)S(1)}, u32[]{:S(2)}, u32[]{:S(2)}) collective-permute-start(f32[128,1280]{1,0:T(8,128)S(1)} %bitcast.22), channel_id=1, source_target_pairs={{0,64},{8,72},{16,80},{24,88},{32,96},{40,104},{48,112},{56,120},{... | collective-permute-start | bytes 1966088 | tf_op jit(solution)/shard_map/ppermute | solution.py:31
  216.4 123.6 %collective-permute-start.15 = (f32[40,2560]{1,0:T(8,128)}, f32[40,2560]{1,0:T(8,128)S(1)}, u32[]{:S(2)}, u32[]{:S(2)}) collective-permute-start(f32[40,2560]{1,0:T(8,128)} %get-tuple-element.87), channel_id=1, source_target_pairs={{0,8},{8,16},{16,24},{24,0},{32,40},{40,48},{48,56},{56,32},{64,72... | collective-permute-start | bytes 1228808 | tf_op jit(solution)/shard_map/ppermute | solution.py:33
  216.4 123.7 %collective-permute-start.16 = (f32[40,2560]{1,0:T(8,128)}, f32[40,2560]{1,0:T(8,128)S(1)}, u32[]{:S(2)}, u32[]{:S(2)}) collective-permute-start(f32[40,2560]{1,0:T(8,128)} %get-tuple-element.88), channel_id=1, source_target_pairs={{0,16},{8,24},{16,0},{24,8},{32,48},{40,56},{48,32},{56,40},{64,80... | collective-permute-start | bytes 1228808 | tf_op jit(solution)/shard_map/ppermute | solution.py:33
  216.4 123.7 %collective-permute-start.17 = (f32[40,2560]{1,0:T(8,128)}, f32[40,2560]{1,0:T(8,128)S(1)}, u32[]{:S(2)}, u32[]{:S(2)}) collective-permute-start(f32[40,2560]{1,0:T(8,128)} %get-tuple-element.89), channel_id=1, source_target_pairs={{0,24},{8,0},{16,8},{24,16},{32,56},{40,32},{48,40},{56,48},{64,88... | collective-permute-start | bytes 1228808 | tf_op jit(solution)/shard_map/ppermute | solution.py:33
  343.4 15.3 %collective-permute-start.19 = (f32[1,128,1280]{2,1,0:T(8,128)S(1)}, f32[1,128,1280]{2,1,0:T(8,128)S(1)}, u32[]{:S(2)}, u32[]{:S(2)}) collective-permute-start(f32[1,128,1280]{2,1,0:T(8,128)S(1)} %bitcast.24), channel_id=1, source_target_pairs={{0,1},{1,0},{2,3},{3,2},{4,5},{5,4},{6,7},{7,6},{8,9},{9,8},{10,11... | collective-permute-start | bytes 1966088 | tf_op jit(solution)/shard_map/ppermute | solution.py:36
  344.6 9.4 %collective-permute-start.20 = (f32[16,2560]{1,0:T(8,128)}, f32[16,2560]{1,0:T(8,128)S(1)}, u32[]{:S(2)}, u32[]{:S(2)}) collective-permute-start(f32[16,2560]{1,0:T(8,128)} %get-tuple-element.97), channel_id=1, source_target_pairs={{0,32},{8,40},{16,48},{24,56},{32,64},{40,72},{48,80},{56,88},{64,... | collective-permute-start | bytes 491528 | tf_op jit(solution)/shard_map/ppermute | solution.py:31
  344.6 11.0 %collective-permute-start.21 = (f32[16,2560]{1,0:T(8,128)}, f32[16,2560]{1,0:T(8,128)S(1)}, u32[]{:S(2)}, u32[]{:S(2)}) collective-permute-start(f32[16,2560]{1,0:T(8,128)} %get-tuple-element.98), channel_id=1, source_target_pairs={{0,64},{8,72},{16,80},{24,88},{32,96},{40,104},{48,112},{56,120},{... | collective-permute-start | bytes 491528 | tf_op jit(solution)/shard_map/ppermute | solution.py:31
  347.4 8.2 %collective-permute-start.22 = (f32[16,2560]{1,0:T(8,128)}, f32[16,2560]{1,0:T(8,128)S(1)}, u32[]{:S(2)}, u32[]{:S(2)}) collective-permute-start(f32[16,2560]{1,0:T(8,128)} %get-tuple-element.99), channel_id=1, source_target_pairs={{0,96},{8,104},{16,112},{24,120},{32,0},{40,8},{48,16},{56,24},{64... | collective-permute-start | bytes 491528 | tf_op jit(solution)/shard_map/ppermute | solution.py:31
  (20 other events, 75.0 us)
Sparse Core Ops, SparseCore 0:
  96.5 112.5 reduce-scatter.1
Sparse Core Ops, SparseCore 1:
  158.5 81.4 all-gather.2

commit v7 on v6

--- a/solution.py
+++ b/solution.py
@@ -264,29 +264,35 @@
     return simple(query_sum_kernel, [parts], (16, 8, D), "query_sum")
 
 
-def place_query_kernel(hops, place, own, other, *refs):
-    out, sems = refs[-2], refs[-1]
-    copies = []
-    for i, hop in enumerate(hops):
-        block = lax.rem(place[0] + 4 - hop, 4) * 128
-        for j, (half, rows) in enumerate(((place[3], own), (1 - place[3], other))):
-            start = pl.multiple_of(half * 512 + block, 128)
-            copies.append(pltpu.make_async_copy(rows.at[i], out.at[pl.ds(start, 128)], sems.at[2 * i + j]))
-    for copy in copies:
-        copy.start()
-    for copy in copies:
-        copy.wait()
-
-
-def place_query(place, hops, own, other, before=None):
+def place_query_kernel(place, own, other, *refs):
+    out = refs[-1]
+
+    @pl.when(pl.program_id(1) == 0)
+    def _():
+        out[...] = own[0]
+
+    @pl.when(pl.program_id(1) == 1)
+    def _():
+        out[...] = other[0]
+
+
+def place_query(place, hop, own, other, before=None):
+    def spot(i, j, p):
+        half = lax.rem(p[3] + j, 2)
+        return half * 4 + lax.rem(p[0] + 4 - hop(i), 4), 0
+
     arrays = [own, other] + ([] if before is None else [before])
     return pl.pallas_call(
-        functools.partial(place_query_kernel, hops),
-        in_specs=[SMEM] + [pl.BlockSpec(memory_space=pl.ANY)] * len(arrays),
-        out_specs=pl.BlockSpec(memory_space=pl.ANY),
+        place_query_kernel,
+        grid_spec=pltpu.PrefetchScalarGridSpec(
+            num_scalar_prefetch=1,
+            grid=(own.shape[0], 2),
+            in_specs=[pl.BlockSpec((1, 128, D), lambda i, j, p: (i, 0, 0))] * 2
+            + [pl.BlockSpec(memory_space=pl.ANY)] * (len(arrays) - 2),
+            out_specs=pl.BlockSpec((128, D), spot),
+        ),
         out_shape=jax.ShapeDtypeStruct((L, D), F32),
         input_output_aliases={} if before is None else {3: 0},
-        scratch_shapes=[pltpu.SemaphoreType.DMA((2 * len(hops),))],
         compiler_params=params(),
         cost_estimate=cost(1e6, 6e6),
         name="place_query",
@@ -368,7 +374,7 @@
     far = shift(own_query, "x", 2)
     rows = exchange(simple(second_kernel, [rows], [(40, 2 * D)] * 4, "second"), "z")
     near_query = jnp.stack([own_query, right, left])
-    query_grad = place_query(place, (0, 1, 3), near_query, shift(near_query, "c", 1))
+    query_grad = place_query(place, lambda i: i + i // 2, near_query, shift(near_query, "c", 1))
     rows = simple(third_kernel, after(query_grad, rows), [(16, 2 * D)] * 4, "third")
     far = after(rows[0], far).reshape(1, 128, D)
     rows = exchange(rows, "x")
@@ -384,7 +390,7 @@
         name="round",
     )(gathered)
     far_other = after(attended, shift(far, "c", 1))
-    query_grad = place_query(place, (2,), far, far_other, query_grad)
+    query_grad = place_query(place, lambda i: 2, far, far_other, query_grad)
     key_rows, value_rows = simple(last_kernel, rows, [(10, D)] * 2, "last")
     return attended.reshape(1, L, D), query_grad, key_rows, value_rows
 

time: 410 us -> 269 us (0.66)
  Pallas kernels: 231 us -> 78.4 us
  waiting for transfers between devices: 72.3 us -> 85.2 us
    pallas_call x2, Pallas kernels: 162 us -> 9.88 us  [place_query(): pl.pallas_call(place_query_kernel, grid_spec=pltpu.PrefetchScalarGridSpec...]
    ppermute x9, waiting for transfers between devices: 46.5 us -> 59.2 us  [shift(): lax.ppermute(array, 'seq', [(a * 4 + b, a * 4 + (b + step) % 4) for a in...]
  transfers between devices with their start and end apart: 26 -> 26, of which waited for: 12 -> 14; matrix products, arithmetic and copies ran while one was open for 1% -> 1% of each run, Pallas kernels for 42% -> 21%
where the time goes in v7:
time: 269 us; the launch traced here: 268 us
  waiting for transfers between devices  85.2 us (32%)
  Pallas kernels  78.4 us (29%)
  starting transfers between devices  47.8 us (18%)
  blocking collectives  32.1 us (12%)
  between operations  15.7 us (6%)
  local copies, waits for them, and re-layouts  6.45 us (2%)
    ppermute x9, waiting for transfers between devices, shift(): lax.ppermute(array, 'seq', [(a * 4 + b, a * 4 + (b + step) % 4) for a in...  59.2 us
    ppermute x12, waiting for transfers between devices, shift(): lax.ppermute(array, 'seq', [(a * 4 + b, (a + step) % 4 * 4 + b) for a in...  25.9 us
    pallas_call x1, Pallas kernels, backward(): pl.pallas_call(backward_kernel, grid=(PAIRS,), in_specs=[full((D, T)), pa...  21.4 us
    all_to_all x1, blocking collectives, on_device(): lax.all_to_all(query_sum(q_parts), ('seq', 'dp'), split_axis=0, concat_ax...  20.4 us
    pallas_call x8, Pallas kernels, simple(): pl.pallas_call(kernel, in_specs=([] if scalars is None else [SMEM]) + spe...  19.9 us
    pallas_call x1, Pallas kernels, forward(): pl.pallas_call(forward_kernel, grid=(PAIRS,), in_specs=[SMEM, full((T, D)...  18.3 us
    ppermute x12, starting transfers between devices, shift(): lax.ppermute(array, 'seq', [(a * 4 + b, (a + step) % 4 * 4 + b) for a in...  16.3 us
    all_to_all x1, starting transfers between devices, spread(): lax.all_to_all(blocks, ('seq', 'dp'), split_axis=0, concat_axis=0, axis_i...  11.9 us
  transfers between devices with their start and end apart: 26, of which 14 were waited for; matrix products, arithmetic and copies ran while one was open for 1% of the time, Pallas kernels for 21%

profile of v7, /device:TPU:1, one launch (start us, length us, event | category | flops | bytes accessed | tf_op | source)
XLA Modules:
  0.0 268.0 jit_solution(2214602797381599907)
XLA Ops:
  8.7 18.3 %forward.1 = (bf16[512,1280]{1,0:T(8,128)(2,1)}, bf16[512,1280]{1,0:T(8,128)(2,1)}, bf16[512,1280]{1,0:T(8,128)(2,1)}, f32[1280,256]{1,0:T(8,128)}, f32[1280,256...) custom-call(s32[4]{0:T(128)} %pad_add_fusion.place, bf16[512,1280]{1,0:T(8,128)(2,1)} %bitcast.23, ...), custom_call_target="tpu_custom_call" | custom-call | flops 240000000 | bytes 480000 | tf_op jit(solution)/shard_map/forward/pallas_call | solution.py:100
  27.0 3.4 %collective-permute-start.2 = (f32[5,4,1024]{2,1,0:T(4,128)}, f32[5,4,1024]{2,1,0:T(4,128)S(1)}, u32[]{:S(2)}, u32[]{:S(2)}) collective-permute-start(f32[5,4,1024]{2,1,0:T(4,128)} %get-tuple-element.74.s0), channel_id=1, source_target_pairs={{0,96},{8,104},{16,112},{24,120},{32,0},{40,8},{48,16},{56,24},{64... | collective-permute-start | bytes 245768 | tf_op jit(solution)/shard_map/ppermute | solution.py:31
  32.1 4.3 %reorder.1.nt = bf16[1280,512]{1,0:T(8,128)(2,1)} custom-call(s32[1,1280]{1,0:T(1,128)} %reshape.21.order, bf16[512,1280]{1,0:T(8,128)(2,1)} %get-tuple-element.54.normed), custom_call_target="tpu_custom_call" | custom-call | flops 33554432 | bytes 60000 | tf_op jit(solution)/shard_map/reorder/pallas_call | solution.py:157
  42.3 3.8 %collective-permute-start.5 = (f32[5,4,1024]{2,1,0:T(4,128)}, f32[5,4,1024]{2,1,0:T(4,128)S(1)}, u32[]{:S(2)}, u32[]{:S(2)}) collective-permute-start(f32[5,4,1024]{2,1,0:T(4,128)} %merge.1.s0), channel_id=1, source_target_pairs={{0,24},{8,0},{16,8},{24,16},{32,56},{40,32},{48,40},{56,48},{64,88... | collective-permute-start | bytes 245768 | tf_op jit(solution)/shard_map/ppermute | solution.py:33
  46.1 2.1 collective-permute-done.5.s3
  48.2 2.9 %collective-permute-done.4.s2 = f32[5,4,1024]{2,1,0:T(4,128)S(1)} collective-permute-done((f32[5,4,1024]{2,1,0:T(4,128)}, f32[5,4,1024]{2,1,0:T(4,128)S(1)}, u32[]{:S(2)}, u32[]{:S(2)}) %collective-permute-start.4) | collective-permute-done | bytes 81952 | tf_op jit(solution)/shard_map/ppermute | solution.py:33
  51.1 4.1 %collective-permute-done.3.s1 = f32[5,4,1024]{2,1,0:T(4,128)S(1)} collective-permute-done((f32[5,4,1024]{2,1,0:T(4,128)}, f32[5,4,1024]{2,1,0:T(4,128)S(1)}, u32[]{:S(2)}, u32[]{:S(2)}) %collective-permute-start.3) | collective-permute-done | bytes 81952 | tf_op jit(solution)/shard_map/ppermute | solution.py:33
  57.6 21.4 %backward.1 = (f32[1280,2560]{1,0:T(8,128)}, f32[2,64,8,1280]{3,2,1,0:T(8,128)}) custom-call(bf16[1280,512]{1,0:T(8,128)(2,1)} %reorder.1.nt, bf16[512,1280]{1,0:T(8,128)(2,1)} %get-tuple-element.59.keys, bf16[512,1280]{1,0:T(8,128)(2,1)} %get-tuple-element.60.vals, bf16[1024,1280]{1,0:T(8,128)(2,1)} %q.3, bf16[1024,1280]{1,0:T(8,128)(2,1)} %bitcast.16, ...), custom_call_target="tpu_custom_call" | custom-call | flops 400000000 | bytes 600000 | tf_op jit(solution)/shard_map/backward/pallas_call | solution.py:196
  79.0 11.7 %all_to_all.15 = f32[2,64,8,1280]{3,2,1,0:T(8,128)S(1)} all-to-all(f32[2,64,8,1280]{3,2,1,0:T(8,128)} %get-tuple-element.65), channel_id=1, replica_groups={{0,1},{2,3},{4,5},{6,7},{8,9},{10,11},{12,13},{14,15},{16,17},{18,19},{..., dimensions={0} | all-to-all | bytes 10485760 | tf_op jit(solution)/shard_map/all_to_all | solution.py:352
  92.5 3.0 %collective-permute-done.7.n2 = f32[1280,256]{1,0:T(8,128)} collective-permute-done((f32[1280,256]{1,0:T(8,128)S(1)}, f32[1280,256]{1,0:T(8,128)}, u32[]{:S(2)}, u32[]{:S(2)}) %collective-permute-start.7) | collective-permute-done | bytes 1310752 | tf_op jit(solution)/shard_map/ppermute | solution.py:31
  96.4 11.9 %all-to-all-start.1 = ((f32[64,8,1280]{2,1,0:T(8,128)}), f32[64,8,1280]{2,1,0:T(8,128)S(1)}, u32[]{:S(2)}, u32[]{:S(2)}) async-start(f32[64,8,1280]{2,1,0:T(8,128)} %fusion), calls=%async_computation.1 | async-start | bytes 5242880 | tf_op jit(solution)/shard_map/all_to_all | solution.py:303
  108.4 4.7 %numer_x.1 = (f32[640,128]{1,0:T(8,128)}, f32[640,128]{1,0:T(8,128)}, f32[640,128]{1,0:T(8,128)}, f32[640,128]{1,0:T(8,128)}) custom-call(s32[4]{0:T(128)} %pad_add_fusion.place, f32[1280,256]{1,0:T(8,128)} %get-tuple-element.70.n0, f32[1280,256]{1,0:T(8,128)} %collective-permute-done.6.n1, f32[1280,256]{1,0:T(8,128)} %collective-permute-done.7.n2, ...), custom_call_target="tpu_custom_call" | custom-call | flops 20000 | bytes 140000 | tf_op jit(solution)/shard_map/numer_x/pallas_call | solution.py:139
  114.4 2.6 collective-permute-start.10
  118.1 29.9 %collective-permute-done.9.z1 = f32[640,128]{1,0:T(8,128)S(1)} collective-permute-done((f32[640,128]{1,0:T(8,128)}, f32[640,128]{1,0:T(8,128)S(1)}, u32[]{:S(2)}, u32[]{:S(2)}) %collective-permute-start.9) | collective-permute-done | bytes 327712 | tf_op jit(solution)/shard_map/ppermute | solution.py:33
  148.0 6.7 %collective-permute-done.10.z2 = f32[640,128]{1,0:T(8,128)S(1)} collective-permute-done((f32[640,128]{1,0:T(8,128)}, f32[640,128]{1,0:T(8,128)S(1)}, u32[]{:S(2)}, u32[]{:S(2)}) %collective-permute-start.10) | collective-permute-done | bytes 327712 | tf_op jit(solution)/shard_map/ppermute | solution.py:33
  156.2 2.2 numer_z.1
  159.9 2.8 %query_sum.1 = f32[16,8,1280]{2,1,0:T(8,128)} custom-call(f32[64,8,1280]{2,1,0:T(8,128)} %copy-done), custom_call_target="tpu_custom_call" | custom-call | flops 20000 | bytes 80000 | tf_op jit(solution)/shard_map/query_sum/pallas_call | solution.py:139
  162.7 20.4 %all_to_all.16 = f32[16,8,1280]{2,1,0:T(8,128)S(1)} all-to-all(f32[16,8,1280]{2,1,0:T(8,128)} %query_sum.1), channel_id=1, replica_groups={{0,2,4,6,8,10,12,14,16,18,20,22,24,26,28,30},{1,3,5,7,9,11,13,15,17,19,..., dimensions={0} | all-to-all | bytes 1310720 | tf_op jit(solution)/shard_map/all_to_all | solution.py:357
  183.1 3.4 %collective-permute-start.13 = (f32[128,1280]{1,0:T(8,128)S(1)}, f32[128,1280]{1,0:T(8,128)S(1)}, u32[]{:S(2)}, u32[]{:S(2)}) collective-permute-start(f32[128,1280]{1,0:T(8,128)S(1)} %bitcast.19), channel_id=1, source_target_pairs={{0,96},{8,104},{16,112},{24,120},{32,0},{40,8},{48,16},{56,24},{64... | collective-permute-start | bytes 1966088 | tf_op jit(solution)/shard_map/ppermute | solution.py:31
  186.5 16.9 %collective-permute-done.13 = f32[128,1280]{1,0:T(8,128)S(1)} collective-permute-done((f32[128,1280]{1,0:T(8,128)S(1)}, f32[128,1280]{1,0:T(8,128)S(1)}, u32[]{:S(2)}, u32[]{:S(2)}) %collective-permute-start.13) | collective-permute-done | bytes 655392 | tf_op jit(solution)/shard_map/ppermute | solution.py:31
  203.4 3.0 %collective-permute-done.12 = f32[128,1280]{1,0:T(8,128)S(1)} collective-permute-done((f32[128,1280]{1,0:T(8,128)S(1)}, f32[128,1280]{1,0:T(8,128)S(1)}, u32[]{:S(2)}, u32[]{:S(2)}) %collective-permute-start.12) | collective-permute-done | bytes 655392 | tf_op jit(solution)/shard_map/ppermute | solution.py:31
  206.6 7.1 %collective-permute-start.14 = (f32[3,128,1280]{2,1,0:T(8,128)S(1)}, f32[3,128,1280]{2,1,0:T(8,128)}, u32[]{:S(2)}, u32[]{:S(2)}) collective-permute-start(f32[3,128,1280]{2,1,0:T(8,128)S(1)} %pad_maximum_fusion.own), channel_id=1, source_target_pairs={{0,1},{1,0},{2,3},{3,2},{4,5},{5,4},{6,7},{7,6},{8,9},{9,8},{10,11... | collective-permute-start | bytes 5898248 | tf_op jit(solution)/shard_map/ppermute | solution.py:36
  213.7 2.7 %second.1 = (f32[40,2560]{1,0:T(8,128)}, f32[40,2560]{1,0:T(8,128)}, f32[40,2560]{1,0:T(8,128)}, f32[40,2560]{1,0:T(8,128)}) custom-call(f32[160,2560]{1,0:T(8,128)} %reduce-scatter.2.cloned.1.call-done.rows), custom_call_target="tpu_custom_call" | custom-call | flops 20000 | bytes 80000 | tf_op jit(solution)/shard_map/second/pallas_call | solution.py:139
  216.4 2.7 collective-permute-start.17
  219.1 6.8 %place_query.2.refs_0_ = f32[1024,1280]{1,0:T(8,128)} custom-call(s32[4]{0:T(128)} %pad_add_fusion.place, f32[3,128,1280]{2,1,0:T(8,128)} %copy-done.1, f32[3,128,1280]{2,1,0:T(8,128)} %collective-permute-done.14.other), custom_call_target="tpu_custom_call" | custom-call | flops 20000 | bytes 120000 | tf_op jit(solution)/shard_map/place_query/pallas_call | solution.py:285
  225.9 12.7 %collective-permute-done.15.a1 = f32[40,2560]{1,0:T(8,128)S(1)} collective-permute-done((f32[40,2560]{1,0:T(8,128)}, f32[40,2560]{1,0:T(8,128)S(1)}, u32[]{:S(2)}, u32[]{:S(2)}) %collective-permute-start.15) | collective-permute-done | bytes 409632 | tf_op jit(solution)/shard_map/ppermute | solution.py:33
  239.6 2.2 third.1
  242.7 2.5 collective-permute-start.21
  245.2 2.1 collective-permute-start.22
  247.3 4.6 %round.1 = bf16[1024,1280]{1,0:T(8,128)(2,1)} custom-call(f32[16,128,640]{2,1,0:T(8,128)} %bitcast.17), custom_call_target="tpu_custom_call" | custom-call | flops 20000 | bytes 160000 | tf_op jit(solution)/shard_map/round/pallas_call | solution.py:382
  254.8 1.8 last.1
  257.5 3.1 %place_query.3 = f32[1024,1280]{1,0:T(8,128)} custom-call(s32[4]{0:T(128)} %pad_add_fusion.place, f32[1,128,1280]{2,1,0:T(8,128)} %bitcast.25, f32[1,128,1280]{2,1,0:T(8,128)} %copy-done.3, f32[1024,1280]{1,0:T(8,128)} %place_query.2.refs_0_), custom_call_target="tpu_custom_call", output_to_operand_aliasing={{}: (3, {})} | custom-call | flops 20000 | bytes 120000 | tf_op jit(solution)/shard_map/place_query/pallas_call | solution.py:285
  (95 shorter events, 24.5 us)
Async XLA Ops:
  8.0 205.7 %reduce-scatter.2.cloned.1.call-start = ((), (), s32[]{:S(2)}) async-start(), calls=%async_computation.4 | async-start | bytes 14745600 | tf_op jit(solution)/shard_map/reduce_scatter | solution.py:356
  8.6 22.8 %copy-start.19 = (s32[1280]{0:T(1024)S(1)}, s32[1280]{0:T(1024)}, u32[]{:S(2)}) copy-start(s32[1280]{0:T(1024)} %constant.82.clone) | copy-start | bytes 15364
  8.6 22.8 %copy-start.20 = (s32[1280]{0:T(1024)S(1)}, s32[1280]{0:T(1024)}, u32[]{:S(2)}) copy-start(s32[1280]{0:T(1024)} %constant.81.clone) | copy-start | bytes 15364
  8.6 22.8 %copy-start.21 = (s32[1280]{0:T(1024)S(1)}, s32[1280]{0:T(1024)}, u32[]{:S(2)}) copy-start(s32[1280]{0:T(1024)} %constant.80.clone) | copy-start | bytes 15364
  8.6 22.8 %copy-start.22 = (s32[1280]{0:T(1024)S(1)}, s32[1280]{0:T(1024)}, u32[]{:S(2)}) copy-start(s32[1280]{0:T(1024)} %constant.79.clone) | copy-start | bytes 15364
  8.7 22.8 %copy-start.23 = (s32[1280]{0:T(1024)S(1)}, s32[1280]{0:T(1024)}, u32[]{:S(2)}) copy-start(s32[1280]{0:T(1024)} %constant.78.clone) | copy-start | bytes 15364
  26.9 12.9 %copy-start.24 = (f32[1280,256]{1,0:T(8,128)S(1)}, f32[1280,256]{1,0:T(8,128)}, u32[]{:S(2)}) copy-start(f32[1280,256]{1,0:T(8,128)} %get-tuple-element.69) | copy-start | bytes 3932164
  27.0 9.5 %collective-permute-start.2 = (f32[5,4,1024]{2,1,0:T(4,128)}, f32[5,4,1024]{2,1,0:T(4,128)S(1)}, u32[]{:S(2)}, u32[]{:S(2)}) collective-permute-start(f32[5,4,1024]{2,1,0:T(4,128)} %get-tuple-element.74.s0), channel_id=1, source_target_pairs={{0,96},{8,104},{16,112},{24,120},{32,0},{40,8},{48,16},{56,24},{64... | collective-permute-start | bytes 245768 | tf_op jit(solution)/shard_map/ppermute | solution.py:31
  30.3 6.1 %collective-permute-start.1 = (f32[5,4,1024]{2,1,0:T(4,128)}, f32[5,4,1024]{2,1,0:T(4,128)S(1)}, u32[]{:S(2)}, u32[]{:S(2)}) collective-permute-start(f32[5,4,1024]{2,1,0:T(4,128)} %get-tuple-element.74.s0), channel_id=1, source_target_pairs={{0,64},{8,72},{16,80},{24,88},{32,96},{40,104},{48,112},{56,120},{... | collective-permute-start | bytes 245768 | tf_op jit(solution)/shard_map/ppermute | solution.py:31
  30.9 5.9 %collective-permute-start = (f32[5,4,1024]{2,1,0:T(4,128)}, f32[5,4,1024]{2,1,0:T(4,128)S(1)}, u32[]{:S(2)}, u32[]{:S(2)}) collective-permute-start(f32[5,4,1024]{2,1,0:T(4,128)} %get-tuple-element.74.s0), channel_id=1, source_target_pairs={{0,32},{8,40},{16,48},{24,56},{32,64},{40,72},{48,80},{56,88},{64,... | collective-permute-start | bytes 245768 | tf_op jit(solution)/shard_map/ppermute | solution.py:31
  36.8 55.7 %collective-permute-start.6 = (f32[1280,256]{1,0:T(8,128)}, f32[1280,256]{1,0:T(8,128)}, u32[]{:S(2)}, u32[]{:S(2)}) collective-permute-start(f32[1280,256]{1,0:T(8,128)} %get-tuple-element.67), channel_id=1, source_target_pairs={{0,32},{8,40},{16,48},{24,56},{32,64},{40,72},{48,80},{56,88},{64,... | collective-permute-start | bytes 3932168 | tf_op jit(solution)/shard_map/ppermute | solution.py:31
  38.1 57.4 %collective-permute-start.7 = (f32[1280,256]{1,0:T(8,128)S(1)}, f32[1280,256]{1,0:T(8,128)}, u32[]{:S(2)}, u32[]{:S(2)}) collective-permute-start(f32[1280,256]{1,0:T(8,128)S(1)} %copy-done.25), channel_id=1, source_target_pairs={{0,64},{8,72},{16,80},{24,88},{32,96},{40,104},{48,112},{56,120},{... | collective-permute-start | bytes 3932168 | tf_op jit(solution)/shard_map/ppermute | solution.py:31
  39.8 56.5 %collective-permute-start.8 = (f32[1280,256]{1,0:T(8,128)S(1)}, f32[1280,256]{1,0:T(8,128)}, u32[]{:S(2)}, u32[]{:S(2)}) collective-permute-start(f32[1280,256]{1,0:T(8,128)S(1)} %copy-done.24), channel_id=1, source_target_pairs={{0,96},{8,104},{16,112},{24,120},{32,0},{40,8},{48,16},{56,24},{64... | collective-permute-start | bytes 3932168 | tf_op jit(solution)/shard_map/ppermute | solution.py:31
  42.3 5.9 %collective-permute-start.5 = (f32[5,4,1024]{2,1,0:T(4,128)}, f32[5,4,1024]{2,1,0:T(4,128)S(1)}, u32[]{:S(2)}, u32[]{:S(2)}) collective-permute-start(f32[5,4,1024]{2,1,0:T(4,128)} %merge.1.s0), channel_id=1, source_target_pairs={{0,24},{8,0},{16,8},{24,16},{32,56},{40,32},{48,40},{56,48},{64,88... | collective-permute-start | bytes 245768 | tf_op jit(solution)/shard_map/ppermute | solution.py:33
  46.1 5.0 %collective-permute-start.4 = (f32[5,4,1024]{2,1,0:T(4,128)}, f32[5,4,1024]{2,1,0:T(4,128)S(1)}, u32[]{:S(2)}, u32[]{:S(2)}) collective-permute-start(f32[5,4,1024]{2,1,0:T(4,128)} %merge.1.s0), channel_id=1, source_target_pairs={{0,16},{8,24},{16,0},{24,8},{32,48},{40,56},{48,32},{56,40},{64,80... | collective-permute-start | bytes 245768 | tf_op jit(solution)/shard_map/ppermute | solution.py:33
  48.2 7.0 %collective-permute-start.3 = (f32[5,4,1024]{2,1,0:T(4,128)}, f32[5,4,1024]{2,1,0:T(4,128)S(1)}, u32[]{:S(2)}, u32[]{:S(2)}) collective-permute-start(f32[5,4,1024]{2,1,0:T(4,128)} %merge.1.s0), channel_id=1, source_target_pairs={{0,8},{8,16},{16,24},{24,0},{32,40},{40,48},{48,56},{56,32},{64,72... | collective-permute-start | bytes 245768 | tf_op jit(solution)/shard_map/ppermute | solution.py:33
  96.4 62.0 %all-to-all-start.1 = ((f32[64,8,1280]{2,1,0:T(8,128)}), f32[64,8,1280]{2,1,0:T(8,128)S(1)}, u32[]{:S(2)}, u32[]{:S(2)}) async-start(f32[64,8,1280]{2,1,0:T(8,128)} %fusion), calls=%async_computation.1 | async-start | bytes 5242880 | tf_op jit(solution)/shard_map/all_to_all | solution.py:303
  108.3 139.0 %all-gather.3.cloned.1.call-start = ((), (), s32[]{:S(2)}) async-start(), calls=%async_computation.5 | async-start | bytes 5570560 | tf_op jit(solution)/shard_map/all_gather | solution.py:371
  113.0 35.0 %collective-permute-start.9 = (f32[640,128]{1,0:T(8,128)}, f32[640,128]{1,0:T(8,128)S(1)}, u32[]{:S(2)}, u32[]{:S(2)}) collective-permute-start(f32[640,128]{1,0:T(8,128)} %get-tuple-element.79), channel_id=1, source_target_pairs={{0,8},{8,16},{16,24},{24,0},{32,40},{40,48},{48,56},{56,32},{64,72... | collective-permute-start | bytes 983048 | tf_op jit(solution)/shard_map/ppermute | solution.py:33
  114.4 40.3 %collective-permute-start.10 = (f32[640,128]{1,0:T(8,128)}, f32[640,128]{1,0:T(8,128)S(1)}, u32[]{:S(2)}, u32[]{:S(2)}) collective-permute-start(f32[640,128]{1,0:T(8,128)} %get-tuple-element.80), channel_id=1, source_target_pairs={{0,16},{8,24},{16,0},{24,8},{32,48},{40,56},{48,32},{56,40},{64,80... | collective-permute-start | bytes 983048 | tf_op jit(solution)/shard_map/ppermute | solution.py:33
  117.0 38.5 %collective-permute-start.11 = (f32[640,128]{1,0:T(8,128)}, f32[640,128]{1,0:T(8,128)S(1)}, u32[]{:S(2)}, u32[]{:S(2)}) collective-permute-start(f32[640,128]{1,0:T(8,128)} %get-tuple-element.81), channel_id=1, source_target_pairs={{0,24},{8,0},{16,8},{24,16},{32,56},{40,32},{48,40},{56,48},{64,88... | collective-permute-start | bytes 983048 | tf_op jit(solution)/shard_map/ppermute | solution.py:33
  183.1 20.4 %collective-permute-start.13 = (f32[128,1280]{1,0:T(8,128)S(1)}, f32[128,1280]{1,0:T(8,128)S(1)}, u32[]{:S(2)}, u32[]{:S(2)}) collective-permute-start(f32[128,1280]{1,0:T(8,128)S(1)} %bitcast.19), channel_id=1, source_target_pairs={{0,96},{8,104},{16,112},{24,120},{32,0},{40,8},{48,16},{56,24},{64... | collective-permute-start | bytes 1966088 | tf_op jit(solution)/shard_map/ppermute | solution.py:31
  186.5 19.9 %collective-permute-start.12 = (f32[128,1280]{1,0:T(8,128)S(1)}, f32[128,1280]{1,0:T(8,128)S(1)}, u32[]{:S(2)}, u32[]{:S(2)}) collective-permute-start(f32[128,1280]{1,0:T(8,128)S(1)} %bitcast.20), channel_id=1, source_target_pairs={{0,32},{8,40},{16,48},{24,56},{32,64},{40,72},{48,80},{56,88},{64,... | collective-permute-start | bytes 1966088 | tf_op jit(solution)/shard_map/ppermute | solution.py:31
  206.6 12.5 %collective-permute-start.14 = (f32[3,128,1280]{2,1,0:T(8,128)S(1)}, f32[3,128,1280]{2,1,0:T(8,128)}, u32[]{:S(2)}, u32[]{:S(2)}) collective-permute-start(f32[3,128,1280]{2,1,0:T(8,128)S(1)} %pad_maximum_fusion.own), channel_id=1, source_target_pairs={{0,1},{1,0},{2,3},{3,2},{4,5},{5,4},{6,7},{7,6},{8,9},{9,8},{10,11... | collective-permute-start | bytes 5898248 | tf_op jit(solution)/shard_map/ppermute | solution.py:36
  213.7 28.1 %collective-permute-start.18 = (f32[128,1280]{1,0:T(8,128)S(1)}, f32[128,1280]{1,0:T(8,128)S(1)}, u32[]{:S(2)}, u32[]{:S(2)}) collective-permute-start(f32[128,1280]{1,0:T(8,128)S(1)} %bitcast.22), channel_id=1, source_target_pairs={{0,64},{8,72},{16,80},{24,88},{32,96},{40,104},{48,112},{56,120},{... | collective-permute-start | bytes 1966088 | tf_op jit(solution)/shard_map/ppermute | solution.py:31
  216.4 22.1 %collective-permute-start.15 = (f32[40,2560]{1,0:T(8,128)}, f32[40,2560]{1,0:T(8,128)S(1)}, u32[]{:S(2)}, u32[]{:S(2)}) collective-permute-start(f32[40,2560]{1,0:T(8,128)} %get-tuple-element.87), channel_id=1, source_target_pairs={{0,8},{8,16},{16,24},{24,0},{32,40},{40,48},{48,56},{56,32},{64,72... | collective-permute-start | bytes 1228808 | tf_op jit(solution)/shard_map/ppermute | solution.py:33
  216.4 22.1 %collective-permute-start.16 = (f32[40,2560]{1,0:T(8,128)}, f32[40,2560]{1,0:T(8,128)S(1)}, u32[]{:S(2)}, u32[]{:S(2)}) collective-permute-start(f32[40,2560]{1,0:T(8,128)} %get-tuple-element.88), channel_id=1, source_target_pairs={{0,16},{8,24},{16,0},{24,8},{32,48},{40,56},{48,32},{56,40},{64,80... | collective-permute-start | bytes 1228808 | tf_op jit(solution)/shard_map/ppermute | solution.py:33
  216.4 22.1 %collective-permute-start.17 = (f32[40,2560]{1,0:T(8,128)}, f32[40,2560]{1,0:T(8,128)S(1)}, u32[]{:S(2)}, u32[]{:S(2)}) collective-permute-start(f32[40,2560]{1,0:T(8,128)} %get-tuple-element.89), channel_id=1, source_target_pairs={{0,24},{8,0},{16,8},{24,16},{32,56},{40,32},{48,40},{56,48},{64,88... | collective-permute-start | bytes 1228808 | tf_op jit(solution)/shard_map/ppermute | solution.py:33
  241.9 14.8 %collective-permute-start.19 = (f32[1,128,1280]{2,1,0:T(8,128)S(1)}, f32[1,128,1280]{2,1,0:T(8,128)S(1)}, u32[]{:S(2)}, u32[]{:S(2)}) collective-permute-start(f32[1,128,1280]{2,1,0:T(8,128)S(1)} %bitcast.24), channel_id=1, source_target_pairs={{0,1},{1,0},{2,3},{3,2},{4,5},{5,4},{6,7},{7,6},{8,9},{9,8},{10,11... | collective-permute-start | bytes 1966088 | tf_op jit(solution)/shard_map/ppermute | solution.py:36
  242.7 9.2 %collective-permute-start.20 = (f32[16,2560]{1,0:T(8,128)}, f32[16,2560]{1,0:T(8,128)S(1)}, u32[]{:S(2)}, u32[]{:S(2)}) collective-permute-start(f32[16,2560]{1,0:T(8,128)} %get-tuple-element.97), channel_id=1, source_target_pairs={{0,32},{8,40},{16,48},{24,56},{32,64},{40,72},{48,80},{56,88},{64,... | collective-permute-start | bytes 491528 | tf_op jit(solution)/shard_map/ppermute | solution.py:31
  242.7 10.8 %collective-permute-start.21 = (f32[16,2560]{1,0:T(8,128)}, f32[16,2560]{1,0:T(8,128)S(1)}, u32[]{:S(2)}, u32[]{:S(2)}) collective-permute-start(f32[16,2560]{1,0:T(8,128)} %get-tuple-element.98), channel_id=1, source_target_pairs={{0,64},{8,72},{16,80},{24,88},{32,96},{40,104},{48,112},{56,120},{... | collective-permute-start | bytes 491528 | tf_op jit(solution)/shard_map/ppermute | solution.py:31
  245.2 8.4 %collective-permute-start.22 = (f32[16,2560]{1,0:T(8,128)}, f32[16,2560]{1,0:T(8,128)S(1)}, u32[]{:S(2)}, u32[]{:S(2)}) collective-permute-start(f32[16,2560]{1,0:T(8,128)} %get-tuple-element.99), channel_id=1, source_target_pairs={{0,96},{8,104},{16,112},{24,120},{32,0},{40,8},{48,16},{56,24},{64... | collective-permute-start | bytes 491528 | tf_op jit(solution)/shard_map/ppermute | solution.py:31
  (20 other events, 74.6 us)
Sparse Core Ops, SparseCore 0:
  96.5 112.5 reduce-scatter.1
Sparse Core Ops, SparseCore 1:
  158.5 81.4 all-gather.2
